TPU v7x, 32 devices: a whole 2x2x4 slice. The times are simulated.
32 devices in a mesh: row: 8 (over y, x, core), col: 4 (over z).
Axes of the slice: x: 2, y: 2, z: 4, core: 2. Of those that a mesh axis runs over, the one named last changes fastest.
Arguments:
- phase: float32 [6, 32768], P(None, ('col', 'row')), may hold values from -6 to 6
- mass: float32 [32768], P(('col', 'row')), may hold values from 0.2 to 5
- active: int32 [256], P(('row', 'col')), may hold values from 0 to 32767, as said below
Outputs:
- accels: float32 [3, 256], P(None, ('row', 'col'))
- jerks: float32 [3, 256], P(None, ('row', 'col'))
Inputs may be any that keep to these rules, and one draw needn't show every extreme that they name: `active`: the 256 indices are distinct.
All inputs are finite; a program needn't handle non-finite values.
Results may differ from a plain program's by a relative error of at most 0.0003.
Values sent between devices are 32-bit elements; how exact they have to be, the bound alone decides.
No kernel may reach another device: no remote copies, remote signals or barrier semaphores. Data moves between devices by JAX's collectives and lax.ppermute only.
A program may use at most 64 MiB of HBM per device.

v0:
```python
import math

import jax
import jax.numpy as jnp
from jax import lax
from jax.sharding import PartitionSpec as P

SOFTENING = 0.0001


def pair_terms(targets, src_phase, src_mass):
    offset = src_phase[0:3, None, :] - targets[0:3, :, None]
    vel_diff = src_phase[3:6, None, :] - targets[3:6, :, None]
    dist_sq = jnp.sum(offset * offset, axis=0) + SOFTENING
    inverse = lax.rsqrt(dist_sq)
    inverse_sq = inverse * inverse
    weight = src_mass[None, :] * inverse * inverse_sq
    radial = 3.0 * jnp.sum(offset * vel_diff, axis=0) * inverse_sq
    accels = jnp.sum(weight[None] * offset, axis=-1)
    jerks = jnp.sum(weight[None] * (vel_diff - radial[None] * offset), axis=-1)
    return (accels, jerks)


def select_stars(source, indices, first):
    columns = source.shape[1]
    offsets = indices - first
    inside = ((offsets >= 0) & (offsets < columns)).astype(jnp.float32)
    picked = jnp.take(source, jnp.clip(offsets, 0, columns - 1), axis=1)
    return picked * inside[None, :]


def sweep_sources(targets, src_phase, src_mass):
    columns = src_phase.shape[1]
    block_len = math.gcd(columns, 2048)

    def add_block(counter, carry):
        first = counter * block_len
        piece = lax.dynamic_slice_in_dim(src_phase, first, block_len, 1)
        masses = lax.dynamic_slice_in_dim(src_mass, first, block_len, 0)
        accels, jerks = pair_terms(targets, piece, masses)
        return (carry[0] + accels, carry[1] + jerks)

    zeros = jnp.zeros((3, targets.shape[1]), jnp.float32)
    return lax.fori_loop(0, columns // block_len, add_block, (zeros, zeros))


def shards(phase, mass, active):
    row_count = lax.axis_size("row")
    col_count = lax.axis_size("col")
    col_at = lax.axis_index("col")
    norming = 1.0 / (phase.shape[1] * row_count * col_count)
    block_ids = lax.all_gather(active, "col", axis=0, tiled=True)
    src_phase, src_mass = (
        lax.all_gather(phase, "row", axis=1, tiled=True),
        lax.all_gather(mass, "row", axis=0, tiled=True),
    )
    picked = select_stars(src_phase, block_ids, col_at * src_phase.shape[1])
    targets = lax.psum(picked, "col")
    accels, jerks = sweep_sources(targets, src_phase, src_mass)
    accels, jerks = (
        lax.psum_scatter(accels, "col", scatter_dimension=1, tiled=True),
        lax.psum_scatter(jerks, "col", scatter_dimension=1, tiled=True),
    )
    return (accels * norming, jerks * norming)


def solution(mesh):
    in_specs = (P(None, ("col", "row")), P(("col", "row")), P(("row", "col")))
    out_specs = (P(None, ("row", "col")), P(None, ("row", "col")))
    return jax.shard_map(shards, mesh=mesh, in_specs=in_specs, out_specs=out_specs, check_vma=False)
```

profile of v0, /device:TPU:0, one launch (start us, length us, event | category | flops | bytes accessed | tf_op | source)
XLA Modules:
  0.0 82.8 jit_solution(15656166970275630786)
XLA Ops:
  0.6 1.3 %fusion.6 = (u32[1]{0:T(128)}, u32[1]{0:T(128)}) fusion(u32[32]{0:T(128)} %constant.78, u32[]{:T(128)S(6)} %add.78, u32[]{:T(128)S(6)} %add.70), kind=kLoop, calls=%fused_computation.25 | loop fusion | bytes 24
  2.6 0.9 %dynamic-update-slice = s32[32]{0:T(128)S(1)} dynamic-update-slice(s32[32]{0:T(128)S(1)} %max.6, s32[8]{0:T(128)} %param.7, u32[]{:T(128)} %bitcast.4) | dynamic-update-slice | bytes 68
  3.5 9.9 %all-reduce = s32[32]{0:T(128)S(1)} all-reduce(s32[32]{0:T(128)S(1)} %dynamic-update-slice), channel_id=1, replica_groups=mesh['row'=8,'col'=4] {'col'}, use_global_device_ids=true, to_apply=%add | all-reduce | flops 32 | bytes 256
  13.4 1.0 %copy.11 = f32[6,1024]{0,1:T(8,128)S(1)} copy(f32[6,1024]{1,0:T(8,128)} %param.5) | data formatting | bytes 49152 | tf_op args[0]
  14.4 24.6 %all_gather.10 = f32[6,8192]{0,1:T(8,128)} all-gather(f32[6,1024]{0,1:T(8,128)S(1)} %copy.11), channel_id=1, replica_groups=mesh['row'=8,'col'=4] {'row'}, dimensions={1}, use_global_device_ids=true | all-gather | bytes 221184 | tf_op jit(solution)/shard_map/all_gather | solution.py:54
  39.0 2.8 %gather_fusion = f32[32,6]{1,0:T(8,128)S(1)} fusion(f32[6,8192]{0,1:T(8,128)} %all_gather.10, s32[1024]{0:T(1024)S(1)} %pad_clamp_fusion), kind=kCustom, calls=%fused_computation | custom fusion | bytes 1664 | tf_op jit(solution)/shard_map/jit(_take)/gather | solution.py:28
  41.9 17.0 %psum.7 = f32[6,32]{0,1:T(8,128)S(1)} all-reduce(f32[6,32]{0,1:T(8,128)S(1)} %multiply_bitcast_fusion), channel_id=1, replica_groups=mesh['row'=8,'col'=4] {'col'}, use_global_device_ids=true, to_apply=%region_0.1 | all-reduce | flops 192 | bytes 1536 | tf_op jit(solution)/shard_map/psum | solution.py:58
  59.0 2.8 %copy.12 = f32[6,8192]{1,0:T(8,128)S(1)} copy(f32[6,8192]{0,1:T(8,128)} %all_gather.10) | data formatting | bytes 393216
  61.8 7.6 %all_gather.9 = f32[8192]{0:T(1024)S(1)} all-gather(f32[1024]{0:T(1024)S(1)} %copy-done), channel_id=1, replica_groups=mesh['row'=8,'col'=4] {'row'}, dimensions={0}, use_global_device_ids=true | all-gather | bytes 36864 | tf_op jit(solution)/shard_map/all_gather | solution.py:55
  69.4 3.7 %while.16 = (s32[]{:T(128)}, f32[3,32]{1,0:T(4,128)S(1)}, f32[3,32]{1,0:T(4,128)S(1)}, f32[8192]{0:T(1024)S(1)}, f32[6,8192]{1,0:T(8,128)S(1)}, /*index=5*/f32[6...) while((s32[]{:T(128)}, f32[3,32]{1,0:T(4,128)S(1)}, ...), condition=%wide.region_6.7_spmd.clone, body=%wide.region_1.6_spmd.clone.sunk | while | flops 3014856 | bytes 2324669 | solution.py:44
  69.4 0.1 constant_dynamic-slice_fusion.2
  69.5 0.3 fusion.11
  69.9 0.4 fusion.12
  70.3 0.1 constant_dynamic-slice_fusion.2
  70.4 0.3 fusion.11
  70.8 0.4 fusion.12
  71.3 0.1 constant_dynamic-slice_fusion.2
  71.4 0.3 fusion.11
  71.8 0.4 fusion.12
  72.2 0.1 constant_dynamic-slice_fusion.2
  72.3 0.3 fusion.11
  72.7 0.4 fusion.12
  73.1 8.4 %all-reduce.3 = (f32[3,32]{1,0:T(4,128)S(1)}, f32[3,32]{1,0:T(4,128)S(1)}) all-reduce(f32[3,32]{1,0:T(4,128)S(1)} %get-tuple-element.112, f32[3,32]{1,0:T(4,128)S(1)} %get-tuple-element.113), channel_id=2, replica_groups=mesh['row'=8,'col'=4] {'col'}, use_global_device_ids=true, to_apply=%region_7.8.clone | all-reduce | flops 192 | bytes 1536
  82.2 0.7 dynamic-slice_multiply_fusion
  (25 shorter events, 0.6 us)
Async XLA Ops:
  14.4 47.4 %copy-start = (f32[1024]{0:T(1024)S(1)}, f32[1024]{0:T(1024)}, u32[]{:S(2)}) copy-start(f32[1024]{0:T(1024)} %param.6) | copy-start | bytes 12292
where the time goes:
time: 83.2 us; the launch traced here: 82.8 us
  blocking collectives  67.5 us (81%)
  local copies, waits for them, and re-layouts  9.27 us (11%)
  other arithmetic  3.87 us (5%)
  between operations  2 us (2%)
    all_gather x1, blocking collectives, shards(): lax.all_gather(phase, 'row', axis=1, tiled=True)  24.6 us
    unnamed x2, blocking collectives  18.3 us
    psum x1, blocking collectives, shards(): targets = lax.psum(picked, 'col')  17 us
    all_gather x1, blocking collectives, shards(): lax.all_gather(mass, 'row', axis=0, tiled=True)  7.59 us
    unnamed x7, local copies, waits for them, and re-layouts  6.09 us
    gather x1, local copies, waits for them, and re-layouts, select_stars(): picked = jnp.take(source, jnp.clip(offsets, 0, columns - 1), axis=1)  2.76 us

commit v1 on v0

v1 whole, which is shorter than its diff:
```python
import functools

import jax
import jax.numpy as jnp
from jax import lax
from jax.experimental import pallas as pl
from jax.experimental.pallas import tpu as pltpu
from jax.sharding import PartitionSpec as P

SOFTENING = 0.0001
LANES = 128


def pack_kernel(phase_ref, mass_ref, packed_ref):
    rows = packed_ref.shape[1]
    for part in range(6):
        for at in range(rows):
            packed_ref[part, at : at + 1, :] = phase_ref[part : part + 1, at * LANES : (at + 1) * LANES]
    packed_ref[6] = mass_ref[...]


def pack(phase, mass):
    rows = phase.shape[1] // LANES
    return pl.pallas_call(
        pack_kernel,
        out_shape=jax.ShapeDtypeStruct((7, rows, LANES), jnp.float32),
        in_specs=[pl.BlockSpec(memory_space=pltpu.VMEM)] * 2,
        out_specs=pl.BlockSpec(memory_space=pltpu.VMEM),
    )(phase, mass.reshape(rows, LANES))


def sweep_kernel(row_count, col_count, active_ref, stars_ref, accels_ref, jerks_ref):
    slots, _, rows, _ = stars_ref.shape
    count = active_ref.shape[0]
    col_at = lax.axis_index("col")
    lane = lax.broadcasted_iota(jnp.int32, (1, LANES), 1)
    picked = [[] for _ in range(6)]
    for target in range(count):
        star = active_ref[target]
        block = star // (rows * LANES)
        slot = (block % row_count) * col_count + ((block // row_count) ^ col_at)
        row = (star // LANES) % rows
        hit = lane == star % LANES
        for part in range(6):
            line = stars_ref[slot, part, pl.ds(row, 1), :]
            picked[part].append(jnp.where(hit, line, 0.0))
    targets = []
    for part in range(6):
        value = jnp.sum(jnp.concatenate(picked[part], axis=0), axis=1, keepdims=True)
        targets.append(jnp.broadcast_to(value, (count, LANES)))

    def add_slot(slot, sums):
        sums = list(sums)
        for row in range(rows):
            source = [
                jnp.broadcast_to(stars_ref[slot, part, row : row + 1, :], (count, LANES))
                for part in range(7)
            ]
            offset = [source[k] - targets[k] for k in range(3)]
            vel_diff = [source[k + 3] - targets[k + 3] for k in range(3)]
            dist_sq = offset[0] * offset[0] + offset[1] * offset[1] + offset[2] * offset[2] + SOFTENING
            along = offset[0] * vel_diff[0] + offset[1] * vel_diff[1] + offset[2] * vel_diff[2]
            inverse = lax.rsqrt(dist_sq)
            inverse_sq = inverse * inverse
            weight = source[6] * inverse * inverse_sq
            pull = weight * (along * inverse_sq)
            for k in range(3):
                sums[k] = sums[k] + weight * offset[k]
                sums[k + 3] = sums[k + 3] + weight * vel_diff[k]
                sums[k + 6] = sums[k + 6] + pull * offset[k]
        return tuple(sums)

    zeros = jnp.zeros((count, LANES), jnp.float32)
    sums = lax.fori_loop(0, slots, add_slot, (zeros,) * 9)
    norming = 1.0 / (slots * rows * LANES)
    out = zeros
    for k in range(6):
        total = sums[k] if k < 3 else sums[k] - 3.0 * sums[k + 3]
        out = jnp.where(lane == k, jnp.sum(total, axis=1, keepdims=True) * norming, out)
    out = out.T
    accels_ref[...] = out[0:3, :]
    jerks_ref[...] = out[3:6, :]


def sweep(active, stars, row_count, col_count):
    count = active.shape[0]
    return pl.pallas_call(
        functools.partial(sweep_kernel, row_count, col_count),
        out_shape=[jax.ShapeDtypeStruct((3, count), jnp.float32)] * 2,
        in_specs=[pl.BlockSpec(memory_space=pltpu.SMEM), pl.BlockSpec(memory_space=pltpu.VMEM)],
        out_specs=[pl.BlockSpec(memory_space=pltpu.VMEM)] * 2,
        compiler_params=pltpu.CompilerParams(vmem_limit_bytes=40 * 1024 * 1024),
    )(active, stars)


def shards(phase, mass, active):
    row_count = lax.axis_size("row")
    col_count = lax.axis_size("col")
    own = pack(phase, mass)
    blocks = [own]
    for step in range(1, col_count):
        blocks.append(lax.ppermute(own, "col", [(at, at ^ step) for at in range(col_count)]))
    stars = lax.all_gather(jnp.stack(blocks), "row", axis=0, tiled=True)
    return sweep(active, stars, row_count, col_count)


def solution(mesh):
    in_specs = (P(None, ("col", "row")), P(("col", "row")), P(("row", "col")))
    out_specs = (P(None, ("row", "col")), P(None, ("row", "col")))
    return jax.shard_map(shards, mesh=mesh, in_specs=in_specs, out_specs=out_specs, check_vma=False)
```

time: 83.2 us -> 26.9 us (0.32)
  blocking collectives: 67.5 us -> 10.7 us
  local copies, waits for them, and re-layouts: 9.27 us -> 0.01 us
  starting transfers between devices: 0 us -> 5.62 us
  Pallas kernels: 0 us -> 4.48 us
  waiting for transfers between devices: 0 us -> 4.41 us
  other arithmetic: 3.87 us -> 0.76 us
  between operations: 2 us -> 0.64 us
    all_gather x2 -> x1, blocking collectives: 32.2 us -> 10.7 us  [shards(): stars = lax.all_gather(jnp.stack(blocks), 'row', axis=0, tiled=True)]
    unnamed x2 -> x0, blocking collectives: 18.3 us -> none
    psum x1 -> x0, blocking collectives: 17 us -> none  [shards(): targets = lax.psum(picked, 'col')]
    unnamed x7 -> x2, local copies, waits for them, and re-layouts: 6.09 us -> 0.01 us
    ppermute x0 -> x3, starting transfers between devices: none -> 5.62 us  [shards(): lax.ppermute(own, 'col', [(at, at ^ step) for at in range(col_count)])]
    pallas_call x0 -> x2, Pallas kernels: none -> 4.48 us  [the longest x1 3.11 us: sweep(): pl.pallas_call(functools.partial(sweep_kernel, row_count, col_count), out...]
    ppermute x0 -> x3, waiting for transfers between devices: none -> 4.41 us  [shards(): lax.ppermute(own, 'col', [(at, at ^ step) for at in range(col_count)])]
    reduce_sum x8 -> x0, other arithmetic: 2.79 us -> none  [the longest x4 1.64 us: pair_terms(): jerks = jnp.sum(weight[None] * (vel_diff - radial[None] * offset), axis=-1)]
  transfers between devices with their start and end apart: 0 -> 3, of which waited for: 0 -> 2; matrix products, arithmetic and copies ran while one was open for 0% -> 0% of each run, Pallas kernels for 0% -> 0%
where the time goes in v1:
time: 26.9 us; the launch traced here: 26.6 us
  blocking collectives  10.7 us (40%)
  starting transfers between devices  5.62 us (21%)
  Pallas kernels  4.48 us (17%)
  waiting for transfers between devices  4.41 us (16%)
  other arithmetic  0.76 us (3%)
  between operations  0.64 us (2%)
    all_gather x1, blocking collectives, shards(): stars = lax.all_gather(jnp.stack(blocks), 'row', axis=0, tiled=True)  10.7 us
    ppermute x3, starting transfers between devices, shards(): lax.ppermute(own, 'col', [(at, at ^ step) for at in range(col_count)])  5.62 us
    ppermute x3, waiting for transfers between devices, shards(): lax.ppermute(own, 'col', [(at, at ^ step) for at in range(col_count)])  4.41 us
    pallas_call x1, Pallas kernels, sweep(): pl.pallas_call(functools.partial(sweep_kernel, row_count, col_count), out...  3.11 us
    pallas_call x1, Pallas kernels, pack(): pl.pallas_call(pack_kernel, out_shape=jax.ShapeDtypeStruct((7, rows, LANE...  1.38 us
    another operation x1, other arithmetic, shards(): stars = lax.all_gather(jnp.stack(blocks), 'row', axis=0, tiled=True)  0.76 us
  transfers between devices with their start and end apart: 3, of which 2 were waited for; matrix products, arithmetic and copies ran while one was open for 0% of the time, Pallas kernels for 0%

profile of v1, /device:TPU:0, one launch (start us, length us, event | category | flops | bytes accessed | tf_op | source)
XLA Modules:
  0.0 26.6 jit_solution(15058822262677801649)
XLA Ops:
  0.6 1.4 %shard_map.50 = f32[7,8,128]{2,1,0:T(8,128)} custom-call(f32[6,1024]{1,0:T(8,128)} %phase_ref.1, f32[8,128]{1,0:T(8,128)} %bitcast.9), custom_call_target="tpu_custom_call" | custom-call | tf_op jit(solution)/shard_map/pallas_call | solution.py:24
  2.0 5.0 %collective-permute-start.2 = (f32[7,8,128]{2,1,0:T(8,128)}, f32[7,8,128]{2,1,0:T(8,128)S(1)}, u32[]{:S(2)}, u32[]{:S(2)}) collective-permute-start(f32[7,8,128]{2,1,0:T(8,128)} %shard_map.50), channel_id=1, source_target_pairs={{0,3},{1,2},{2,1},{3,0},{4,7},{5,6},{6,5},{7,4},{8,11},{9,10},{10,... | collective-permute-start | bytes 86024 | tf_op jit(solution)/shard_map/ppermute | solution.py:102
  7.1 0.0 collective-permute-start.1
  7.1 0.6 %collective-permute-start = (f32[7,8,128]{2,1,0:T(8,128)}, f32[7,8,128]{2,1,0:T(8,128)S(1)}, u32[]{:S(2)}, u32[]{:S(2)}) collective-permute-start(f32[7,8,128]{2,1,0:T(8,128)} %shard_map.50), channel_id=1, source_target_pairs={{0,1},{1,0},{2,3},{3,2},{4,5},{5,4},{6,7},{7,6},{8,9},{9,8},{10,11... | collective-permute-start | bytes 86024 | tf_op jit(solution)/shard_map/ppermute | solution.py:102
  7.6 1.5 %collective-permute-done.2 = f32[7,8,128]{2,1,0:T(8,128)S(1)} collective-permute-done((f32[7,8,128]{2,1,0:T(8,128)}, f32[7,8,128]{2,1,0:T(8,128)S(1)}, u32[]{:S(2)}, u32[]{:S(2)}) %collective-permute-start.2) | collective-permute-done | bytes 28704 | tf_op jit(solution)/shard_map/ppermute | solution.py:102
  9.1 2.9 %collective-permute-done.1 = f32[7,8,128]{2,1,0:T(8,128)S(1)} collective-permute-done((f32[7,8,128]{2,1,0:T(8,128)}, f32[7,8,128]{2,1,0:T(8,128)S(1)}, u32[]{:S(2)}, u32[]{:S(2)}) %collective-permute-start.1) | collective-permute-done | bytes 28704 | tf_op jit(solution)/shard_map/ppermute | solution.py:102
  12.0 0.0 collective-permute-done
  12.0 0.8 %pad_maximum_fusion = f32[4,7,8,128]{3,2,1,0:T(8,128)S(1)} fusion(f32[1,7,8,128]{3,2,1,0:T(8,128)S(1)} %bitcast.6, f32[1,7,8,128]{3,2,1,0:T(8,128)S(1)} %bitcast.7, f32[1,7,8,128]{3,2,1,0:T(8,128)S(1)} %bitcast.8, f32[1,7,8,128]{3,2,1,0:T(8,128)} %bitcast.5), kind=kLoop, calls=%fused_computation | loop fusion | flops 86016 | bytes 229376 | tf_op jit(solution)/shard_map/stack | solution.py:103
  12.8 0.0 copy-start
  12.8 10.7 %all_gather.3.stars_ref = f32[32,7,8,128]{3,2,1,0:T(8,128)S(1)} all-gather(f32[4,7,8,128]{3,2,1,0:T(8,128)S(1)} %pad_maximum_fusion), channel_id=1, replica_groups=mesh['row'=8,'col'=4] {'row'}, dimensions={0}, use_global_device_ids=true | all-gather | bytes 1032192 | tf_op jit(solution)/shard_map/all_gather | solution.py:103
  23.5 0.0 copy-done
  23.5 3.1 %shard_map.51 = (f32[3,8]{1,0:T(4,128)}, f32[3,8]{1,0:T(4,128)}) custom-call(s32[8]{0:T(128)S(1)} %copy-done, f32[32,7,8,128]{3,2,1,0:T(8,128)S(1)} %all_gather.3.stars_ref), custom_call_target="tpu_custom_call" | custom-call | tf_op jit(solution)/shard_map/pallas_call | solution.py:87
Async XLA Ops:
  2.0 7.1 %collective-permute-start.2 = (f32[7,8,128]{2,1,0:T(8,128)}, f32[7,8,128]{2,1,0:T(8,128)S(1)}, u32[]{:S(2)}, u32[]{:S(2)}) collective-permute-start(f32[7,8,128]{2,1,0:T(8,128)} %shard_map.50), channel_id=1, source_target_pairs={{0,3},{1,2},{2,1},{3,0},{4,7},{5,6},{6,5},{7,4},{8,11},{9,10},{10,... | collective-permute-start | bytes 86024 | tf_op jit(solution)/shard_map/ppermute | solution.py:102
  7.1 5.0 %collective-permute-start.1 = (f32[7,8,128]{2,1,0:T(8,128)}, f32[7,8,128]{2,1,0:T(8,128)S(1)}, u32[]{:S(2)}, u32[]{:S(2)}) collective-permute-start(f32[7,8,128]{2,1,0:T(8,128)} %shard_map.50), channel_id=1, source_target_pairs={{0,2},{1,3},{2,0},{3,1},{4,6},{5,7},{6,4},{7,5},{8,10},{9,11},{10,... | collective-permute-start | bytes 86024 | tf_op jit(solution)/shard_map/ppermute | solution.py:102
  7.1 5.0 %collective-permute-start = (f32[7,8,128]{2,1,0:T(8,128)}, f32[7,8,128]{2,1,0:T(8,128)S(1)}, u32[]{:S(2)}, u32[]{:S(2)}) collective-permute-start(f32[7,8,128]{2,1,0:T(8,128)} %shard_map.50), channel_id=1, source_target_pairs={{0,1},{1,0},{2,3},{3,2},{4,5},{5,4},{6,7},{7,6},{8,9},{9,8},{10,11... | collective-permute-start | bytes 86024 | tf_op jit(solution)/shard_map/ppermute | solution.py:102
  12.8 10.7 %copy-start = (s32[8]{0:T(128)S(1)}, s32[8]{0:T(128)}, u32[]{:S(2)}) copy-start(s32[8]{0:T(128)} %active_ref.1) | copy-start | bytes 100

commit v2 on v1

v2 whole, which is shorter than its diff:
```python
import functools
import math

import jax
import jax.numpy as jnp
from jax import lax
from jax.experimental import pallas as pl
from jax.experimental.pallas import tpu as pltpu
from jax.sharding import PartitionSpec as P

SOFTENING = 0.0001
LANES = 128


def exchange_order(count):
    return sorted(range(1, count), key=lambda mask: (-mask.bit_length(), mask))


def swap(values, axis, mask):
    return lax.ppermute(values, axis, [(at, at ^ mask) for at in range(lax.axis_size(axis))])


def add_pairs(source, targets, sums):
    offset = [source[k] - targets[k] for k in range(3)]
    vel_diff = [source[k + 3] - targets[k + 3] for k in range(3)]
    dist_sq = offset[0] * offset[0] + offset[1] * offset[1] + offset[2] * offset[2] + SOFTENING
    along = offset[0] * vel_diff[0] + offset[1] * vel_diff[1] + offset[2] * vel_diff[2]
    inverse = lax.rsqrt(dist_sq)
    inverse_sq = inverse * inverse
    weight = source[6] * inverse * inverse_sq
    pull = weight * (along * inverse_sq)
    sums = list(sums)
    for k in range(3):
        sums[k] = sums[k] + weight * offset[k]
        sums[k + 3] = sums[k + 3] + weight * vel_diff[k]
        sums[k + 6] = sums[k + 6] + pull * offset[k]
    return tuple(sums)


def sweep_kernel(row_count, masks, active_ref, *refs):
    stacks, (accels_ref, jerks_ref) = refs[: len(masks)], refs[len(masks) :]
    slots, _, rows, _ = stacks[0].shape
    count = active_ref.shape[1]
    row_at, col_at = lax.axis_index("row"), lax.axis_index("col")
    lane = lax.broadcasted_iota(jnp.int32, (1, LANES), 1)
    place = lax.broadcasted_iota(jnp.int32, (1, count), 1)
    active = active_ref[...].astype(jnp.float32)
    picked = [[] for _ in range(6)]
    for target in range(count):
        star = jnp.sum(jnp.where(place == target, active, 0.0)).astype(jnp.int32)
        block = star // (rows * LANES)
        slot = (block // row_count) ^ col_at
        mask = (block % row_count) ^ row_at
        row = (star // LANES) % rows
        hit = lane == star % LANES
        for part in range(6):
            line = stacks[0][slot, part, pl.ds(row, 1), :]
            for at in range(1, len(masks)):
                line = jnp.where(mask == masks[at], stacks[at][slot, part, pl.ds(row, 1), :], line)
            picked[part].append(jnp.where(hit, line, 0.0))
    targets = []
    for part in range(6):
        value = jnp.sum(jnp.concatenate(picked[part], axis=0), axis=1, keepdims=True)
        targets.append(jnp.broadcast_to(value, (count, LANES)))

    zeros = jnp.zeros((count, LANES), jnp.float32)
    sums = (zeros,) * 9
    unroll = math.gcd(slots, 4)
    for stack in stacks:

        def add_slots(step, sums, stack=stack):
            for at in range(unroll):
                for row in range(rows):
                    source = [
                        jnp.broadcast_to(stack[step * unroll + at, part, row : row + 1, :], (count, LANES))
                        for part in range(7)
                    ]
                    sums = add_pairs(source, targets, sums)
            return sums

        sums = lax.fori_loop(0, slots // unroll, add_slots, sums)
    norming = 1.0 / (len(masks) * slots * rows * LANES)
    out = zeros
    for k in range(6):
        total = sums[k] if k < 3 else sums[k] - 3.0 * sums[k + 3]
        out = jnp.where(lane == k, jnp.sum(total, axis=1, keepdims=True) * norming, out)
    out = out.T
    accels_ref[...] = out[0:3, :]
    jerks_ref[...] = out[3:6, :]


def sweep(active, stacks, masks, row_count):
    count = active.shape[0]
    return pl.pallas_call(
        functools.partial(sweep_kernel, row_count, masks),
        out_shape=[jax.ShapeDtypeStruct((3, count), jnp.float32)] * 2,
        in_specs=[pl.BlockSpec(memory_space=pltpu.VMEM)] * (len(stacks) + 1),
        out_specs=[pl.BlockSpec(memory_space=pltpu.VMEM)] * 2,
        compiler_params=pltpu.CompilerParams(vmem_limit_bytes=40 * 1024 * 1024),
    )(active.reshape(1, count), *stacks)


def shards(phase, mass, active):
    row_count = lax.axis_size("row")
    col_count = lax.axis_size("col")
    rows = phase.shape[1] // LANES
    own = jnp.concatenate([phase.reshape(6, rows, LANES), mass.reshape(1, rows, LANES)], axis=0)
    stack = lax.dynamic_update_slice(jnp.zeros((col_count,) + own.shape, jnp.float32), own[None], (0, 0, 0, 0))
    for mask in exchange_order(col_count):
        stack = lax.dynamic_update_slice(stack, swap(own, "col", mask)[None], (mask, 0, 0, 0))
    stacks, masks = [], []
    for mask in [0] + [2 * mask for mask in reversed(exchange_order(row_count // 2))]:
        held = stack if mask == 0 else swap(stack, "row", mask)
        stacks += [held, swap(held, "row", 1)]
        masks += [mask, mask + 1]
    return sweep(active, stacks, masks, row_count)


def solution(mesh):
    in_specs = (P(None, ("col", "row")), P(("col", "row")), P(("row", "col")))
    out_specs = (P(None, ("row", "col")), P(None, ("row", "col")))
    return jax.shard_map(shards, mesh=mesh, in_specs=in_specs, out_specs=out_specs, check_vma=False)
```

time: 26.9 us -> 23.6 us (0.88)
  blocking collectives: 10.7 us -> 0 us
  waiting for transfers between devices: 4.41 us -> 9.64 us
  starting transfers between devices: 5.62 us -> 9.24 us
  Pallas kernels: 4.48 us -> 3.05 us
  local copies, waits for them, and re-layouts: 0.01 us -> 0.8 us
  other arithmetic: 0.76 us -> 0.01 us
    all_gather x1 -> x0, blocking collectives: 10.7 us -> none  [shards(): stars = lax.all_gather(jnp.stack(blocks), 'row', axis=0, tiled=True)]
    ppermute x3 -> x10, waiting for transfers between devices: 4.41 us -> 9.64 us  [swap(): lax.ppermute(values, axis, [(at, at ^ mask) for at in range(lax.axis_size...]
    ppermute x3 -> x10, starting transfers between devices: 5.62 us -> 9.24 us  [swap(): lax.ppermute(values, axis, [(at, at ^ mask) for at in range(lax.axis_size...]
    pallas_call x2 -> x1, Pallas kernels: 4.48 us -> 3.05 us  [sweep(): pl.pallas_call(functools.partial(sweep_kernel, row_count, masks), out_sha...]
    unnamed x2 -> x5, local copies, waits for them, and re-layouts: 0.01 us -> 0.78 us
    another operation x1 -> x0, other arithmetic: 0.76 us -> none  [shards(): stars = lax.all_gather(jnp.stack(blocks), 'row', axis=0, tiled=True)]
  transfers between devices with their start and end apart: 3 -> 10, of which waited for: 2 -> 7; matrix products, arithmetic and copies ran while one was open for 0% -> 0% of each run, Pallas kernels for 0% -> 0%
where the time goes in v2:
time: 23.6 us; the launch traced here: 23.4 us
  waiting for transfers between devices  9.64 us (41%)
  starting transfers between devices  9.24 us (39%)
  Pallas kernels  3.05 us (13%)
  local copies, waits for them, and re-layouts  0.8 us (3%)
  between operations  0.67 us (3%)
    ppermute x10, waiting for transfers between devices, swap(): lax.ppermute(values, axis, [(at, at ^ mask) for at in range(lax.axis_size...  9.64 us
    ppermute x10, starting transfers between devices, swap(): lax.ppermute(values, axis, [(at, at ^ mask) for at in range(lax.axis_size...  9.24 us
    pallas_call x1, Pallas kernels, sweep(): pl.pallas_call(functools.partial(sweep_kernel, row_count, masks), out_sha...  3.05 us
    unnamed x5, local copies, waits for them, and re-layouts  0.78 us
  transfers between devices with their start and end apart: 10, of which 7 were waited for; matrix products, arithmetic and copies ran while one was open for 0% of the time, Pallas kernels for 0%

profile of v2, /device:TPU:0, one launch (start us, length us, event | category | flops | bytes accessed | tf_op | source)
XLA Modules:
  0.0 23.4 jit_solution(16085086674934501672)
XLA Ops:
  0.6 0.0 copy-start.1
  0.6 0.8 %copy.7 = f32[1,6,8,128]{3,2,1,0:T(8,128)S(1)} copy(f32[1,6,8,128]{3,1,2,0:T(8,128)} %bitcast.16) | data formatting | bytes 49152
  1.4 4.1 %collective-permute-start = (f32[7,8,128]{2,1,0:T(8,128)S(1)}, f32[7,8,128]{2,1,0:T(8,128)S(1)}, u32[]{:S(2)}, u32[]{:S(2)}) collective-permute-start(f32[7,8,128]{2,1,0:T(8,128)S(1)} %get-tuple-element.2), channel_id=1, source_target_pairs={{0,2},{1,3},{2,0},{3,1},{4,6},{5,7},{6,4},{7,5},{8,10},{9,11},{10,... | collective-permute-start | bytes 86024 | tf_op jit(solution)/shard_map/ppermute | solution.py:20
  5.5 1.3 %collective-permute-start.1 = (f32[7,8,128]{2,1,0:T(8,128)S(1)}, f32[7,8,128]{2,1,0:T(8,128)S(1)}, u32[]{:S(2)}, u32[]{:S(2)}) collective-permute-start(f32[7,8,128]{2,1,0:T(8,128)S(1)} %get-tuple-element.2), channel_id=1, source_target_pairs={{0,3},{1,2},{2,1},{3,0},{4,7},{5,6},{6,5},{7,4},{8,11},{9,10},{10,... | collective-permute-start | bytes 86024 | tf_op jit(solution)/shard_map/ppermute | solution.py:20
  6.9 0.2 collective-permute-start.2
  7.1 0.3 %collective-permute-done = f32[7,8,128]{2,1,0:T(8,128)S(1)} collective-permute-done((f32[7,8,128]{2,1,0:T(8,128)S(1)}, f32[7,8,128]{2,1,0:T(8,128)S(1)}, u32[]{:S(2)}, u32[]{:S(2)}) %collective-permute-start) | collective-permute-done | bytes 28704 | tf_op jit(solution)/shard_map/ppermute | solution.py:20
  7.4 3.8 %collective-permute-done.1 = f32[7,8,128]{2,1,0:T(8,128)S(1)} collective-permute-done((f32[7,8,128]{2,1,0:T(8,128)S(1)}, f32[7,8,128]{2,1,0:T(8,128)S(1)}, u32[]{:S(2)}, u32[]{:S(2)}) %collective-permute-start.1) | collective-permute-done | bytes 28704 | tf_op jit(solution)/shard_map/ppermute | solution.py:20
  11.2 0.0 collective-permute-done.2
  11.2 0.0 copy-start
  11.2 1.6 %collective-permute-start.8 = (f32[4,7,8,128]{3,2,1,0:T(8,128)S(1)}, f32[4,7,8,128]{3,2,1,0:T(8,128)S(1)}, u32[]{:S(2)}, u32[]{:S(2)}) collective-permute-start(f32[4,7,8,128]{3,2,1,0:T(8,128)S(1)} %bitcast_dynamic-update-slice_fusion.refs_0_), channel_id=1, source_target_pairs={{0,16},{4,20},{8,24},{12,28},{16,0},{20,4},{24,8},{28,12},{1,17},{... | collective-permute-start | bytes 344072 | tf_op jit(solution)/shard_map/ppermute | solution.py:20
  12.8 1.4 %collective-permute-start.6 = (f32[4,7,8,128]{3,2,1,0:T(8,128)S(1)}, f32[4,7,8,128]{3,2,1,0:T(8,128)S(1)}, u32[]{:S(2)}, u32[]{:S(2)}) collective-permute-start(f32[4,7,8,128]{3,2,1,0:T(8,128)S(1)} %bitcast_dynamic-update-slice_fusion.refs_0_), channel_id=1, source_target_pairs={{0,24},{4,28},{8,16},{12,20},{16,8},{20,12},{24,0},{28,4},{1,25},{... | collective-permute-start | bytes 344072 | tf_op jit(solution)/shard_map/ppermute | solution.py:20
  14.2 0.5 %collective-permute-start.4 = (f32[4,7,8,128]{3,2,1,0:T(8,128)S(1)}, f32[4,7,8,128]{3,2,1,0:T(8,128)S(1)}, u32[]{:S(2)}, u32[]{:S(2)}) collective-permute-start(f32[4,7,8,128]{3,2,1,0:T(8,128)S(1)} %bitcast_dynamic-update-slice_fusion.refs_0_), channel_id=1, source_target_pairs={{0,8},{4,12},{8,0},{12,4},{16,24},{20,28},{24,16},{28,20},{1,9},{5... | collective-permute-start | bytes 344072 | tf_op jit(solution)/shard_map/ppermute | solution.py:20
  14.8 0.0 collective-permute-start.3
  14.8 2.1 %collective-permute-done.8.refs_6_ = f32[4,7,8,128]{3,2,1,0:T(8,128)S(1)} collective-permute-done((f32[4,7,8,128]{3,2,1,0:T(8,128)S(1)}, f32[4,7,8,128]{3,2,1,0:T(8,128)S(1)}, u32[]{:S(2)}, u32[]{:S(2)}) %collective-permute-start.8) | collective-permute-done | bytes 114720 | tf_op jit(solution)/shard_map/ppermute | solution.py:20
  16.9 0.0 collective-permute-start.9
  16.9 1.6 %collective-permute-done.6.refs_4_ = f32[4,7,8,128]{3,2,1,0:T(8,128)S(1)} collective-permute-done((f32[4,7,8,128]{3,2,1,0:T(8,128)S(1)}, f32[4,7,8,128]{3,2,1,0:T(8,128)S(1)}, u32[]{:S(2)}, u32[]{:S(2)}) %collective-permute-start.6) | collective-permute-done | bytes 114720 | tf_op jit(solution)/shard_map/ppermute | solution.py:20
  18.5 0.0 collective-permute-start.7
  18.5 0.5 %collective-permute-done.4.refs_2_ = f32[4,7,8,128]{3,2,1,0:T(8,128)S(1)} collective-permute-done((f32[4,7,8,128]{3,2,1,0:T(8,128)S(1)}, f32[4,7,8,128]{3,2,1,0:T(8,128)S(1)}, u32[]{:S(2)}, u32[]{:S(2)}) %collective-permute-start.4) | collective-permute-done | bytes 114720 | tf_op jit(solution)/shard_map/ppermute | solution.py:20
  19.0 0.0 collective-permute-start.5
  19.0 0.0 collective-permute-done.3.refs_1_
  19.0 0.0 collective-permute-done.9.refs_7_
  19.0 0.8 %collective-permute-done.7.refs_5_ = f32[4,7,8,128]{3,2,1,0:T(8,128)S(1)} collective-permute-done((f32[4,7,8,128]{3,2,1,0:T(8,128)S(1)}, f32[4,7,8,128]{3,2,1,0:T(8,128)S(1)}, u32[]{:S(2)}, u32[]{:S(2)}) %collective-permute-start.7) | collective-permute-done | bytes 114720 | tf_op jit(solution)/shard_map/ppermute | solution.py:20
  19.8 0.5 %collective-permute-done.5.refs_3_ = f32[4,7,8,128]{3,2,1,0:T(8,128)S(1)} collective-permute-done((f32[4,7,8,128]{3,2,1,0:T(8,128)S(1)}, f32[4,7,8,128]{3,2,1,0:T(8,128)S(1)}, u32[]{:S(2)}, u32[]{:S(2)}) %collective-permute-start.5) | collective-permute-done | bytes 114720 | tf_op jit(solution)/shard_map/ppermute | solution.py:20
  20.4 3.0 %shard_map.50 = (f32[3,8]{1,0:T(4,128)}, f32[3,8]{1,0:T(4,128)}) custom-call(s32[1,8]{1,0:T(1,128)S(1)} %bitcast.14, f32[4,7,8,128]{3,2,1,0:T(8,128)S(1)} %bitcast_dynamic-update-slice_fusion.refs_0_, f32[4,7,8,128]{3,2,1,0:T(8,128)S(1)} %collective-permute-done.3.refs_1_, f32[4,7,8,128]{3,2,1,0:T(8,128)S(1)} %collective-permute-done.4.refs_2_, ...), custom_call_target="tpu_custom_call" | custom-call | tf_op jit(solution)/shard_map/pallas_call | solution.py:94
  (7 shorter events, 0.0 us)
Async XLA Ops:
  0.6 0.8 %copy-start.1 = (f32[1024]{0:T(1024)S(1)}, f32[1024]{0:T(1024)}, u32[]{:S(2)}) copy-start(f32[1024]{0:T(1024)} %param.4) | copy-start | bytes 12292
  1.4 6.0 %collective-permute-start = (f32[7,8,128]{2,1,0:T(8,128)S(1)}, f32[7,8,128]{2,1,0:T(8,128)S(1)}, u32[]{:S(2)}, u32[]{:S(2)}) collective-permute-start(f32[7,8,128]{2,1,0:T(8,128)S(1)} %get-tuple-element.2), channel_id=1, source_target_pairs={{0,2},{1,3},{2,0},{3,1},{4,6},{5,7},{6,4},{7,5},{8,10},{9,11},{10,... | collective-permute-start | bytes 86024 | tf_op jit(solution)/shard_map/ppermute | solution.py:20
  5.5 5.7 %collective-permute-start.1 = (f32[7,8,128]{2,1,0:T(8,128)S(1)}, f32[7,8,128]{2,1,0:T(8,128)S(1)}, u32[]{:S(2)}, u32[]{:S(2)}) collective-permute-start(f32[7,8,128]{2,1,0:T(8,128)S(1)} %get-tuple-element.2), channel_id=1, source_target_pairs={{0,3},{1,2},{2,1},{3,0},{4,7},{5,6},{6,5},{7,4},{8,11},{9,10},{10,... | collective-permute-start | bytes 86024 | tf_op jit(solution)/shard_map/ppermute | solution.py:20
  6.9 4.3 %collective-permute-start.2 = (f32[7,8,128]{2,1,0:T(8,128)S(1)}, f32[7,8,128]{2,1,0:T(8,128)S(1)}, u32[]{:S(2)}, u32[]{:S(2)}) collective-permute-start(f32[7,8,128]{2,1,0:T(8,128)S(1)} %get-tuple-element.2), channel_id=1, source_target_pairs={{0,1},{1,0},{2,3},{3,2},{4,5},{5,4},{6,7},{7,6},{8,9},{9,8},{10,11... | collective-permute-start | bytes 86024 | tf_op jit(solution)/shard_map/ppermute | solution.py:20
  11.2 9.2 %copy-start = (s32[8]{0:T(128)S(1)}, s32[8]{0:T(128)}, u32[]{:S(2)}) copy-start(s32[8]{0:T(128)} %param.5) | copy-start | bytes 100
  11.2 5.7 %collective-permute-start.8 = (f32[4,7,8,128]{3,2,1,0:T(8,128)S(1)}, f32[4,7,8,128]{3,2,1,0:T(8,128)S(1)}, u32[]{:S(2)}, u32[]{:S(2)}) collective-permute-start(f32[4,7,8,128]{3,2,1,0:T(8,128)S(1)} %bitcast_dynamic-update-slice_fusion.refs_0_), channel_id=1, source_target_pairs={{0,16},{4,20},{8,24},{12,28},{16,0},{20,4},{24,8},{28,12},{1,17},{... | collective-permute-start | bytes 344072 | tf_op jit(solution)/shard_map/ppermute | solution.py:20
  12.8 5.7 %collective-permute-start.6 = (f32[4,7,8,128]{3,2,1,0:T(8,128)S(1)}, f32[4,7,8,128]{3,2,1,0:T(8,128)S(1)}, u32[]{:S(2)}, u32[]{:S(2)}) collective-permute-start(f32[4,7,8,128]{3,2,1,0:T(8,128)S(1)} %bitcast_dynamic-update-slice_fusion.refs_0_), channel_id=1, source_target_pairs={{0,24},{4,28},{8,16},{12,20},{16,8},{20,12},{24,0},{28,4},{1,25},{... | collective-permute-start | bytes 344072 | tf_op jit(solution)/shard_map/ppermute | solution.py:20
  14.2 4.8 %collective-permute-start.4 = (f32[4,7,8,128]{3,2,1,0:T(8,128)S(1)}, f32[4,7,8,128]{3,2,1,0:T(8,128)S(1)}, u32[]{:S(2)}, u32[]{:S(2)}) collective-permute-start(f32[4,7,8,128]{3,2,1,0:T(8,128)S(1)} %bitcast_dynamic-update-slice_fusion.refs_0_), channel_id=1, source_target_pairs={{0,8},{4,12},{8,0},{12,4},{16,24},{20,28},{24,16},{28,20},{1,9},{5... | collective-permute-start | bytes 344072 | tf_op jit(solution)/shard_map/ppermute | solution.py:20
  14.8 4.3 %collective-permute-start.3 = (f32[4,7,8,128]{3,2,1,0:T(8,128)S(1)}, f32[4,7,8,128]{3,2,1,0:T(8,128)S(1)}, u32[]{:S(2)}, u32[]{:S(2)}) collective-permute-start(f32[4,7,8,128]{3,2,1,0:T(8,128)S(1)} %bitcast_dynamic-update-slice_fusion.refs_0_), channel_id=1, source_target_pairs={{0,4},{4,0},{8,12},{12,8},{16,20},{20,16},{24,28},{28,24},{1,5},{5... | collective-permute-start | bytes 344072 | tf_op jit(solution)/shard_map/ppermute | solution.py:20
  16.9 2.2 %collective-permute-start.9 = (f32[4,7,8,128]{3,2,1,0:T(8,128)S(1)}, f32[4,7,8,128]{3,2,1,0:T(8,128)S(1)}, u32[]{:S(2)}, u32[]{:S(2)}) collective-permute-start(f32[4,7,8,128]{3,2,1,0:T(8,128)S(1)} %collective-permute-done.8.refs_6_), channel_id=1, source_target_pairs={{0,4},{4,0},{8,12},{12,8},{16,20},{20,16},{24,28},{28,24},{1,5},{5... | collective-permute-start | bytes 344072 | tf_op jit(solution)/shard_map/ppermute | solution.py:20
  18.5 1.3 %collective-permute-start.7 = (f32[4,7,8,128]{3,2,1,0:T(8,128)S(1)}, f32[4,7,8,128]{3,2,1,0:T(8,128)S(1)}, u32[]{:S(2)}, u32[]{:S(2)}) collective-permute-start(f32[4,7,8,128]{3,2,1,0:T(8,128)S(1)} %collective-permute-done.6.refs_4_), channel_id=1, source_target_pairs={{0,4},{4,0},{8,12},{12,8},{16,20},{20,16},{24,28},{28,24},{1,5},{5... | collective-permute-start | bytes 344072 | tf_op jit(solution)/shard_map/ppermute | solution.py:20
  19.0 1.3 %collective-permute-start.5 = (f32[4,7,8,128]{3,2,1,0:T(8,128)S(1)}, f32[4,7,8,128]{3,2,1,0:T(8,128)S(1)}, u32[]{:S(2)}, u32[]{:S(2)}) collective-permute-start(f32[4,7,8,128]{3,2,1,0:T(8,128)S(1)} %collective-permute-done.4.refs_2_), channel_id=1, source_target_pairs={{0,4},{4,0},{8,12},{12,8},{16,20},{20,16},{24,28},{28,24},{1,5},{5... | collective-permute-start | bytes 344072 | tf_op jit(solution)/shard_map/ppermute | solution.py:20

commit v3 on v2

v3 whole, which is shorter than its diff:
```python
import functools

import jax
import jax.numpy as jnp
from jax import lax
from jax.experimental import pallas as pl
from jax.experimental.pallas import tpu as pltpu
from jax.sharding import PartitionSpec as P

SOFTENING = 0.0001
LANES = 128
PARTS = 7


def bit_reverse(value, count):
    out = 0
    for _ in range(count.bit_length() - 1):
        out = 2 * out + value % 2
        value = value // 2
    return out


def shift_order(count):
    return sorted(range(1, count), key=lambda shift: (min(shift, count - shift), shift))


def mask_order(count):
    return sorted(range(1, count), key=lambda mask: (-bin(mask).count("1"), mask))


def shift_cols(values, shift):
    count = lax.axis_size("col")
    pairs = [(at, bit_reverse((bit_reverse(at, count) + shift) % count, count)) for at in range(count)]
    return lax.ppermute(values, "col", pairs)


def swap_rows(values, mask):
    return lax.ppermute(values, "row", [(at, at ^ mask) for at in range(lax.axis_size("row"))])


def add_pairs(source, targets, sums):
    offset = [source[k] - targets[k] for k in range(3)]
    vel_diff = [source[k + 3] - targets[k + 3] for k in range(3)]
    dist_sq = offset[0] * offset[0] + offset[1] * offset[1] + offset[2] * offset[2] + SOFTENING
    along = offset[0] * vel_diff[0] + offset[1] * vel_diff[1] + offset[2] * vel_diff[2]
    inverse = lax.rsqrt(dist_sq)
    inverse_sq = inverse * inverse
    weight = source[6] * inverse * inverse_sq
    pull = weight * (along * inverse_sq)
    sums = list(sums)
    for k in range(3):
        sums[k] = sums[k] + weight * offset[k]
        sums[k + 3] = sums[k + 3] + weight * vel_diff[k]
        sums[k + 6] = sums[k + 6] + pull * offset[k]
    return tuple(sums)


def sweep_kernel(row_count, col_count, masks, active_ref, *refs):
    stacks, (accels_ref, jerks_ref) = refs[: len(masks)], refs[len(masks) :]
    rows = stacks[0].shape[0] // (PARTS * col_count)
    count = active_ref.shape[1]
    row_at = lax.axis_index("row")
    col_at = bit_reverse(lax.axis_index("col"), col_count)
    lane = lax.broadcasted_iota(jnp.int32, (count, LANES), 1)
    place = lax.broadcasted_iota(jnp.int32, (count, LANES), 0)
    zeros = jnp.zeros((count, LANES), jnp.float32)

    def lines(stack, first):
        return [
            jnp.broadcast_to(stack[pl.ds(first + part * rows, 1), :], (count, LANES)) for part in range(PARTS)
        ]

    picked = [[zeros, zeros] for _ in range(6)]
    for target in range(count):
        star = active_ref[0, target]
        block = star // (rows * LANES)
        slot = (col_at - bit_reverse(block // row_count, col_count) + col_count) % col_count
        mask = (block % row_count) ^ row_at
        first = slot * (PARTS * rows) + (star // LANES) % rows
        for at, stack in enumerate(stacks):
            hit = (lane == jnp.where(mask == masks[at], star % LANES, -1)) & (place == target)
            line = lines(stack, first)
            for part in range(6):
                picked[part][at % 2] = jnp.where(hit, line[part], picked[part][at % 2])
    targets = [
        jnp.broadcast_to(jnp.sum(one + other, axis=1, keepdims=True), (count, LANES)) for one, other in picked
    ]

    sums = (zeros,) * 9
    for stack in stacks:

        def add_slot(slot, sums, stack=stack):
            for row in range(rows):
                sums = add_pairs(lines(stack, slot * (PARTS * rows) + row), targets, sums)
            return sums

        sums = lax.fori_loop(0, col_count, add_slot, sums)
    norming = 1.0 / (row_count * col_count * rows * LANES)
    out = zeros
    for k in range(6):
        total = sums[k] if k < 3 else sums[k] - 3.0 * sums[k + 3]
        out = jnp.where(lane == k, jnp.sum(total, axis=1, keepdims=True) * norming, out)
    out = out.T
    accels_ref[...] = out[0:3, :]
    jerks_ref[...] = out[3:6, :]


def sweep(active, stacks, masks, row_count, col_count):
    count = active.shape[0]
    return pl.pallas_call(
        functools.partial(sweep_kernel, row_count, col_count, masks),
        out_shape=[jax.ShapeDtypeStruct((3, count), jnp.float32)] * 2,
        in_specs=[pl.BlockSpec(memory_space=pltpu.VMEM)] * (len(stacks) + 1),
        out_specs=[pl.BlockSpec(memory_space=pltpu.VMEM)] * 2,
        compiler_params=pltpu.CompilerParams(vmem_limit_bytes=40 * 1024 * 1024),
    )(active.reshape(1, count), *[stack.reshape(-1, LANES) for stack in stacks])


def shards(phase, mass, active):
    row_count = lax.axis_size("row")
    col_count = lax.axis_size("col")
    rows = phase.shape[1] // LANES
    own = jnp.concatenate([phase.reshape(6, rows, LANES), mass.reshape(1, rows, LANES)], axis=0)
    stack = lax.dynamic_update_slice(jnp.zeros((col_count,) + own.shape, jnp.float32), own[None], (0, 0, 0, 0))
    for shift in shift_order(col_count):
        stack = lax.dynamic_update_slice(stack, shift_cols(own, shift)[None], (shift, 0, 0, 0))
    stacks, masks = [], []
    for mask in [0] + [2 * mask for mask in reversed(mask_order(row_count // 2))]:
        held = stack if mask == 0 else swap_rows(stack, mask)
        stacks += [held, swap_rows(held, 1)]
        masks += [mask, mask + 1]
    return sweep(active, stacks, masks, row_count, col_count)


def solution(mesh):
    in_specs = (P(None, ("col", "row")), P(("col", "row")), P(("row", "col")))
    out_specs = (P(None, ("row", "col")), P(None, ("row", "col")))
    return jax.shard_map(shards, mesh=mesh, in_specs=in_specs, out_specs=out_specs, check_vma=False)
```

time: 23.6 us -> 23.5 us (level)
  local copies, waits for them, and re-layouts: 0.8 us -> 1.45 us
  waiting for transfers between devices: 9.64 us -> 9.1 us
    unnamed x5, local copies, waits for them, and re-layouts: 0.78 us -> 1.43 us
    ppermute x10, waiting for transfers between devices: 9.64 us -> 9.1 us  [the longest x7 5.62 us: swap_rows(): lax.ppermute(values, 'row', [(at, at ^ mask) for at in range(lax.axis_siz...]
  transfers between devices with their start and end apart: 10 -> 10, of which waited for: 7 -> 8; matrix products, arithmetic and copies ran while one was open for 0% -> 0% of each run, Pallas kernels for 0% -> 0%
where the time goes in v3:
time: 23.5 us; the launch traced here: 23.3 us
  starting transfers between devices  9.17 us (39%)
  waiting for transfers between devices  9.1 us (39%)
  Pallas kernels  2.88 us (12%)
  local copies, waits for them, and re-layouts  1.45 us (6%)
  between operations  0.66 us (3%)
    ppermute x3, starting transfers between devices, shift_cols(): return lax.ppermute(values, 'col', pairs)  5.67 us
    ppermute x7, waiting for transfers between devices, swap_rows(): lax.ppermute(values, 'row', [(at, at ^ mask) for at in range(lax.axis_siz...  5.62 us
    ppermute x7, starting transfers between devices, swap_rows(): lax.ppermute(values, 'row', [(at, at ^ mask) for at in range(lax.axis_siz...  3.5 us
    ppermute x3, waiting for transfers between devices, shift_cols(): return lax.ppermute(values, 'col', pairs)  3.48 us
    pallas_call x1, Pallas kernels, sweep(): pl.pallas_call(functools.partial(sweep_kernel, row_count, col_count, mask...  2.88 us
    unnamed x5, local copies, waits for them, and re-layouts  1.43 us
  transfers between devices with their start and end apart: 10, of which 8 were waited for; matrix products, arithmetic and copies ran while one was open for 0% of the time, Pallas kernels for 0%

profile of v3, /device:TPU:0, one launch (start us, length us, event | category | flops | bytes accessed | tf_op | source)
XLA Modules:
  0.0 23.3 jit_solution(14596953050371831831)
XLA Ops:
  0.6 0.8 %copy.7 = f32[1,6,8,128]{3,2,1,0:T(8,128)S(1)} copy(f32[1,6,8,128]{3,1,2,0:T(8,128)} %bitcast.32) | data formatting | bytes 49152
  1.4 0.0 copy-done.1
  1.4 4.1 %collective-permute-start = (f32[7,8,128]{2,1,0:T(8,128)S(1)}, f32[7,8,128]{2,1,0:T(8,128)S(1)}, u32[]{:S(2)}, u32[]{:S(2)}) collective-permute-start(f32[7,8,128]{2,1,0:T(8,128)S(1)} %get-tuple-element.2), channel_id=1, source_target_pairs={{0,2},{1,3},{2,1},{3,0},{4,6},{5,7},{6,5},{7,4},{8,10},{9,11},{10,... | collective-permute-start | bytes 86024 | tf_op jit(solution)/shard_map/ppermute | solution.py:34
  5.5 1.1 %collective-permute-start.1 = (f32[7,8,128]{2,1,0:T(8,128)S(1)}, f32[7,8,128]{2,1,0:T(8,128)S(1)}, u32[]{:S(2)}, u32[]{:S(2)}) collective-permute-start(f32[7,8,128]{2,1,0:T(8,128)S(1)} %get-tuple-element.2), channel_id=1, source_target_pairs={{0,3},{1,2},{2,0},{3,1},{4,7},{5,6},{6,4},{7,5},{8,11},{9,10},{10,... | collective-permute-start | bytes 86024 | tf_op jit(solution)/shard_map/ppermute | solution.py:34
  6.6 0.5 %collective-permute-start.2 = (f32[7,8,128]{2,1,0:T(8,128)S(1)}, f32[7,8,128]{2,1,0:T(8,128)S(1)}, u32[]{:S(2)}, u32[]{:S(2)}) collective-permute-start(f32[7,8,128]{2,1,0:T(8,128)S(1)} %get-tuple-element.2), channel_id=1, source_target_pairs={{0,1},{1,0},{2,3},{3,2},{4,5},{5,4},{6,7},{7,6},{8,9},{9,8},{10,11... | collective-permute-start | bytes 86024 | tf_op jit(solution)/shard_map/ppermute | solution.py:34
  7.1 1.3 %collective-permute-done = f32[7,8,128]{2,1,0:T(8,128)S(1)} collective-permute-done((f32[7,8,128]{2,1,0:T(8,128)S(1)}, f32[7,8,128]{2,1,0:T(8,128)S(1)}, u32[]{:S(2)}, u32[]{:S(2)}) %collective-permute-start) | collective-permute-done | bytes 28704 | tf_op jit(solution)/shard_map/ppermute | solution.py:34
  8.4 1.9 %collective-permute-done.1 = f32[7,8,128]{2,1,0:T(8,128)S(1)} collective-permute-done((f32[7,8,128]{2,1,0:T(8,128)S(1)}, f32[7,8,128]{2,1,0:T(8,128)S(1)}, u32[]{:S(2)}, u32[]{:S(2)}) %collective-permute-start.1) | collective-permute-done | bytes 28704 | tf_op jit(solution)/shard_map/ppermute | solution.py:34
  10.3 0.3 %collective-permute-done.2 = f32[7,8,128]{2,1,0:T(8,128)S(1)} collective-permute-done((f32[7,8,128]{2,1,0:T(8,128)S(1)}, f32[7,8,128]{2,1,0:T(8,128)S(1)}, u32[]{:S(2)}, u32[]{:S(2)}) %collective-permute-start.2) | collective-permute-done | bytes 28704 | tf_op jit(solution)/shard_map/ppermute | solution.py:34
  10.6 2.5 %collective-permute-start.8 = (f32[4,7,8,128]{3,2,1,0:T(8,128)S(1)}, f32[4,7,8,128]{3,2,1,0:T(8,128)S(1)}, u32[]{:S(2)}, u32[]{:S(2)}) collective-permute-start(f32[4,7,8,128]{3,2,1,0:T(8,128)S(1)} %bitcast_dynamic-update-slice_fusion), channel_id=1, source_target_pairs={{0,24},{4,28},{8,16},{12,20},{16,8},{20,12},{24,0},{28,4},{1,25},{... | collective-permute-start | bytes 344072 | tf_op jit(solution)/shard_map/ppermute | solution.py:38
  13.1 0.5 %collective-permute-start.6 = (f32[4,7,8,128]{3,2,1,0:T(8,128)S(1)}, f32[4,7,8,128]{3,2,1,0:T(8,128)S(1)}, u32[]{:S(2)}, u32[]{:S(2)}) collective-permute-start(f32[4,7,8,128]{3,2,1,0:T(8,128)S(1)} %bitcast_dynamic-update-slice_fusion), channel_id=1, source_target_pairs={{0,8},{4,12},{8,0},{12,4},{16,24},{20,28},{24,16},{28,20},{1,9},{5... | collective-permute-start | bytes 344072 | tf_op jit(solution)/shard_map/ppermute | solution.py:38
  13.6 0.5 %collective-permute-start.4 = (f32[4,7,8,128]{3,2,1,0:T(8,128)S(1)}, f32[4,7,8,128]{3,2,1,0:T(8,128)S(1)}, u32[]{:S(2)}, u32[]{:S(2)}) collective-permute-start(f32[4,7,8,128]{3,2,1,0:T(8,128)S(1)} %bitcast_dynamic-update-slice_fusion), channel_id=1, source_target_pairs={{0,16},{4,20},{8,24},{12,28},{16,0},{20,4},{24,8},{28,12},{1,17},{... | collective-permute-start | bytes 344072 | tf_op jit(solution)/shard_map/ppermute | solution.py:38
  14.1 0.0 collective-permute-start.3
  14.1 2.3 %collective-permute-done.8 = f32[4,7,8,128]{3,2,1,0:T(8,128)S(1)} collective-permute-done((f32[4,7,8,128]{3,2,1,0:T(8,128)S(1)}, f32[4,7,8,128]{3,2,1,0:T(8,128)S(1)}, u32[]{:S(2)}, u32[]{:S(2)}) %collective-permute-start.8) | collective-permute-done | bytes 114720 | tf_op jit(solution)/shard_map/ppermute | solution.py:38
  16.4 0.0 collective-permute-start.9
  16.4 1.5 %collective-permute-done.6 = f32[4,7,8,128]{3,2,1,0:T(8,128)S(1)} collective-permute-done((f32[4,7,8,128]{3,2,1,0:T(8,128)S(1)}, f32[4,7,8,128]{3,2,1,0:T(8,128)S(1)}, u32[]{:S(2)}, u32[]{:S(2)}) %collective-permute-start.6) | collective-permute-done | bytes 114720 | tf_op jit(solution)/shard_map/ppermute | solution.py:38
  17.9 0.0 collective-permute-start.7
  17.9 0.5 %collective-permute-done.4 = f32[4,7,8,128]{3,2,1,0:T(8,128)S(1)} collective-permute-done((f32[4,7,8,128]{3,2,1,0:T(8,128)S(1)}, f32[4,7,8,128]{3,2,1,0:T(8,128)S(1)}, u32[]{:S(2)}, u32[]{:S(2)}) %collective-permute-start.4) | collective-permute-done | bytes 114720 | tf_op jit(solution)/shard_map/ppermute | solution.py:38
  18.4 0.0 collective-permute-start.5
  18.4 0.0 collective-permute-done.3
  18.4 0.0 collective-permute-done.9
  18.4 0.8 %collective-permute-done.7 = f32[4,7,8,128]{3,2,1,0:T(8,128)S(1)} collective-permute-done((f32[4,7,8,128]{3,2,1,0:T(8,128)S(1)}, f32[4,7,8,128]{3,2,1,0:T(8,128)S(1)}, u32[]{:S(2)}, u32[]{:S(2)}) %collective-permute-start.7) | collective-permute-done | bytes 114720 | tf_op jit(solution)/shard_map/ppermute | solution.py:38
  19.2 0.5 %collective-permute-done.5 = f32[4,7,8,128]{3,2,1,0:T(8,128)S(1)} collective-permute-done((f32[4,7,8,128]{3,2,1,0:T(8,128)S(1)}, f32[4,7,8,128]{3,2,1,0:T(8,128)S(1)}, u32[]{:S(2)}, u32[]{:S(2)}) %collective-permute-start.5) | collective-permute-done | bytes 114720 | tf_op jit(solution)/shard_map/ppermute | solution.py:38
  19.7 0.7 %copy-done = s32[8]{0:T(128)S(1)} copy-done((s32[8]{0:T(128)S(1)}, s32[8]{0:T(128)}, u32[]{:S(2)}) %copy-start) | copy-done | bytes 56
  20.4 2.9 %shard_map.50 = (f32[3,8]{1,0:T(4,128)}, f32[3,8]{1,0:T(4,128)}) custom-call(s32[1,8]{1,0:T(1,128)S(1)} %bitcast.30, f32[224,128]{1,0:T(8,128)S(1)} %bitcast.22, f32[224,128]{1,0:T(8,128)S(1)} %bitcast.26, f32[224,128]{1,0:T(8,128)S(1)} %bitcast.25, f32[224,128]{1,0:T(8,128)S(1)} %bitcast.29, f32[224,128]{1,0:T(8,128)S(1)} %bitcast.24, ...), custom_call_target="tpu_custom_call" | custom-call | tf_op jit(solution)/shard_map/pallas_call | solution.py:110
  (7 shorter events, 0.0 us)
Async XLA Ops:
  0.6 0.8 %copy-start.1 = (f32[1024]{0:T(1024)S(1)}, f32[1024]{0:T(1024)}, u32[]{:S(2)}) copy-start(f32[1024]{0:T(1024)} %param.4) | copy-start | bytes 12292
  1.4 7.0 %collective-permute-start = (f32[7,8,128]{2,1,0:T(8,128)S(1)}, f32[7,8,128]{2,1,0:T(8,128)S(1)}, u32[]{:S(2)}, u32[]{:S(2)}) collective-permute-start(f32[7,8,128]{2,1,0:T(8,128)S(1)} %get-tuple-element.2), channel_id=1, source_target_pairs={{0,2},{1,3},{2,1},{3,0},{4,6},{5,7},{6,5},{7,4},{8,10},{9,11},{10,... | collective-permute-start | bytes 86024 | tf_op jit(solution)/shard_map/ppermute | solution.py:34
  5.5 4.8 %collective-permute-start.1 = (f32[7,8,128]{2,1,0:T(8,128)S(1)}, f32[7,8,128]{2,1,0:T(8,128)S(1)}, u32[]{:S(2)}, u32[]{:S(2)}) collective-permute-start(f32[7,8,128]{2,1,0:T(8,128)S(1)} %get-tuple-element.2), channel_id=1, source_target_pairs={{0,3},{1,2},{2,0},{3,1},{4,7},{5,6},{6,4},{7,5},{8,11},{9,10},{10,... | collective-permute-start | bytes 86024 | tf_op jit(solution)/shard_map/ppermute | solution.py:34
  6.6 4.0 %collective-permute-start.2 = (f32[7,8,128]{2,1,0:T(8,128)S(1)}, f32[7,8,128]{2,1,0:T(8,128)S(1)}, u32[]{:S(2)}, u32[]{:S(2)}) collective-permute-start(f32[7,8,128]{2,1,0:T(8,128)S(1)} %get-tuple-element.2), channel_id=1, source_target_pairs={{0,1},{1,0},{2,3},{3,2},{4,5},{5,4},{6,7},{7,6},{8,9},{9,8},{10,11... | collective-permute-start | bytes 86024 | tf_op jit(solution)/shard_map/ppermute | solution.py:34
  10.6 5.8 %collective-permute-start.8 = (f32[4,7,8,128]{3,2,1,0:T(8,128)S(1)}, f32[4,7,8,128]{3,2,1,0:T(8,128)S(1)}, u32[]{:S(2)}, u32[]{:S(2)}) collective-permute-start(f32[4,7,8,128]{3,2,1,0:T(8,128)S(1)} %bitcast_dynamic-update-slice_fusion), channel_id=1, source_target_pairs={{0,24},{4,28},{8,16},{12,20},{16,8},{20,12},{24,0},{28,4},{1,25},{... | collective-permute-start | bytes 344072 | tf_op jit(solution)/shard_map/ppermute | solution.py:38
  13.1 4.8 %collective-permute-start.6 = (f32[4,7,8,128]{3,2,1,0:T(8,128)S(1)}, f32[4,7,8,128]{3,2,1,0:T(8,128)S(1)}, u32[]{:S(2)}, u32[]{:S(2)}) collective-permute-start(f32[4,7,8,128]{3,2,1,0:T(8,128)S(1)} %bitcast_dynamic-update-slice_fusion), channel_id=1, source_target_pairs={{0,8},{4,12},{8,0},{12,4},{16,24},{20,28},{24,16},{28,20},{1,9},{5... | collective-permute-start | bytes 344072 | tf_op jit(solution)/shard_map/ppermute | solution.py:38
  13.6 4.8 %collective-permute-start.4 = (f32[4,7,8,128]{3,2,1,0:T(8,128)S(1)}, f32[4,7,8,128]{3,2,1,0:T(8,128)S(1)}, u32[]{:S(2)}, u32[]{:S(2)}) collective-permute-start(f32[4,7,8,128]{3,2,1,0:T(8,128)S(1)} %bitcast_dynamic-update-slice_fusion), channel_id=1, source_target_pairs={{0,16},{4,20},{8,24},{12,28},{16,0},{20,4},{24,8},{28,12},{1,17},{... | collective-permute-start | bytes 344072 | tf_op jit(solution)/shard_map/ppermute | solution.py:38
  14.1 4.3 %collective-permute-start.3 = (f32[4,7,8,128]{3,2,1,0:T(8,128)S(1)}, f32[4,7,8,128]{3,2,1,0:T(8,128)S(1)}, u32[]{:S(2)}, u32[]{:S(2)}) collective-permute-start(f32[4,7,8,128]{3,2,1,0:T(8,128)S(1)} %bitcast_dynamic-update-slice_fusion), channel_id=1, source_target_pairs={{0,4},{4,0},{8,12},{12,8},{16,20},{20,16},{24,28},{28,24},{1,5},{5... | collective-permute-start | bytes 344072 | tf_op jit(solution)/shard_map/ppermute | solution.py:38
  16.4 2.0 %collective-permute-start.9 = (f32[4,7,8,128]{3,2,1,0:T(8,128)S(1)}, f32[4,7,8,128]{3,2,1,0:T(8,128)S(1)}, u32[]{:S(2)}, u32[]{:S(2)}) collective-permute-start(f32[4,7,8,128]{3,2,1,0:T(8,128)S(1)} %collective-permute-done.8), channel_id=1, source_target_pairs={{0,4},{4,0},{8,12},{12,8},{16,20},{20,16},{24,28},{28,24},{1,5},{5... | collective-permute-start | bytes 344072 | tf_op jit(solution)/shard_map/ppermute | solution.py:38
  17.9 1.3 %collective-permute-start.7 = (f32[4,7,8,128]{3,2,1,0:T(8,128)S(1)}, f32[4,7,8,128]{3,2,1,0:T(8,128)S(1)}, u32[]{:S(2)}, u32[]{:S(2)}) collective-permute-start(f32[4,7,8,128]{3,2,1,0:T(8,128)S(1)} %collective-permute-done.6), channel_id=1, source_target_pairs={{0,4},{4,0},{8,12},{12,8},{16,20},{20,16},{24,28},{28,24},{1,5},{5... | collective-permute-start | bytes 344072 | tf_op jit(solution)/shard_map/ppermute | solution.py:38
  18.4 1.3 %collective-permute-start.5 = (f32[4,7,8,128]{3,2,1,0:T(8,128)S(1)}, f32[4,7,8,128]{3,2,1,0:T(8,128)S(1)}, u32[]{:S(2)}, u32[]{:S(2)}) collective-permute-start(f32[4,7,8,128]{3,2,1,0:T(8,128)S(1)} %collective-permute-done.4), channel_id=1, source_target_pairs={{0,4},{4,0},{8,12},{12,8},{16,20},{20,16},{24,28},{28,24},{1,5},{5... | collective-permute-start | bytes 344072 | tf_op jit(solution)/shard_map/ppermute | solution.py:38
  19.7 0.7 %copy-start = (s32[8]{0:T(128)S(1)}, s32[8]{0:T(128)}, u32[]{:S(2)}) copy-start(s32[8]{0:T(128)} %param.5) | copy-start | bytes 100

commit v4 on v3

--- a/solution.py
+++ b/solution.py
@@ -57,7 +57,7 @@
 
 def sweep_kernel(row_count, col_count, masks, active_ref, *refs):
     stacks, (accels_ref, jerks_ref) = refs[: len(masks)], refs[len(masks) :]
-    rows = stacks[0].shape[0] // (PARTS * col_count)
+    rows = stacks[0].shape[2]
     count = active_ref.shape[1]
     row_at = lax.axis_index("row")
     col_at = bit_reverse(lax.axis_index("col"), col_count)
@@ -65,9 +65,9 @@
     place = lax.broadcasted_iota(jnp.int32, (count, LANES), 0)
     zeros = jnp.zeros((count, LANES), jnp.float32)
 
-    def lines(stack, first):
+    def lines(stack, slot, row):
         return [
-            jnp.broadcast_to(stack[pl.ds(first + part * rows, 1), :], (count, LANES)) for part in range(PARTS)
+            jnp.broadcast_to(stack[slot, part, pl.ds(row, 1), :], (count, LANES)) for part in range(PARTS)
         ]
 
     picked = [[zeros, zeros] for _ in range(6)]
@@ -76,10 +76,10 @@
         block = star // (rows * LANES)
         slot = (col_at - bit_reverse(block // row_count, col_count) + col_count) % col_count
         mask = (block % row_count) ^ row_at
-        first = slot * (PARTS * rows) + (star // LANES) % rows
+        row = (star // LANES) % rows
         for at, stack in enumerate(stacks):
             hit = (lane == jnp.where(mask == masks[at], star % LANES, -1)) & (place == target)
-            line = lines(stack, first)
+            line = lines(stack, slot, row)
             for part in range(6):
                 picked[part][at % 2] = jnp.where(hit, line[part], picked[part][at % 2])
     targets = [
@@ -91,7 +91,7 @@
 
         def add_slot(slot, sums, stack=stack):
             for row in range(rows):
-                sums = add_pairs(lines(stack, slot * (PARTS * rows) + row), targets, sums)
+                sums = add_pairs(lines(stack, slot, row), targets, sums)
             return sums
 
         sums = lax.fori_loop(0, col_count, add_slot, sums)
@@ -113,7 +113,7 @@
         in_specs=[pl.BlockSpec(memory_space=pltpu.VMEM)] * (len(stacks) + 1),
         out_specs=[pl.BlockSpec(memory_space=pltpu.VMEM)] * 2,
         compiler_params=pltpu.CompilerParams(vmem_limit_bytes=40 * 1024 * 1024),
-    )(active.reshape(1, count), *[stack.reshape(-1, LANES) for stack in stacks])
+    )(active.reshape(1, count), *stacks)
 
 
 def shards(phase, mass, active):

time: 23.5 us -> 22.8 us (0.970)
  local copies, waits for them, and re-layouts: 1.45 us -> 0.8 us
    unnamed x5, local copies, waits for them, and re-layouts: 1.43 us -> 0.78 us
where the time goes in v4:
time: 22.8 us; the launch traced here: 22.6 us
  starting transfers between devices  9.17 us (40%)
  waiting for transfers between devices  9.1 us (40%)
  Pallas kernels  2.88 us (13%)
  local copies, waits for them, and re-layouts  0.8 us (4%)
  between operations  0.66 us (3%)
    ppermute x3, starting transfers between devices, shift_cols(): return lax.ppermute(values, 'col', pairs)  5.67 us
    ppermute x7, waiting for transfers between devices, swap_rows(): lax.ppermute(values, 'row', [(at, at ^ mask) for at in range(lax.axis_siz...  5.62 us
    ppermute x7, starting transfers between devices, swap_rows(): lax.ppermute(values, 'row', [(at, at ^ mask) for at in range(lax.axis_siz...  3.5 us
    ppermute x3, waiting for transfers between devices, shift_cols(): return lax.ppermute(values, 'col', pairs)  3.48 us
    pallas_call x1, Pallas kernels, sweep(): pl.pallas_call(functools.partial(sweep_kernel, row_count, col_count, mask...  2.88 us
    unnamed x5, local copies, waits for them, and re-layouts  0.78 us
  transfers between devices with their start and end apart: 10, of which 8 were waited for; matrix products, arithmetic and copies ran while one was open for 0% of the time, Pallas kernels for 0%

profile of v4, /device:TPU:0, one launch (start us, length us, event | category | flops | bytes accessed | tf_op | source)
XLA Modules:
  0.0 22.6 jit_solution(15912045465578245799)
XLA Ops:
  0.6 0.0 copy-start.1
  0.6 0.8 %copy.7 = f32[1,6,8,128]{3,2,1,0:T(8,128)S(1)} copy(f32[1,6,8,128]{3,1,2,0:T(8,128)} %bitcast.16) | data formatting | bytes 49152
  1.4 0.0 copy-done.1
  1.4 4.1 %collective-permute-start = (f32[7,8,128]{2,1,0:T(8,128)S(1)}, f32[7,8,128]{2,1,0:T(8,128)S(1)}, u32[]{:S(2)}, u32[]{:S(2)}) collective-permute-start(f32[7,8,128]{2,1,0:T(8,128)S(1)} %get-tuple-element.2), channel_id=1, source_target_pairs={{0,2},{1,3},{2,1},{3,0},{4,6},{5,7},{6,5},{7,4},{8,10},{9,11},{10,... | collective-permute-start | bytes 86024 | tf_op jit(solution)/shard_map/ppermute | solution.py:34
  5.5 1.1 %collective-permute-start.1 = (f32[7,8,128]{2,1,0:T(8,128)S(1)}, f32[7,8,128]{2,1,0:T(8,128)S(1)}, u32[]{:S(2)}, u32[]{:S(2)}) collective-permute-start(f32[7,8,128]{2,1,0:T(8,128)S(1)} %get-tuple-element.2), channel_id=1, source_target_pairs={{0,3},{1,2},{2,0},{3,1},{4,7},{5,6},{6,4},{7,5},{8,11},{9,10},{10,... | collective-permute-start | bytes 86024 | tf_op jit(solution)/shard_map/ppermute | solution.py:34
  6.6 0.5 %collective-permute-start.2 = (f32[7,8,128]{2,1,0:T(8,128)S(1)}, f32[7,8,128]{2,1,0:T(8,128)S(1)}, u32[]{:S(2)}, u32[]{:S(2)}) collective-permute-start(f32[7,8,128]{2,1,0:T(8,128)S(1)} %get-tuple-element.2), channel_id=1, source_target_pairs={{0,1},{1,0},{2,3},{3,2},{4,5},{5,4},{6,7},{7,6},{8,9},{9,8},{10,11... | collective-permute-start | bytes 86024 | tf_op jit(solution)/shard_map/ppermute | solution.py:34
  7.1 1.3 %collective-permute-done = f32[7,8,128]{2,1,0:T(8,128)S(1)} collective-permute-done((f32[7,8,128]{2,1,0:T(8,128)S(1)}, f32[7,8,128]{2,1,0:T(8,128)S(1)}, u32[]{:S(2)}, u32[]{:S(2)}) %collective-permute-start) | collective-permute-done | bytes 28704 | tf_op jit(solution)/shard_map/ppermute | solution.py:34
  8.4 1.9 %collective-permute-done.1 = f32[7,8,128]{2,1,0:T(8,128)S(1)} collective-permute-done((f32[7,8,128]{2,1,0:T(8,128)S(1)}, f32[7,8,128]{2,1,0:T(8,128)S(1)}, u32[]{:S(2)}, u32[]{:S(2)}) %collective-permute-start.1) | collective-permute-done | bytes 28704 | tf_op jit(solution)/shard_map/ppermute | solution.py:34
  10.3 0.3 %collective-permute-done.2 = f32[7,8,128]{2,1,0:T(8,128)S(1)} collective-permute-done((f32[7,8,128]{2,1,0:T(8,128)S(1)}, f32[7,8,128]{2,1,0:T(8,128)S(1)}, u32[]{:S(2)}, u32[]{:S(2)}) %collective-permute-start.2) | collective-permute-done | bytes 28704 | tf_op jit(solution)/shard_map/ppermute | solution.py:34
  10.6 2.5 %collective-permute-start.8 = (f32[4,7,8,128]{3,2,1,0:T(8,128)S(1)}, f32[4,7,8,128]{3,2,1,0:T(8,128)S(1)}, u32[]{:S(2)}, u32[]{:S(2)}) collective-permute-start(f32[4,7,8,128]{3,2,1,0:T(8,128)S(1)} %bitcast_dynamic-update-slice_fusion.refs_0_), channel_id=1, source_target_pairs={{0,24},{4,28},{8,16},{12,20},{16,8},{20,12},{24,0},{28,4},{1,25},{... | collective-permute-start | bytes 344072 | tf_op jit(solution)/shard_map/ppermute | solution.py:38
  13.1 0.5 %collective-permute-start.6 = (f32[4,7,8,128]{3,2,1,0:T(8,128)S(1)}, f32[4,7,8,128]{3,2,1,0:T(8,128)S(1)}, u32[]{:S(2)}, u32[]{:S(2)}) collective-permute-start(f32[4,7,8,128]{3,2,1,0:T(8,128)S(1)} %bitcast_dynamic-update-slice_fusion.refs_0_), channel_id=1, source_target_pairs={{0,8},{4,12},{8,0},{12,4},{16,24},{20,28},{24,16},{28,20},{1,9},{5... | collective-permute-start | bytes 344072 | tf_op jit(solution)/shard_map/ppermute | solution.py:38
  13.6 0.5 %collective-permute-start.4 = (f32[4,7,8,128]{3,2,1,0:T(8,128)S(1)}, f32[4,7,8,128]{3,2,1,0:T(8,128)S(1)}, u32[]{:S(2)}, u32[]{:S(2)}) collective-permute-start(f32[4,7,8,128]{3,2,1,0:T(8,128)S(1)} %bitcast_dynamic-update-slice_fusion.refs_0_), channel_id=1, source_target_pairs={{0,16},{4,20},{8,24},{12,28},{16,0},{20,4},{24,8},{28,12},{1,17},{... | collective-permute-start | bytes 344072 | tf_op jit(solution)/shard_map/ppermute | solution.py:38
  14.1 0.0 collective-permute-start.3
  14.1 2.3 %collective-permute-done.8.refs_6_ = f32[4,7,8,128]{3,2,1,0:T(8,128)S(1)} collective-permute-done((f32[4,7,8,128]{3,2,1,0:T(8,128)S(1)}, f32[4,7,8,128]{3,2,1,0:T(8,128)S(1)}, u32[]{:S(2)}, u32[]{:S(2)}) %collective-permute-start.8) | collective-permute-done | bytes 114720 | tf_op jit(solution)/shard_map/ppermute | solution.py:38
  16.4 0.0 collective-permute-start.9
  16.4 1.5 %collective-permute-done.6.refs_4_ = f32[4,7,8,128]{3,2,1,0:T(8,128)S(1)} collective-permute-done((f32[4,7,8,128]{3,2,1,0:T(8,128)S(1)}, f32[4,7,8,128]{3,2,1,0:T(8,128)S(1)}, u32[]{:S(2)}, u32[]{:S(2)}) %collective-permute-start.6) | collective-permute-done | bytes 114720 | tf_op jit(solution)/shard_map/ppermute | solution.py:38
  17.9 0.0 collective-permute-start.7
  17.9 0.5 %collective-permute-done.4.refs_2_ = f32[4,7,8,128]{3,2,1,0:T(8,128)S(1)} collective-permute-done((f32[4,7,8,128]{3,2,1,0:T(8,128)S(1)}, f32[4,7,8,128]{3,2,1,0:T(8,128)S(1)}, u32[]{:S(2)}, u32[]{:S(2)}) %collective-permute-start.4) | collective-permute-done | bytes 114720 | tf_op jit(solution)/shard_map/ppermute | solution.py:38
  18.4 0.0 collective-permute-start.5
  18.4 0.0 collective-permute-done.3.refs_1_
  18.4 0.0 collective-permute-done.9.refs_7_
  18.4 0.8 %collective-permute-done.7.refs_5_ = f32[4,7,8,128]{3,2,1,0:T(8,128)S(1)} collective-permute-done((f32[4,7,8,128]{3,2,1,0:T(8,128)S(1)}, f32[4,7,8,128]{3,2,1,0:T(8,128)S(1)}, u32[]{:S(2)}, u32[]{:S(2)}) %collective-permute-start.7) | collective-permute-done | bytes 114720 | tf_op jit(solution)/shard_map/ppermute | solution.py:38
  19.2 0.5 %collective-permute-done.5.refs_3_ = f32[4,7,8,128]{3,2,1,0:T(8,128)S(1)} collective-permute-done((f32[4,7,8,128]{3,2,1,0:T(8,128)S(1)}, f32[4,7,8,128]{3,2,1,0:T(8,128)S(1)}, u32[]{:S(2)}, u32[]{:S(2)}) %collective-permute-start.5) | collective-permute-done | bytes 114720 | tf_op jit(solution)/shard_map/ppermute | solution.py:38
  19.7 2.9 %shard_map.50 = (f32[3,8]{1,0:T(4,128)}, f32[3,8]{1,0:T(4,128)}) custom-call(s32[1,8]{1,0:T(1,128)S(1)} %bitcast.14, f32[4,7,8,128]{3,2,1,0:T(8,128)S(1)} %bitcast_dynamic-update-slice_fusion.refs_0_, f32[4,7,8,128]{3,2,1,0:T(8,128)S(1)} %collective-permute-done.3.refs_1_, f32[4,7,8,128]{3,2,1,0:T(8,128)S(1)} %collective-permute-done.4.refs_2_, ...), custom_call_target="tpu_custom_call" | custom-call | tf_op jit(solution)/shard_map/pallas_call | solution.py:110
  (7 shorter events, 0.0 us)
Async XLA Ops:
  0.6 0.8 %copy-start.1 = (f32[1024]{0:T(1024)S(1)}, f32[1024]{0:T(1024)}, u32[]{:S(2)}) copy-start(f32[1024]{0:T(1024)} %param.4) | copy-start | bytes 12292
  1.4 7.0 %collective-permute-start = (f32[7,8,128]{2,1,0:T(8,128)S(1)}, f32[7,8,128]{2,1,0:T(8,128)S(1)}, u32[]{:S(2)}, u32[]{:S(2)}) collective-permute-start(f32[7,8,128]{2,1,0:T(8,128)S(1)} %get-tuple-element.2), channel_id=1, source_target_pairs={{0,2},{1,3},{2,1},{3,0},{4,6},{5,7},{6,5},{7,4},{8,10},{9,11},{10,... | collective-permute-start | bytes 86024 | tf_op jit(solution)/shard_map/ppermute | solution.py:34
  5.5 4.8 %collective-permute-start.1 = (f32[7,8,128]{2,1,0:T(8,128)S(1)}, f32[7,8,128]{2,1,0:T(8,128)S(1)}, u32[]{:S(2)}, u32[]{:S(2)}) collective-permute-start(f32[7,8,128]{2,1,0:T(8,128)S(1)} %get-tuple-element.2), channel_id=1, source_target_pairs={{0,3},{1,2},{2,0},{3,1},{4,7},{5,6},{6,4},{7,5},{8,11},{9,10},{10,... | collective-permute-start | bytes 86024 | tf_op jit(solution)/shard_map/ppermute | solution.py:34
  6.6 4.0 %collective-permute-start.2 = (f32[7,8,128]{2,1,0:T(8,128)S(1)}, f32[7,8,128]{2,1,0:T(8,128)S(1)}, u32[]{:S(2)}, u32[]{:S(2)}) collective-permute-start(f32[7,8,128]{2,1,0:T(8,128)S(1)} %get-tuple-element.2), channel_id=1, source_target_pairs={{0,1},{1,0},{2,3},{3,2},{4,5},{5,4},{6,7},{7,6},{8,9},{9,8},{10,11... | collective-permute-start | bytes 86024 | tf_op jit(solution)/shard_map/ppermute | solution.py:34
  10.6 9.1 %copy-start = (s32[8]{0:T(128)S(1)}, s32[8]{0:T(128)}, u32[]{:S(2)}) copy-start(s32[8]{0:T(128)} %param.5) | copy-start | bytes 100
  10.6 5.8 %collective-permute-start.8 = (f32[4,7,8,128]{3,2,1,0:T(8,128)S(1)}, f32[4,7,8,128]{3,2,1,0:T(8,128)S(1)}, u32[]{:S(2)}, u32[]{:S(2)}) collective-permute-start(f32[4,7,8,128]{3,2,1,0:T(8,128)S(1)} %bitcast_dynamic-update-slice_fusion.refs_0_), channel_id=1, source_target_pairs={{0,24},{4,28},{8,16},{12,20},{16,8},{20,12},{24,0},{28,4},{1,25},{... | collective-permute-start | bytes 344072 | tf_op jit(solution)/shard_map/ppermute | solution.py:38
  13.1 4.8 %collective-permute-start.6 = (f32[4,7,8,128]{3,2,1,0:T(8,128)S(1)}, f32[4,7,8,128]{3,2,1,0:T(8,128)S(1)}, u32[]{:S(2)}, u32[]{:S(2)}) collective-permute-start(f32[4,7,8,128]{3,2,1,0:T(8,128)S(1)} %bitcast_dynamic-update-slice_fusion.refs_0_), channel_id=1, source_target_pairs={{0,8},{4,12},{8,0},{12,4},{16,24},{20,28},{24,16},{28,20},{1,9},{5... | collective-permute-start | bytes 344072 | tf_op jit(solution)/shard_map/ppermute | solution.py:38
  13.6 4.8 %collective-permute-start.4 = (f32[4,7,8,128]{3,2,1,0:T(8,128)S(1)}, f32[4,7,8,128]{3,2,1,0:T(8,128)S(1)}, u32[]{:S(2)}, u32[]{:S(2)}) collective-permute-start(f32[4,7,8,128]{3,2,1,0:T(8,128)S(1)} %bitcast_dynamic-update-slice_fusion.refs_0_), channel_id=1, source_target_pairs={{0,16},{4,20},{8,24},{12,28},{16,0},{20,4},{24,8},{28,12},{1,17},{... | collective-permute-start | bytes 344072 | tf_op jit(solution)/shard_map/ppermute | solution.py:38
  14.1 4.3 %collective-permute-start.3 = (f32[4,7,8,128]{3,2,1,0:T(8,128)S(1)}, f32[4,7,8,128]{3,2,1,0:T(8,128)S(1)}, u32[]{:S(2)}, u32[]{:S(2)}) collective-permute-start(f32[4,7,8,128]{3,2,1,0:T(8,128)S(1)} %bitcast_dynamic-update-slice_fusion.refs_0_), channel_id=1, source_target_pairs={{0,4},{4,0},{8,12},{12,8},{16,20},{20,16},{24,28},{28,24},{1,5},{5... | collective-permute-start | bytes 344072 | tf_op jit(solution)/shard_map/ppermute | solution.py:38
  16.4 2.0 %collective-permute-start.9 = (f32[4,7,8,128]{3,2,1,0:T(8,128)S(1)}, f32[4,7,8,128]{3,2,1,0:T(8,128)S(1)}, u32[]{:S(2)}, u32[]{:S(2)}) collective-permute-start(f32[4,7,8,128]{3,2,1,0:T(8,128)S(1)} %collective-permute-done.8.refs_6_), channel_id=1, source_target_pairs={{0,4},{4,0},{8,12},{12,8},{16,20},{20,16},{24,28},{28,24},{1,5},{5... | collective-permute-start | bytes 344072 | tf_op jit(solution)/shard_map/ppermute | solution.py:38
  17.9 1.3 %collective-permute-start.7 = (f32[4,7,8,128]{3,2,1,0:T(8,128)S(1)}, f32[4,7,8,128]{3,2,1,0:T(8,128)S(1)}, u32[]{:S(2)}, u32[]{:S(2)}) collective-permute-start(f32[4,7,8,128]{3,2,1,0:T(8,128)S(1)} %collective-permute-done.6.refs_4_), channel_id=1, source_target_pairs={{0,4},{4,0},{8,12},{12,8},{16,20},{20,16},{24,28},{28,24},{1,5},{5... | collective-permute-start | bytes 344072 | tf_op jit(solution)/shard_map/ppermute | solution.py:38
  18.4 1.3 %collective-permute-start.5 = (f32[4,7,8,128]{3,2,1,0:T(8,128)S(1)}, f32[4,7,8,128]{3,2,1,0:T(8,128)S(1)}, u32[]{:S(2)}, u32[]{:S(2)}) collective-permute-start(f32[4,7,8,128]{3,2,1,0:T(8,128)S(1)} %collective-permute-done.4.refs_2_), channel_id=1, source_target_pairs={{0,4},{4,0},{8,12},{12,8},{16,20},{20,16},{24,28},{28,24},{1,5},{5... | collective-permute-start | bytes 344072 | tf_op jit(solution)/shard_map/ppermute | solution.py:38

commit v5 on v4

--- a/solution.py
+++ b/solution.py
@@ -12,30 +12,55 @@
 PARTS = 7
 
 
-def bit_reverse(value, count):
-    out = 0
-    for _ in range(count.bit_length() - 1):
-        out = 2 * out + value % 2
-        value = value // 2
-    return out
-
-
-def shift_order(count):
-    return sorted(range(1, count), key=lambda shift: (min(shift, count - shift), shift))
+def split_index(value, size):
+    if size & (size - 1) == 0:
+        return value >> (size.bit_length() - 1), value & (size - 1)
+    return lax.div(value, jnp.int32(size)), lax.rem(value, jnp.int32(size))
 
 
 def mask_order(count):
     return sorted(range(1, count), key=lambda mask: (-bin(mask).count("1"), mask))
 
 
-def shift_cols(values, shift):
-    count = lax.axis_size("col")
-    pairs = [(at, bit_reverse((bit_reverse(at, count) + shift) % count, count)) for at in range(count)]
-    return lax.ppermute(values, "col", pairs)
+def swap_rows(values, mask):
+    return lax.ppermute(values, "row", [(at, at ^ mask) for at in range(lax.axis_size("row"))])
 
 
-def swap_rows(values, mask):
-    return lax.ppermute(values, "row", [(at, at ^ mask) for at in range(lax.axis_size("row"))])
+def shift_cols(values, even, odd):
+    rows, cols = lax.axis_size("row"), lax.axis_size("col")
+    pairs = []
+    for row in range(rows):
+        for col in range(cols):
+            to = (col + (odd if row % 2 else even)) % cols
+            pairs.append((row * cols + col, row * cols + to))
+    return lax.ppermute(values, ("row", "col"), pairs)
+
+
+def put(values, block, at):
+    return lax.dynamic_update_slice(values, block, (at, 0, 0, 0))
+
+
+def gather_cols(own):
+    cols = lax.axis_size("col")
+    stack = put(jnp.zeros((cols,) + own.shape, jnp.float32), own[None], 0)
+    pair = put(jnp.zeros((2,) + own.shape, jnp.float32), own[None], 0)
+    pair = put(pair, swap_rows(own, 1)[None], 1)
+    if cols > 1:
+        stack = put(stack, shift_cols(own, 1, 1)[None], 1)
+    for shift in range(2, cols, 2):
+        stack = put(stack, shift_cols(pair, shift, shift + 1), shift)
+    return stack
+
+
+def locate(star, rows, row_count, col_count):
+    block, inside = split_index(star, rows * LANES)
+    line, lane = split_index(inside, LANES)
+    col, row = split_index(block, row_count)
+    back = split_index(lax.axis_index("col") - col + col_count, col_count)[1]
+    far = back >= 2
+    holder = jnp.where(far, (row & -2) | (back & 1), row)
+    slot = jnp.where(far, (back & -2) + jnp.where(holder == row, 0, 1), back)
+    return holder ^ lax.axis_index("row"), slot, line, lane
 
 
 def add_pairs(source, targets, sums):
@@ -59,8 +84,6 @@
     stacks, (accels_ref, jerks_ref) = refs[: len(masks)], refs[len(masks) :]
     rows = stacks[0].shape[2]
     count = active_ref.shape[1]
-    row_at = lax.axis_index("row")
-    col_at = bit_reverse(lax.axis_index("col"), col_count)
     lane = lax.broadcasted_iota(jnp.int32, (count, LANES), 1)
     place = lax.broadcasted_iota(jnp.int32, (count, LANES), 0)
     zeros = jnp.zeros((count, LANES), jnp.float32)
@@ -72,13 +95,9 @@
 
     picked = [[zeros, zeros] for _ in range(6)]
     for target in range(count):
-        star = active_ref[0, target]
-        block = star // (rows * LANES)
-        slot = (col_at - bit_reverse(block // row_count, col_count) + col_count) % col_count
-        mask = (block % row_count) ^ row_at
-        row = (star // LANES) % rows
+        mask, slot, row, spot = locate(active_ref[0, target], rows, row_count, col_count)
         for at, stack in enumerate(stacks):
-            hit = (lane == jnp.where(mask == masks[at], star % LANES, -1)) & (place == target)
+            hit = (lane == jnp.where(mask == masks[at], spot, -1)) & (place == target)
             line = lines(stack, slot, row)
             for part in range(6):
                 picked[part][at % 2] = jnp.where(hit, line[part], picked[part][at % 2])
@@ -121,9 +140,7 @@
     col_count = lax.axis_size("col")
     rows = phase.shape[1] // LANES
     own = jnp.concatenate([phase.reshape(6, rows, LANES), mass.reshape(1, rows, LANES)], axis=0)
-    stack = lax.dynamic_update_slice(jnp.zeros((col_count,) + own.shape, jnp.float32), own[None], (0, 0, 0, 0))
-    for shift in shift_order(col_count):
-        stack = lax.dynamic_update_slice(stack, shift_cols(own, shift)[None], (shift, 0, 0, 0))
+    stack = gather_cols(own)
     stacks, masks = [], []
     for mask in [0] + [2 * mask for mask in reversed(mask_order(row_count // 2))]:
         held = stack if mask == 0 else swap_rows(stack, mask)

time: 22.8 us -> 21.9 us (0.961)
  waiting for transfers between devices: 9.1 us -> 7.97 us
  starting transfers between devices: 9.17 us -> 9.63 us
    ppermute x3 -> x2, waiting for transfers between devices: 3.48 us -> 2.48 us  [shift_cols(): return lax.ppermute(values, ('row', 'col'), pairs)]
    ppermute x7 -> x8, starting transfers between devices: 3.5 us -> 4.36 us  [swap_rows(): lax.ppermute(values, 'row', [(at, at ^ mask) for at in range(lax.axis_siz...]
    ppermute x3 -> x2, starting transfers between devices: 5.67 us -> 5.28 us  [shift_cols(): return lax.ppermute(values, ('row', 'col'), pairs)]
    ppermute x7 -> x8, waiting for transfers between devices: 5.62 us -> 5.49 us  [swap_rows(): lax.ppermute(values, 'row', [(at, at ^ mask) for at in range(lax.axis_siz...]
  transfers between devices with their start and end apart: 10 -> 10, of which waited for: 8 -> 7; matrix products, arithmetic and copies ran while one was open for 0% -> 0% of each run, Pallas kernels for 0% -> 0%
where the time goes in v5:
time: 21.9 us; the launch traced here: 21.7 us
  starting transfers between devices  9.63 us (44%)
  waiting for transfers between devices  7.97 us (36%)
  Pallas kernels  2.66 us (12%)
  local copies, waits for them, and re-layouts  0.79 us (4%)
  between operations  0.67 us (3%)
    ppermute x8, waiting for transfers between devices, swap_rows(): lax.ppermute(values, 'row', [(at, at ^ mask) for at in range(lax.axis_siz...  5.49 us
    ppermute x2, starting transfers between devices, shift_cols(): return lax.ppermute(values, ('row', 'col'), pairs)  5.28 us
    ppermute x8, starting transfers between devices, swap_rows(): lax.ppermute(values, 'row', [(at, at ^ mask) for at in range(lax.axis_siz...  4.36 us
    pallas_call x1, Pallas kernels, sweep(): pl.pallas_call(functools.partial(sweep_kernel, row_count, col_count, mask...  2.66 us
    ppermute x2, waiting for transfers between devices, shift_cols(): return lax.ppermute(values, ('row', 'col'), pairs)  2.48 us
    unnamed x5, local copies, waits for them, and re-layouts  0.78 us
  transfers between devices with their start and end apart: 10, of which 7 were waited for; matrix products, arithmetic and copies ran while one was open for 0% of the time, Pallas kernels for 0%

profile of v5, /device:TPU:0, one launch (start us, length us, event | category | flops | bytes accessed | tf_op | source)
XLA Modules:
  0.0 21.7 jit_solution(3764849892827976760)
XLA Ops:
  0.6 0.0 copy-start.1
  0.6 0.8 %copy.7 = f32[1,6,8,128]{3,2,1,0:T(8,128)S(1)} copy(f32[1,6,8,128]{3,1,2,0:T(8,128)} %bitcast.13) | data formatting | bytes 49152
  1.4 0.0 copy-done.1
  1.4 0.5 %collective-permute-start.1 = (f32[7,8,128]{2,1,0:T(8,128)S(1)}, f32[7,8,128]{2,1,0:T(8,128)S(1)}, u32[]{:S(2)}, u32[]{:S(2)}) collective-permute-start(f32[7,8,128]{2,1,0:T(8,128)S(1)} %get-tuple-element.2), channel_id=1, source_target_pairs={{0,4},{4,0},{8,12},{12,8},{16,20},{20,16},{24,28},{28,24},{1,5},{5... | collective-permute-start | bytes 86024 | tf_op jit(solution)/shard_map/ppermute | solution.py:26
  1.9 2.6 %collective-permute-start = (f32[7,8,128]{2,1,0:T(8,128)S(1)}, f32[7,8,128]{2,1,0:T(8,128)S(1)}, u32[]{:S(2)}, u32[]{:S(2)}) collective-permute-start(f32[7,8,128]{2,1,0:T(8,128)S(1)} %get-tuple-element.2), channel_id=1, source_target_pairs={{0,1},{1,2},{2,3},{3,0},{4,5},{5,6},{6,7},{7,4},{8,9},{9,10},{10,1... | collective-permute-start | bytes 86024 | tf_op jit(solution)/shard_map/ppermute | solution.py:36
  4.6 0.0 collective-permute-done.1
  4.6 2.6 %collective-permute-start.2 = (f32[2,7,8,128]{3,2,1,0:T(8,128)S(1)}, f32[2,7,8,128]{3,2,1,0:T(8,128)S(1)}, u32[]{:S(2)}, u32[]{:S(2)}) collective-permute-start(f32[2,7,8,128]{3,2,1,0:T(8,128)S(1)} %pad_maximum_fusion), channel_id=1, source_target_pairs={{0,2},{1,3},{2,0},{3,1},{4,7},{5,4},{6,5},{7,6},{8,10},{9,11},{10,... | collective-permute-start | bytes 172040 | tf_op jit(solution)/shard_map/ppermute | solution.py:36
  7.3 1.4 %collective-permute-done = f32[7,8,128]{2,1,0:T(8,128)S(1)} collective-permute-done((f32[7,8,128]{2,1,0:T(8,128)S(1)}, f32[7,8,128]{2,1,0:T(8,128)S(1)}, u32[]{:S(2)}, u32[]{:S(2)}) %collective-permute-start) | collective-permute-done | bytes 28704 | tf_op jit(solution)/shard_map/ppermute | solution.py:36
  8.6 1.1 %collective-permute-done.2 = f32[2,7,8,128]{3,2,1,0:T(8,128)S(1)} collective-permute-done((f32[2,7,8,128]{3,2,1,0:T(8,128)S(1)}, f32[2,7,8,128]{3,2,1,0:T(8,128)S(1)}, u32[]{:S(2)}, u32[]{:S(2)}) %collective-permute-start.2) | collective-permute-done | bytes 57376 | tf_op jit(solution)/shard_map/ppermute | solution.py:36
  9.8 2.7 %collective-permute-start.8 = (f32[4,7,8,128]{3,2,1,0:T(8,128)S(1)}, f32[4,7,8,128]{3,2,1,0:T(8,128)S(1)}, u32[]{:S(2)}, u32[]{:S(2)}) collective-permute-start(f32[4,7,8,128]{3,2,1,0:T(8,128)S(1)} %constant_dynamic-update-slice_fusion.refs_0_), channel_id=1, source_target_pairs={{0,24},{4,28},{8,16},{12,20},{16,8},{20,12},{24,0},{28,4},{1,25},{... | collective-permute-start | bytes 344072 | tf_op jit(solution)/shard_map/ppermute | solution.py:26
  12.4 0.5 %collective-permute-start.6 = (f32[4,7,8,128]{3,2,1,0:T(8,128)S(1)}, f32[4,7,8,128]{3,2,1,0:T(8,128)S(1)}, u32[]{:S(2)}, u32[]{:S(2)}) collective-permute-start(f32[4,7,8,128]{3,2,1,0:T(8,128)S(1)} %constant_dynamic-update-slice_fusion.refs_0_), channel_id=1, source_target_pairs={{0,8},{4,12},{8,0},{12,4},{16,24},{20,28},{24,16},{28,20},{1,9},{5... | collective-permute-start | bytes 344072 | tf_op jit(solution)/shard_map/ppermute | solution.py:26
  13.0 0.3 %collective-permute-start.4 = (f32[4,7,8,128]{3,2,1,0:T(8,128)S(1)}, f32[4,7,8,128]{3,2,1,0:T(8,128)S(1)}, u32[]{:S(2)}, u32[]{:S(2)}) collective-permute-start(f32[4,7,8,128]{3,2,1,0:T(8,128)S(1)} %constant_dynamic-update-slice_fusion.refs_0_), channel_id=1, source_target_pairs={{0,16},{4,20},{8,24},{12,28},{16,0},{20,4},{24,8},{28,12},{1,17},{... | collective-permute-start | bytes 344072 | tf_op jit(solution)/shard_map/ppermute | solution.py:26
  13.3 0.0 collective-permute-start.3
  13.3 3.0 %collective-permute-done.8.refs_6_ = f32[4,7,8,128]{3,2,1,0:T(8,128)S(1)} collective-permute-done((f32[4,7,8,128]{3,2,1,0:T(8,128)S(1)}, f32[4,7,8,128]{3,2,1,0:T(8,128)S(1)}, u32[]{:S(2)}, u32[]{:S(2)}) %collective-permute-start.8) | collective-permute-done | bytes 114720 | tf_op jit(solution)/shard_map/ppermute | solution.py:26
  16.3 0.0 collective-permute-start.9
  16.3 1.2 %collective-permute-done.6.refs_4_ = f32[4,7,8,128]{3,2,1,0:T(8,128)S(1)} collective-permute-done((f32[4,7,8,128]{3,2,1,0:T(8,128)S(1)}, f32[4,7,8,128]{3,2,1,0:T(8,128)S(1)}, u32[]{:S(2)}, u32[]{:S(2)}) %collective-permute-start.6) | collective-permute-done | bytes 114720 | tf_op jit(solution)/shard_map/ppermute | solution.py:26
  17.5 0.0 collective-permute-start.7
  17.5 0.2 %collective-permute-done.4.refs_2_ = f32[4,7,8,128]{3,2,1,0:T(8,128)S(1)} collective-permute-done((f32[4,7,8,128]{3,2,1,0:T(8,128)S(1)}, f32[4,7,8,128]{3,2,1,0:T(8,128)S(1)}, u32[]{:S(2)}, u32[]{:S(2)}) %collective-permute-start.4) | collective-permute-done | bytes 114720 | tf_op jit(solution)/shard_map/ppermute | solution.py:26
  17.8 0.3 %collective-permute-start.5 = (f32[4,7,8,128]{3,2,1,0:T(8,128)S(1)}, f32[4,7,8,128]{3,2,1,0:T(8,128)S(1)}, u32[]{:S(2)}, u32[]{:S(2)}) collective-permute-start(f32[4,7,8,128]{3,2,1,0:T(8,128)S(1)} %collective-permute-done.4.refs_2_), channel_id=1, source_target_pairs={{0,4},{4,0},{8,12},{12,8},{16,20},{20,16},{24,28},{28,24},{1,5},{5... | collective-permute-start | bytes 344072 | tf_op jit(solution)/shard_map/ppermute | solution.py:26
  18.0 0.0 collective-permute-done.3.refs_1_
  18.0 0.0 collective-permute-done.9.refs_7_
  18.0 0.8 %collective-permute-done.7.refs_5_ = f32[4,7,8,128]{3,2,1,0:T(8,128)S(1)} collective-permute-done((f32[4,7,8,128]{3,2,1,0:T(8,128)S(1)}, f32[4,7,8,128]{3,2,1,0:T(8,128)S(1)}, u32[]{:S(2)}, u32[]{:S(2)}) %collective-permute-start.7) | collective-permute-done | bytes 114720 | tf_op jit(solution)/shard_map/ppermute | solution.py:26
  18.8 0.2 %collective-permute-done.5.refs_3_ = f32[4,7,8,128]{3,2,1,0:T(8,128)S(1)} collective-permute-done((f32[4,7,8,128]{3,2,1,0:T(8,128)S(1)}, f32[4,7,8,128]{3,2,1,0:T(8,128)S(1)}, u32[]{:S(2)}, u32[]{:S(2)}) %collective-permute-start.5) | collective-permute-done | bytes 114720 | tf_op jit(solution)/shard_map/ppermute | solution.py:26
  19.1 2.7 %shard_map.50 = (f32[3,8]{1,0:T(4,128)}, f32[3,8]{1,0:T(4,128)}) custom-call(s32[1,8]{1,0:T(1,128)S(1)} %bitcast.11, f32[4,7,8,128]{3,2,1,0:T(8,128)S(1)} %constant_dynamic-update-slice_fusion.refs_0_, f32[4,7,8,128]{3,2,1,0:T(8,128)S(1)} %collective-permute-done.3.refs_1_, f32[4,7,8,128]{3,2,1,0:T(8,128)S(1)} %collective-permute-done.4.refs_2_, ...), custom_call_target="tpu_custom_call" | custom-call | tf_op jit(solution)/shard_map/pallas_call | solution.py:129
  (7 shorter events, 0.0 us)
Async XLA Ops:
  0.6 0.8 %copy-start.1 = (f32[1024]{0:T(1024)S(1)}, f32[1024]{0:T(1024)}, u32[]{:S(2)}) copy-start(f32[1024]{0:T(1024)} %param.4) | copy-start | bytes 12292
  1.4 3.2 %collective-permute-start.1 = (f32[7,8,128]{2,1,0:T(8,128)S(1)}, f32[7,8,128]{2,1,0:T(8,128)S(1)}, u32[]{:S(2)}, u32[]{:S(2)}) collective-permute-start(f32[7,8,128]{2,1,0:T(8,128)S(1)} %get-tuple-element.2), channel_id=1, source_target_pairs={{0,4},{4,0},{8,12},{12,8},{16,20},{20,16},{24,28},{28,24},{1,5},{5... | collective-permute-start | bytes 86024 | tf_op jit(solution)/shard_map/ppermute | solution.py:26
  1.9 6.7 %collective-permute-start = (f32[7,8,128]{2,1,0:T(8,128)S(1)}, f32[7,8,128]{2,1,0:T(8,128)S(1)}, u32[]{:S(2)}, u32[]{:S(2)}) collective-permute-start(f32[7,8,128]{2,1,0:T(8,128)S(1)} %get-tuple-element.2), channel_id=1, source_target_pairs={{0,1},{1,2},{2,3},{3,0},{4,5},{5,6},{6,7},{7,4},{8,9},{9,10},{10,1... | collective-permute-start | bytes 86024 | tf_op jit(solution)/shard_map/ppermute | solution.py:36
  4.6 5.1 %collective-permute-start.2 = (f32[2,7,8,128]{3,2,1,0:T(8,128)S(1)}, f32[2,7,8,128]{3,2,1,0:T(8,128)S(1)}, u32[]{:S(2)}, u32[]{:S(2)}) collective-permute-start(f32[2,7,8,128]{3,2,1,0:T(8,128)S(1)} %pad_maximum_fusion), channel_id=1, source_target_pairs={{0,2},{1,3},{2,0},{3,1},{4,7},{5,4},{6,5},{7,6},{8,10},{9,11},{10,... | collective-permute-start | bytes 172040 | tf_op jit(solution)/shard_map/ppermute | solution.py:36
  9.7 9.3 %copy-start = (s32[8]{0:T(128)S(1)}, s32[8]{0:T(128)}, u32[]{:S(2)}) copy-start(s32[8]{0:T(128)} %param.5) | copy-start | bytes 100
  9.8 6.6 %collective-permute-start.8 = (f32[4,7,8,128]{3,2,1,0:T(8,128)S(1)}, f32[4,7,8,128]{3,2,1,0:T(8,128)S(1)}, u32[]{:S(2)}, u32[]{:S(2)}) collective-permute-start(f32[4,7,8,128]{3,2,1,0:T(8,128)S(1)} %constant_dynamic-update-slice_fusion.refs_0_), channel_id=1, source_target_pairs={{0,24},{4,28},{8,16},{12,20},{16,8},{20,12},{24,0},{28,4},{1,25},{... | collective-permute-start | bytes 344072 | tf_op jit(solution)/shard_map/ppermute | solution.py:26
  12.4 5.1 %collective-permute-start.6 = (f32[4,7,8,128]{3,2,1,0:T(8,128)S(1)}, f32[4,7,8,128]{3,2,1,0:T(8,128)S(1)}, u32[]{:S(2)}, u32[]{:S(2)}) collective-permute-start(f32[4,7,8,128]{3,2,1,0:T(8,128)S(1)} %constant_dynamic-update-slice_fusion.refs_0_), channel_id=1, source_target_pairs={{0,8},{4,12},{8,0},{12,4},{16,24},{20,28},{24,16},{28,20},{1,9},{5... | collective-permute-start | bytes 344072 | tf_op jit(solution)/shard_map/ppermute | solution.py:26
  13.0 4.8 %collective-permute-start.4 = (f32[4,7,8,128]{3,2,1,0:T(8,128)S(1)}, f32[4,7,8,128]{3,2,1,0:T(8,128)S(1)}, u32[]{:S(2)}, u32[]{:S(2)}) collective-permute-start(f32[4,7,8,128]{3,2,1,0:T(8,128)S(1)} %constant_dynamic-update-slice_fusion.refs_0_), channel_id=1, source_target_pairs={{0,16},{4,20},{8,24},{12,28},{16,0},{20,4},{24,8},{28,12},{1,17},{... | collective-permute-start | bytes 344072 | tf_op jit(solution)/shard_map/ppermute | solution.py:26
  13.3 4.7 %collective-permute-start.3 = (f32[4,7,8,128]{3,2,1,0:T(8,128)S(1)}, f32[4,7,8,128]{3,2,1,0:T(8,128)S(1)}, u32[]{:S(2)}, u32[]{:S(2)}) collective-permute-start(f32[4,7,8,128]{3,2,1,0:T(8,128)S(1)} %constant_dynamic-update-slice_fusion.refs_0_), channel_id=1, source_target_pairs={{0,4},{4,0},{8,12},{12,8},{16,20},{20,16},{24,28},{28,24},{1,5},{5... | collective-permute-start | bytes 344072 | tf_op jit(solution)/shard_map/ppermute | solution.py:26
  16.3 1.7 %collective-permute-start.9 = (f32[4,7,8,128]{3,2,1,0:T(8,128)S(1)}, f32[4,7,8,128]{3,2,1,0:T(8,128)S(1)}, u32[]{:S(2)}, u32[]{:S(2)}) collective-permute-start(f32[4,7,8,128]{3,2,1,0:T(8,128)S(1)} %collective-permute-done.8.refs_6_), channel_id=1, source_target_pairs={{0,4},{4,0},{8,12},{12,8},{16,20},{20,16},{24,28},{28,24},{1,5},{5... | collective-permute-start | bytes 344072 | tf_op jit(solution)/shard_map/ppermute | solution.py:26
  17.5 1.3 %collective-permute-start.7 = (f32[4,7,8,128]{3,2,1,0:T(8,128)S(1)}, f32[4,7,8,128]{3,2,1,0:T(8,128)S(1)}, u32[]{:S(2)}, u32[]{:S(2)}) collective-permute-start(f32[4,7,8,128]{3,2,1,0:T(8,128)S(1)} %collective-permute-done.6.refs_4_), channel_id=1, source_target_pairs={{0,4},{4,0},{8,12},{12,8},{16,20},{20,16},{24,28},{28,24},{1,5},{5... | collective-permute-start | bytes 344072 | tf_op jit(solution)/shard_map/ppermute | solution.py:26
  17.8 1.3 %collective-permute-start.5 = (f32[4,7,8,128]{3,2,1,0:T(8,128)S(1)}, f32[4,7,8,128]{3,2,1,0:T(8,128)S(1)}, u32[]{:S(2)}, u32[]{:S(2)}) collective-permute-start(f32[4,7,8,128]{3,2,1,0:T(8,128)S(1)} %collective-permute-done.4.refs_2_), channel_id=1, source_target_pairs={{0,4},{4,0},{8,12},{12,8},{16,20},{20,16},{24,28},{28,24},{1,5},{5... | collective-permute-start | bytes 344072 | tf_op jit(solution)/shard_map/ppermute | solution.py:26

commit v6 on v5

--- a/solution.py
+++ b/solution.py
@@ -1,4 +1,5 @@
 import functools
+import math
 
 import jax
 import jax.numpy as jnp
@@ -71,12 +72,13 @@
     inverse = lax.rsqrt(dist_sq)
     inverse_sq = inverse * inverse
     weight = source[6] * inverse * inverse_sq
-    pull = weight * (along * inverse_sq)
+    along = along * inverse_sq
     sums = list(sums)
     for k in range(3):
-        sums[k] = sums[k] + weight * offset[k]
+        pull = weight * offset[k]
+        sums[k] = sums[k] + pull
         sums[k + 3] = sums[k + 3] + weight * vel_diff[k]
-        sums[k + 6] = sums[k + 6] + pull * offset[k]
+        sums[k + 6] = sums[k + 6] + along * pull
     return tuple(sums)
 
 
@@ -93,27 +95,26 @@
             jnp.broadcast_to(stack[slot, part, pl.ds(row, 1), :], (count, LANES)) for part in range(PARTS)
         ]
 
-    picked = [[zeros, zeros] for _ in range(6)]
+    picked = [zeros] * 6
     for target in range(count):
         mask, slot, row, spot = locate(active_ref[0, target], rows, row_count, col_count)
         for at, stack in enumerate(stacks):
             hit = (lane == jnp.where(mask == masks[at], spot, -1)) & (place == target)
             line = lines(stack, slot, row)
-            for part in range(6):
-                picked[part][at % 2] = jnp.where(hit, line[part], picked[part][at % 2])
-    targets = [
-        jnp.broadcast_to(jnp.sum(one + other, axis=1, keepdims=True), (count, LANES)) for one, other in picked
-    ]
+            picked = [jnp.where(hit, line[part], picked[part]) for part in range(6)]
+    targets = [jnp.broadcast_to(jnp.sum(value, axis=1, keepdims=True), (count, LANES)) for value in picked]
 
     sums = (zeros,) * 9
+    unroll = math.gcd(col_count, 2)
     for stack in stacks:
 
-        def add_slot(slot, sums, stack=stack):
-            for row in range(rows):
-                sums = add_pairs(lines(stack, slot, row), targets, sums)
+        def add_slots(step, sums, stack=stack):
+            for at in range(unroll):
+                for row in range(rows):
+                    sums = add_pairs(lines(stack, step * unroll + at, row), targets, sums)
             return sums
 
-        sums = lax.fori_loop(0, col_count, add_slot, sums)
+        sums = lax.fori_loop(0, col_count // unroll, add_slots, sums)
     norming = 1.0 / (row_count * col_count * rows * LANES)
     out = zeros
     for k in range(6):

time: 21.9 us -> 21.8 us (level)
  no operation moved by 1% of the time
where the time goes in v6:
time: 21.8 us; the launch traced here: 21.6 us
  starting transfers between devices  9.63 us (44%)
  waiting for transfers between devices  7.97 us (37%)
  Pallas kernels  2.48 us (11%)
  local copies, waits for them, and re-layouts  0.79 us (4%)
  between operations  0.67 us (3%)
    ppermute x8, waiting for transfers between devices, swap_rows(): lax.ppermute(values, 'row', [(at, at ^ mask) for at in range(lax.axis_siz...  5.49 us
    ppermute x2, starting transfers between devices, shift_cols(): return lax.ppermute(values, ('row', 'col'), pairs)  5.28 us
    ppermute x8, starting transfers between devices, swap_rows(): lax.ppermute(values, 'row', [(at, at ^ mask) for at in range(lax.axis_siz...  4.36 us
    pallas_call x1, Pallas kernels, sweep(): pl.pallas_call(functools.partial(sweep_kernel, row_count, col_count, mask...  2.48 us
    ppermute x2, waiting for transfers between devices, shift_cols(): return lax.ppermute(values, ('row', 'col'), pairs)  2.48 us
    unnamed x5, local copies, waits for them, and re-layouts  0.78 us
  transfers between devices with their start and end apart: 10, of which 7 were waited for; matrix products, arithmetic and copies ran while one was open for 0% of the time, Pallas kernels for 0%

profile of v6, /device:TPU:0, one launch (start us, length us, event | category | flops | bytes accessed | tf_op | source)
XLA Modules:
  0.0 21.6 jit_solution(2877660165408031973)
XLA Ops:
  0.6 0.0 copy-start.1
  0.6 0.8 %copy.7 = f32[1,6,8,128]{3,2,1,0:T(8,128)S(1)} copy(f32[1,6,8,128]{3,1,2,0:T(8,128)} %bitcast.13) | data formatting | bytes 49152
  1.4 0.0 copy-done.1
  1.4 0.5 %collective-permute-start.1 = (f32[7,8,128]{2,1,0:T(8,128)S(1)}, f32[7,8,128]{2,1,0:T(8,128)S(1)}, u32[]{:S(2)}, u32[]{:S(2)}) collective-permute-start(f32[7,8,128]{2,1,0:T(8,128)S(1)} %get-tuple-element.2), channel_id=1, source_target_pairs={{0,4},{4,0},{8,12},{12,8},{16,20},{20,16},{24,28},{28,24},{1,5},{5... | collective-permute-start | bytes 86024 | tf_op jit(solution)/shard_map/ppermute | solution.py:27
  1.9 2.6 %collective-permute-start = (f32[7,8,128]{2,1,0:T(8,128)S(1)}, f32[7,8,128]{2,1,0:T(8,128)S(1)}, u32[]{:S(2)}, u32[]{:S(2)}) collective-permute-start(f32[7,8,128]{2,1,0:T(8,128)S(1)} %get-tuple-element.2), channel_id=1, source_target_pairs={{0,1},{1,2},{2,3},{3,0},{4,5},{5,6},{6,7},{7,4},{8,9},{9,10},{10,1... | collective-permute-start | bytes 86024 | tf_op jit(solution)/shard_map/ppermute | solution.py:37
  4.6 0.0 collective-permute-done.1
  4.6 2.6 %collective-permute-start.2 = (f32[2,7,8,128]{3,2,1,0:T(8,128)S(1)}, f32[2,7,8,128]{3,2,1,0:T(8,128)S(1)}, u32[]{:S(2)}, u32[]{:S(2)}) collective-permute-start(f32[2,7,8,128]{3,2,1,0:T(8,128)S(1)} %pad_maximum_fusion), channel_id=1, source_target_pairs={{0,2},{1,3},{2,0},{3,1},{4,7},{5,4},{6,5},{7,6},{8,10},{9,11},{10,... | collective-permute-start | bytes 172040 | tf_op jit(solution)/shard_map/ppermute | solution.py:37
  7.3 1.4 %collective-permute-done = f32[7,8,128]{2,1,0:T(8,128)S(1)} collective-permute-done((f32[7,8,128]{2,1,0:T(8,128)S(1)}, f32[7,8,128]{2,1,0:T(8,128)S(1)}, u32[]{:S(2)}, u32[]{:S(2)}) %collective-permute-start) | collective-permute-done | bytes 28704 | tf_op jit(solution)/shard_map/ppermute | solution.py:37
  8.6 1.1 %collective-permute-done.2 = f32[2,7,8,128]{3,2,1,0:T(8,128)S(1)} collective-permute-done((f32[2,7,8,128]{3,2,1,0:T(8,128)S(1)}, f32[2,7,8,128]{3,2,1,0:T(8,128)S(1)}, u32[]{:S(2)}, u32[]{:S(2)}) %collective-permute-start.2) | collective-permute-done | bytes 57376 | tf_op jit(solution)/shard_map/ppermute | solution.py:37
  9.8 2.7 %collective-permute-start.8 = (f32[4,7,8,128]{3,2,1,0:T(8,128)S(1)}, f32[4,7,8,128]{3,2,1,0:T(8,128)S(1)}, u32[]{:S(2)}, u32[]{:S(2)}) collective-permute-start(f32[4,7,8,128]{3,2,1,0:T(8,128)S(1)} %constant_dynamic-update-slice_fusion.refs_0_), channel_id=1, source_target_pairs={{0,24},{4,28},{8,16},{12,20},{16,8},{20,12},{24,0},{28,4},{1,25},{... | collective-permute-start | bytes 344072 | tf_op jit(solution)/shard_map/ppermute | solution.py:27
  12.4 0.5 %collective-permute-start.6 = (f32[4,7,8,128]{3,2,1,0:T(8,128)S(1)}, f32[4,7,8,128]{3,2,1,0:T(8,128)S(1)}, u32[]{:S(2)}, u32[]{:S(2)}) collective-permute-start(f32[4,7,8,128]{3,2,1,0:T(8,128)S(1)} %constant_dynamic-update-slice_fusion.refs_0_), channel_id=1, source_target_pairs={{0,8},{4,12},{8,0},{12,4},{16,24},{20,28},{24,16},{28,20},{1,9},{5... | collective-permute-start | bytes 344072 | tf_op jit(solution)/shard_map/ppermute | solution.py:27
  13.0 0.3 %collective-permute-start.4 = (f32[4,7,8,128]{3,2,1,0:T(8,128)S(1)}, f32[4,7,8,128]{3,2,1,0:T(8,128)S(1)}, u32[]{:S(2)}, u32[]{:S(2)}) collective-permute-start(f32[4,7,8,128]{3,2,1,0:T(8,128)S(1)} %constant_dynamic-update-slice_fusion.refs_0_), channel_id=1, source_target_pairs={{0,16},{4,20},{8,24},{12,28},{16,0},{20,4},{24,8},{28,12},{1,17},{... | collective-permute-start | bytes 344072 | tf_op jit(solution)/shard_map/ppermute | solution.py:27
  13.3 0.0 collective-permute-start.3
  13.3 3.0 %collective-permute-done.8.refs_6_ = f32[4,7,8,128]{3,2,1,0:T(8,128)S(1)} collective-permute-done((f32[4,7,8,128]{3,2,1,0:T(8,128)S(1)}, f32[4,7,8,128]{3,2,1,0:T(8,128)S(1)}, u32[]{:S(2)}, u32[]{:S(2)}) %collective-permute-start.8) | collective-permute-done | bytes 114720 | tf_op jit(solution)/shard_map/ppermute | solution.py:27
  16.3 0.0 collective-permute-start.9
  16.3 1.2 %collective-permute-done.6.refs_4_ = f32[4,7,8,128]{3,2,1,0:T(8,128)S(1)} collective-permute-done((f32[4,7,8,128]{3,2,1,0:T(8,128)S(1)}, f32[4,7,8,128]{3,2,1,0:T(8,128)S(1)}, u32[]{:S(2)}, u32[]{:S(2)}) %collective-permute-start.6) | collective-permute-done | bytes 114720 | tf_op jit(solution)/shard_map/ppermute | solution.py:27
  17.5 0.0 collective-permute-start.7
  17.5 0.2 %collective-permute-done.4.refs_2_ = f32[4,7,8,128]{3,2,1,0:T(8,128)S(1)} collective-permute-done((f32[4,7,8,128]{3,2,1,0:T(8,128)S(1)}, f32[4,7,8,128]{3,2,1,0:T(8,128)S(1)}, u32[]{:S(2)}, u32[]{:S(2)}) %collective-permute-start.4) | collective-permute-done | bytes 114720 | tf_op jit(solution)/shard_map/ppermute | solution.py:27
  17.8 0.3 %collective-permute-start.5 = (f32[4,7,8,128]{3,2,1,0:T(8,128)S(1)}, f32[4,7,8,128]{3,2,1,0:T(8,128)S(1)}, u32[]{:S(2)}, u32[]{:S(2)}) collective-permute-start(f32[4,7,8,128]{3,2,1,0:T(8,128)S(1)} %collective-permute-done.4.refs_2_), channel_id=1, source_target_pairs={{0,4},{4,0},{8,12},{12,8},{16,20},{20,16},{24,28},{28,24},{1,5},{5... | collective-permute-start | bytes 344072 | tf_op jit(solution)/shard_map/ppermute | solution.py:27
  18.0 0.0 collective-permute-done.3.refs_1_
  18.0 0.0 collective-permute-done.9.refs_7_
  18.0 0.8 %collective-permute-done.7.refs_5_ = f32[4,7,8,128]{3,2,1,0:T(8,128)S(1)} collective-permute-done((f32[4,7,8,128]{3,2,1,0:T(8,128)S(1)}, f32[4,7,8,128]{3,2,1,0:T(8,128)S(1)}, u32[]{:S(2)}, u32[]{:S(2)}) %collective-permute-start.7) | collective-permute-done | bytes 114720 | tf_op jit(solution)/shard_map/ppermute | solution.py:27
  18.8 0.2 %collective-permute-done.5.refs_3_ = f32[4,7,8,128]{3,2,1,0:T(8,128)S(1)} collective-permute-done((f32[4,7,8,128]{3,2,1,0:T(8,128)S(1)}, f32[4,7,8,128]{3,2,1,0:T(8,128)S(1)}, u32[]{:S(2)}, u32[]{:S(2)}) %collective-permute-start.5) | collective-permute-done | bytes 114720 | tf_op jit(solution)/shard_map/ppermute | solution.py:27
  19.1 2.5 %shard_map.50 = (f32[3,8]{1,0:T(4,128)}, f32[3,8]{1,0:T(4,128)}) custom-call(s32[1,8]{1,0:T(1,128)S(1)} %bitcast.11, f32[4,7,8,128]{3,2,1,0:T(8,128)S(1)} %constant_dynamic-update-slice_fusion.refs_0_, f32[4,7,8,128]{3,2,1,0:T(8,128)S(1)} %collective-permute-done.3.refs_1_, f32[4,7,8,128]{3,2,1,0:T(8,128)S(1)} %collective-permute-done.4.refs_2_, ...), custom_call_target="tpu_custom_call" | custom-call | tf_op jit(solution)/shard_map/pallas_call | solution.py:130
  (7 shorter events, 0.0 us)
Async XLA Ops:
  0.6 0.8 %copy-start.1 = (f32[1024]{0:T(1024)S(1)}, f32[1024]{0:T(1024)}, u32[]{:S(2)}) copy-start(f32[1024]{0:T(1024)} %param.4) | copy-start | bytes 12292
  1.4 3.2 %collective-permute-start.1 = (f32[7,8,128]{2,1,0:T(8,128)S(1)}, f32[7,8,128]{2,1,0:T(8,128)S(1)}, u32[]{:S(2)}, u32[]{:S(2)}) collective-permute-start(f32[7,8,128]{2,1,0:T(8,128)S(1)} %get-tuple-element.2), channel_id=1, source_target_pairs={{0,4},{4,0},{8,12},{12,8},{16,20},{20,16},{24,28},{28,24},{1,5},{5... | collective-permute-start | bytes 86024 | tf_op jit(solution)/shard_map/ppermute | solution.py:27
  1.9 6.7 %collective-permute-start = (f32[7,8,128]{2,1,0:T(8,128)S(1)}, f32[7,8,128]{2,1,0:T(8,128)S(1)}, u32[]{:S(2)}, u32[]{:S(2)}) collective-permute-start(f32[7,8,128]{2,1,0:T(8,128)S(1)} %get-tuple-element.2), channel_id=1, source_target_pairs={{0,1},{1,2},{2,3},{3,0},{4,5},{5,6},{6,7},{7,4},{8,9},{9,10},{10,1... | collective-permute-start | bytes 86024 | tf_op jit(solution)/shard_map/ppermute | solution.py:37
  4.6 5.1 %collective-permute-start.2 = (f32[2,7,8,128]{3,2,1,0:T(8,128)S(1)}, f32[2,7,8,128]{3,2,1,0:T(8,128)S(1)}, u32[]{:S(2)}, u32[]{:S(2)}) collective-permute-start(f32[2,7,8,128]{3,2,1,0:T(8,128)S(1)} %pad_maximum_fusion), channel_id=1, source_target_pairs={{0,2},{1,3},{2,0},{3,1},{4,7},{5,4},{6,5},{7,6},{8,10},{9,11},{10,... | collective-permute-start | bytes 172040 | tf_op jit(solution)/shard_map/ppermute | solution.py:37
  9.7 9.3 %copy-start = (s32[8]{0:T(128)S(1)}, s32[8]{0:T(128)}, u32[]{:S(2)}) copy-start(s32[8]{0:T(128)} %param.5) | copy-start | bytes 100
  9.8 6.6 %collective-permute-start.8 = (f32[4,7,8,128]{3,2,1,0:T(8,128)S(1)}, f32[4,7,8,128]{3,2,1,0:T(8,128)S(1)}, u32[]{:S(2)}, u32[]{:S(2)}) collective-permute-start(f32[4,7,8,128]{3,2,1,0:T(8,128)S(1)} %constant_dynamic-update-slice_fusion.refs_0_), channel_id=1, source_target_pairs={{0,24},{4,28},{8,16},{12,20},{16,8},{20,12},{24,0},{28,4},{1,25},{... | collective-permute-start | bytes 344072 | tf_op jit(solution)/shard_map/ppermute | solution.py:27
  12.4 5.1 %collective-permute-start.6 = (f32[4,7,8,128]{3,2,1,0:T(8,128)S(1)}, f32[4,7,8,128]{3,2,1,0:T(8,128)S(1)}, u32[]{:S(2)}, u32[]{:S(2)}) collective-permute-start(f32[4,7,8,128]{3,2,1,0:T(8,128)S(1)} %constant_dynamic-update-slice_fusion.refs_0_), channel_id=1, source_target_pairs={{0,8},{4,12},{8,0},{12,4},{16,24},{20,28},{24,16},{28,20},{1,9},{5... | collective-permute-start | bytes 344072 | tf_op jit(solution)/shard_map/ppermute | solution.py:27
  13.0 4.8 %collective-permute-start.4 = (f32[4,7,8,128]{3,2,1,0:T(8,128)S(1)}, f32[4,7,8,128]{3,2,1,0:T(8,128)S(1)}, u32[]{:S(2)}, u32[]{:S(2)}) collective-permute-start(f32[4,7,8,128]{3,2,1,0:T(8,128)S(1)} %constant_dynamic-update-slice_fusion.refs_0_), channel_id=1, source_target_pairs={{0,16},{4,20},{8,24},{12,28},{16,0},{20,4},{24,8},{28,12},{1,17},{... | collective-permute-start | bytes 344072 | tf_op jit(solution)/shard_map/ppermute | solution.py:27
  13.3 4.7 %collective-permute-start.3 = (f32[4,7,8,128]{3,2,1,0:T(8,128)S(1)}, f32[4,7,8,128]{3,2,1,0:T(8,128)S(1)}, u32[]{:S(2)}, u32[]{:S(2)}) collective-permute-start(f32[4,7,8,128]{3,2,1,0:T(8,128)S(1)} %constant_dynamic-update-slice_fusion.refs_0_), channel_id=1, source_target_pairs={{0,4},{4,0},{8,12},{12,8},{16,20},{20,16},{24,28},{28,24},{1,5},{5... | collective-permute-start | bytes 344072 | tf_op jit(solution)/shard_map/ppermute | solution.py:27
  16.3 1.7 %collective-permute-start.9 = (f32[4,7,8,128]{3,2,1,0:T(8,128)S(1)}, f32[4,7,8,128]{3,2,1,0:T(8,128)S(1)}, u32[]{:S(2)}, u32[]{:S(2)}) collective-permute-start(f32[4,7,8,128]{3,2,1,0:T(8,128)S(1)} %collective-permute-done.8.refs_6_), channel_id=1, source_target_pairs={{0,4},{4,0},{8,12},{12,8},{16,20},{20,16},{24,28},{28,24},{1,5},{5... | collective-permute-start | bytes 344072 | tf_op jit(solution)/shard_map/ppermute | solution.py:27
  17.5 1.3 %collective-permute-start.7 = (f32[4,7,8,128]{3,2,1,0:T(8,128)S(1)}, f32[4,7,8,128]{3,2,1,0:T(8,128)S(1)}, u32[]{:S(2)}, u32[]{:S(2)}) collective-permute-start(f32[4,7,8,128]{3,2,1,0:T(8,128)S(1)} %collective-permute-done.6.refs_4_), channel_id=1, source_target_pairs={{0,4},{4,0},{8,12},{12,8},{16,20},{20,16},{24,28},{28,24},{1,5},{5... | collective-permute-start | bytes 344072 | tf_op jit(solution)/shard_map/ppermute | solution.py:27
  17.8 1.3 %collective-permute-start.5 = (f32[4,7,8,128]{3,2,1,0:T(8,128)S(1)}, f32[4,7,8,128]{3,2,1,0:T(8,128)S(1)}, u32[]{:S(2)}, u32[]{:S(2)}) collective-permute-start(f32[4,7,8,128]{3,2,1,0:T(8,128)S(1)} %collective-permute-done.4.refs_2_), channel_id=1, source_target_pairs={{0,4},{4,0},{8,12},{12,8},{16,20},{20,16},{24,28},{28,24},{1,5},{5... | collective-permute-start | bytes 344072 | tf_op jit(solution)/shard_map/ppermute | solution.py:27

commit v7 on v6

--- a/solution.py
+++ b/solution.py
@@ -1,5 +1,4 @@
 import functools
-import math
 
 import jax
 import jax.numpy as jnp
@@ -104,25 +103,22 @@
             picked = [jnp.where(hit, line[part], picked[part]) for part in range(6)]
     targets = [jnp.broadcast_to(jnp.sum(value, axis=1, keepdims=True), (count, LANES)) for value in picked]
 
-    sums = (zeros,) * 9
-    unroll = math.gcd(col_count, 2)
-    for stack in stacks:
+    def add_slot(slot, sums):
+        for stack in stacks:
+            for row in range(rows):
+                sums = add_pairs(lines(stack, slot, row), targets, sums)
+        return sums
 
-        def add_slots(step, sums, stack=stack):
-            for at in range(unroll):
-                for row in range(rows):
-                    sums = add_pairs(lines(stack, step * unroll + at, row), targets, sums)
-            return sums
-
-        sums = lax.fori_loop(0, col_count // unroll, add_slots, sums)
+    sums = lax.fori_loop(0, col_count, add_slot, (zeros,) * 9)
     norming = 1.0 / (row_count * col_count * rows * LANES)
-    out = zeros
     for k in range(6):
         total = sums[k] if k < 3 else sums[k] - 3.0 * sums[k + 3]
-        out = jnp.where(lane == k, jnp.sum(total, axis=1, keepdims=True) * norming, out)
-    out = out.T
-    accels_ref[...] = out[0:3, :]
-    jerks_ref[...] = out[3:6, :]
+        total = jnp.sum(total, axis=1, keepdims=True) * norming
+        total = jnp.sum(jnp.where(lane == place, total, 0.0), axis=0, keepdims=True)[:, 0:count]
+        if k < 3:
+            accels_ref[k : k + 1, :] = total
+        else:
+            jerks_ref[k - 3 : k - 2, :] = total
 
 
 def sweep(active, stacks, masks, row_count, col_count):

time: 21.8 us -> 21.6 us (level)
  no operation moved by 1% of the time
where the time goes in v7:
time: 21.6 us; the launch traced here: 21.4 us
  starting transfers between devices  9.63 us (45%)
  waiting for transfers between devices  7.97 us (37%)
  Pallas kernels  2.35 us (11%)
  local copies, waits for them, and re-layouts  0.79 us (4%)
  between operations  0.67 us (3%)
    ppermute x8, waiting for transfers between devices, swap_rows(): lax.ppermute(values, 'row', [(at, at ^ mask) for at in range(lax.axis_siz...  5.49 us
    ppermute x2, starting transfers between devices, shift_cols(): return lax.ppermute(values, ('row', 'col'), pairs)  5.28 us
    ppermute x8, starting transfers between devices, swap_rows(): lax.ppermute(values, 'row', [(at, at ^ mask) for at in range(lax.axis_siz...  4.36 us
    ppermute x2, waiting for transfers between devices, shift_cols(): return lax.ppermute(values, ('row', 'col'), pairs)  2.48 us
    pallas_call x1, Pallas kernels, sweep(): pl.pallas_call(functools.partial(sweep_kernel, row_count, col_count, mask...  2.35 us
    unnamed x5, local copies, waits for them, and re-layouts  0.78 us
  transfers between devices with their start and end apart: 10, of which 7 were waited for; matrix products, arithmetic and copies ran while one was open for 0% of the time, Pallas kernels for 0%

profile of v7, /device:TPU:0, one launch (start us, length us, event | category | flops | bytes accessed | tf_op | source)
XLA Modules:
  0.0 21.4 jit_solution(484859506166084164)
XLA Ops:
  0.6 0.0 copy-start.1
  0.6 0.8 %copy.7 = f32[1,6,8,128]{3,2,1,0:T(8,128)S(1)} copy(f32[1,6,8,128]{3,1,2,0:T(8,128)} %bitcast.13) | data formatting | bytes 49152
  1.4 0.0 copy-done.1
  1.4 0.5 %collective-permute-start.1 = (f32[7,8,128]{2,1,0:T(8,128)S(1)}, f32[7,8,128]{2,1,0:T(8,128)S(1)}, u32[]{:S(2)}, u32[]{:S(2)}) collective-permute-start(f32[7,8,128]{2,1,0:T(8,128)S(1)} %get-tuple-element.2), channel_id=1, source_target_pairs={{0,4},{4,0},{8,12},{12,8},{16,20},{20,16},{24,28},{28,24},{1,5},{5... | collective-permute-start | bytes 86024 | tf_op jit(solution)/shard_map/ppermute | solution.py:26
  1.9 2.6 %collective-permute-start = (f32[7,8,128]{2,1,0:T(8,128)S(1)}, f32[7,8,128]{2,1,0:T(8,128)S(1)}, u32[]{:S(2)}, u32[]{:S(2)}) collective-permute-start(f32[7,8,128]{2,1,0:T(8,128)S(1)} %get-tuple-element.2), channel_id=1, source_target_pairs={{0,1},{1,2},{2,3},{3,0},{4,5},{5,6},{6,7},{7,4},{8,9},{9,10},{10,1... | collective-permute-start | bytes 86024 | tf_op jit(solution)/shard_map/ppermute | solution.py:36
  4.6 0.0 collective-permute-done.1
  4.6 2.6 %collective-permute-start.2 = (f32[2,7,8,128]{3,2,1,0:T(8,128)S(1)}, f32[2,7,8,128]{3,2,1,0:T(8,128)S(1)}, u32[]{:S(2)}, u32[]{:S(2)}) collective-permute-start(f32[2,7,8,128]{3,2,1,0:T(8,128)S(1)} %pad_maximum_fusion), channel_id=1, source_target_pairs={{0,2},{1,3},{2,0},{3,1},{4,7},{5,4},{6,5},{7,6},{8,10},{9,11},{10,... | collective-permute-start | bytes 172040 | tf_op jit(solution)/shard_map/ppermute | solution.py:36
  7.3 1.4 %collective-permute-done = f32[7,8,128]{2,1,0:T(8,128)S(1)} collective-permute-done((f32[7,8,128]{2,1,0:T(8,128)S(1)}, f32[7,8,128]{2,1,0:T(8,128)S(1)}, u32[]{:S(2)}, u32[]{:S(2)}) %collective-permute-start) | collective-permute-done | bytes 28704 | tf_op jit(solution)/shard_map/ppermute | solution.py:36
  8.6 1.1 %collective-permute-done.2 = f32[2,7,8,128]{3,2,1,0:T(8,128)S(1)} collective-permute-done((f32[2,7,8,128]{3,2,1,0:T(8,128)S(1)}, f32[2,7,8,128]{3,2,1,0:T(8,128)S(1)}, u32[]{:S(2)}, u32[]{:S(2)}) %collective-permute-start.2) | collective-permute-done | bytes 57376 | tf_op jit(solution)/shard_map/ppermute | solution.py:36
  9.8 2.7 %collective-permute-start.8 = (f32[4,7,8,128]{3,2,1,0:T(8,128)S(1)}, f32[4,7,8,128]{3,2,1,0:T(8,128)S(1)}, u32[]{:S(2)}, u32[]{:S(2)}) collective-permute-start(f32[4,7,8,128]{3,2,1,0:T(8,128)S(1)} %constant_dynamic-update-slice_fusion.refs_0_), channel_id=1, source_target_pairs={{0,24},{4,28},{8,16},{12,20},{16,8},{20,12},{24,0},{28,4},{1,25},{... | collective-permute-start | bytes 344072 | tf_op jit(solution)/shard_map/ppermute | solution.py:26
  12.4 0.5 %collective-permute-start.6 = (f32[4,7,8,128]{3,2,1,0:T(8,128)S(1)}, f32[4,7,8,128]{3,2,1,0:T(8,128)S(1)}, u32[]{:S(2)}, u32[]{:S(2)}) collective-permute-start(f32[4,7,8,128]{3,2,1,0:T(8,128)S(1)} %constant_dynamic-update-slice_fusion.refs_0_), channel_id=1, source_target_pairs={{0,8},{4,12},{8,0},{12,4},{16,24},{20,28},{24,16},{28,20},{1,9},{5... | collective-permute-start | bytes 344072 | tf_op jit(solution)/shard_map/ppermute | solution.py:26
  13.0 0.3 %collective-permute-start.4 = (f32[4,7,8,128]{3,2,1,0:T(8,128)S(1)}, f32[4,7,8,128]{3,2,1,0:T(8,128)S(1)}, u32[]{:S(2)}, u32[]{:S(2)}) collective-permute-start(f32[4,7,8,128]{3,2,1,0:T(8,128)S(1)} %constant_dynamic-update-slice_fusion.refs_0_), channel_id=1, source_target_pairs={{0,16},{4,20},{8,24},{12,28},{16,0},{20,4},{24,8},{28,12},{1,17},{... | collective-permute-start | bytes 344072 | tf_op jit(solution)/shard_map/ppermute | solution.py:26
  13.3 0.0 collective-permute-start.3
  13.3 3.0 %collective-permute-done.8.refs_6_ = f32[4,7,8,128]{3,2,1,0:T(8,128)S(1)} collective-permute-done((f32[4,7,8,128]{3,2,1,0:T(8,128)S(1)}, f32[4,7,8,128]{3,2,1,0:T(8,128)S(1)}, u32[]{:S(2)}, u32[]{:S(2)}) %collective-permute-start.8) | collective-permute-done | bytes 114720 | tf_op jit(solution)/shard_map/ppermute | solution.py:26
  16.3 0.0 collective-permute-start.9
  16.3 1.2 %collective-permute-done.6.refs_4_ = f32[4,7,8,128]{3,2,1,0:T(8,128)S(1)} collective-permute-done((f32[4,7,8,128]{3,2,1,0:T(8,128)S(1)}, f32[4,7,8,128]{3,2,1,0:T(8,128)S(1)}, u32[]{:S(2)}, u32[]{:S(2)}) %collective-permute-start.6) | collective-permute-done | bytes 114720 | tf_op jit(solution)/shard_map/ppermute | solution.py:26
  17.5 0.0 collective-permute-start.7
  17.5 0.2 %collective-permute-done.4.refs_2_ = f32[4,7,8,128]{3,2,1,0:T(8,128)S(1)} collective-permute-done((f32[4,7,8,128]{3,2,1,0:T(8,128)S(1)}, f32[4,7,8,128]{3,2,1,0:T(8,128)S(1)}, u32[]{:S(2)}, u32[]{:S(2)}) %collective-permute-start.4) | collective-permute-done | bytes 114720 | tf_op jit(solution)/shard_map/ppermute | solution.py:26
  17.8 0.3 %collective-permute-start.5 = (f32[4,7,8,128]{3,2,1,0:T(8,128)S(1)}, f32[4,7,8,128]{3,2,1,0:T(8,128)S(1)}, u32[]{:S(2)}, u32[]{:S(2)}) collective-permute-start(f32[4,7,8,128]{3,2,1,0:T(8,128)S(1)} %collective-permute-done.4.refs_2_), channel_id=1, source_target_pairs={{0,4},{4,0},{8,12},{12,8},{16,20},{20,16},{24,28},{28,24},{1,5},{5... | collective-permute-start | bytes 344072 | tf_op jit(solution)/shard_map/ppermute | solution.py:26
  18.0 0.0 collective-permute-done.3.refs_1_
  18.0 0.0 collective-permute-done.9.refs_7_
  18.0 0.8 %collective-permute-done.7.refs_5_ = f32[4,7,8,128]{3,2,1,0:T(8,128)S(1)} collective-permute-done((f32[4,7,8,128]{3,2,1,0:T(8,128)S(1)}, f32[4,7,8,128]{3,2,1,0:T(8,128)S(1)}, u32[]{:S(2)}, u32[]{:S(2)}) %collective-permute-start.7) | collective-permute-done | bytes 114720 | tf_op jit(solution)/shard_map/ppermute | solution.py:26
  18.8 0.2 %collective-permute-done.5.refs_3_ = f32[4,7,8,128]{3,2,1,0:T(8,128)S(1)} collective-permute-done((f32[4,7,8,128]{3,2,1,0:T(8,128)S(1)}, f32[4,7,8,128]{3,2,1,0:T(8,128)S(1)}, u32[]{:S(2)}, u32[]{:S(2)}) %collective-permute-start.5) | collective-permute-done | bytes 114720 | tf_op jit(solution)/shard_map/ppermute | solution.py:26
  19.1 2.4 %shard_map.50 = (f32[3,8]{1,0:T(4,128)}, f32[3,8]{1,0:T(4,128)}) custom-call(s32[1,8]{1,0:T(1,128)S(1)} %bitcast.11, f32[4,7,8,128]{3,2,1,0:T(8,128)S(1)} %constant_dynamic-update-slice_fusion.refs_0_, f32[4,7,8,128]{3,2,1,0:T(8,128)S(1)} %collective-permute-done.3.refs_1_, f32[4,7,8,128]{3,2,1,0:T(8,128)S(1)} %collective-permute-done.4.refs_2_, ...), custom_call_target="tpu_custom_call" | custom-call | tf_op jit(solution)/shard_map/pallas_call | solution.py:126
  (7 shorter events, 0.0 us)
Async XLA Ops:
  0.6 0.8 %copy-start.1 = (f32[1024]{0:T(1024)S(1)}, f32[1024]{0:T(1024)}, u32[]{:S(2)}) copy-start(f32[1024]{0:T(1024)} %param.4) | copy-start | bytes 12292
  1.4 3.2 %collective-permute-start.1 = (f32[7,8,128]{2,1,0:T(8,128)S(1)}, f32[7,8,128]{2,1,0:T(8,128)S(1)}, u32[]{:S(2)}, u32[]{:S(2)}) collective-permute-start(f32[7,8,128]{2,1,0:T(8,128)S(1)} %get-tuple-element.2), channel_id=1, source_target_pairs={{0,4},{4,0},{8,12},{12,8},{16,20},{20,16},{24,28},{28,24},{1,5},{5... | collective-permute-start | bytes 86024 | tf_op jit(solution)/shard_map/ppermute | solution.py:26
  1.9 6.7 %collective-permute-start = (f32[7,8,128]{2,1,0:T(8,128)S(1)}, f32[7,8,128]{2,1,0:T(8,128)S(1)}, u32[]{:S(2)}, u32[]{:S(2)}) collective-permute-start(f32[7,8,128]{2,1,0:T(8,128)S(1)} %get-tuple-element.2), channel_id=1, source_target_pairs={{0,1},{1,2},{2,3},{3,0},{4,5},{5,6},{6,7},{7,4},{8,9},{9,10},{10,1... | collective-permute-start | bytes 86024 | tf_op jit(solution)/shard_map/ppermute | solution.py:36
  4.6 5.1 %collective-permute-start.2 = (f32[2,7,8,128]{3,2,1,0:T(8,128)S(1)}, f32[2,7,8,128]{3,2,1,0:T(8,128)S(1)}, u32[]{:S(2)}, u32[]{:S(2)}) collective-permute-start(f32[2,7,8,128]{3,2,1,0:T(8,128)S(1)} %pad_maximum_fusion), channel_id=1, source_target_pairs={{0,2},{1,3},{2,0},{3,1},{4,7},{5,4},{6,5},{7,6},{8,10},{9,11},{10,... | collective-permute-start | bytes 172040 | tf_op jit(solution)/shard_map/ppermute | solution.py:36
  9.7 9.3 %copy-start = (s32[8]{0:T(128)S(1)}, s32[8]{0:T(128)}, u32[]{:S(2)}) copy-start(s32[8]{0:T(128)} %param.5) | copy-start | bytes 100
  9.8 6.6 %collective-permute-start.8 = (f32[4,7,8,128]{3,2,1,0:T(8,128)S(1)}, f32[4,7,8,128]{3,2,1,0:T(8,128)S(1)}, u32[]{:S(2)}, u32[]{:S(2)}) collective-permute-start(f32[4,7,8,128]{3,2,1,0:T(8,128)S(1)} %constant_dynamic-update-slice_fusion.refs_0_), channel_id=1, source_target_pairs={{0,24},{4,28},{8,16},{12,20},{16,8},{20,12},{24,0},{28,4},{1,25},{... | collective-permute-start | bytes 344072 | tf_op jit(solution)/shard_map/ppermute | solution.py:26
  12.4 5.1 %collective-permute-start.6 = (f32[4,7,8,128]{3,2,1,0:T(8,128)S(1)}, f32[4,7,8,128]{3,2,1,0:T(8,128)S(1)}, u32[]{:S(2)}, u32[]{:S(2)}) collective-permute-start(f32[4,7,8,128]{3,2,1,0:T(8,128)S(1)} %constant_dynamic-update-slice_fusion.refs_0_), channel_id=1, source_target_pairs={{0,8},{4,12},{8,0},{12,4},{16,24},{20,28},{24,16},{28,20},{1,9},{5... | collective-permute-start | bytes 344072 | tf_op jit(solution)/shard_map/ppermute | solution.py:26
  13.0 4.8 %collective-permute-start.4 = (f32[4,7,8,128]{3,2,1,0:T(8,128)S(1)}, f32[4,7,8,128]{3,2,1,0:T(8,128)S(1)}, u32[]{:S(2)}, u32[]{:S(2)}) collective-permute-start(f32[4,7,8,128]{3,2,1,0:T(8,128)S(1)} %constant_dynamic-update-slice_fusion.refs_0_), channel_id=1, source_target_pairs={{0,16},{4,20},{8,24},{12,28},{16,0},{20,4},{24,8},{28,12},{1,17},{... | collective-permute-start | bytes 344072 | tf_op jit(solution)/shard_map/ppermute | solution.py:26
  13.3 4.7 %collective-permute-start.3 = (f32[4,7,8,128]{3,2,1,0:T(8,128)S(1)}, f32[4,7,8,128]{3,2,1,0:T(8,128)S(1)}, u32[]{:S(2)}, u32[]{:S(2)}) collective-permute-start(f32[4,7,8,128]{3,2,1,0:T(8,128)S(1)} %constant_dynamic-update-slice_fusion.refs_0_), channel_id=1, source_target_pairs={{0,4},{4,0},{8,12},{12,8},{16,20},{20,16},{24,28},{28,24},{1,5},{5... | collective-permute-start | bytes 344072 | tf_op jit(solution)/shard_map/ppermute | solution.py:26
  16.3 1.7 %collective-permute-start.9 = (f32[4,7,8,128]{3,2,1,0:T(8,128)S(1)}, f32[4,7,8,128]{3,2,1,0:T(8,128)S(1)}, u32[]{:S(2)}, u32[]{:S(2)}) collective-permute-start(f32[4,7,8,128]{3,2,1,0:T(8,128)S(1)} %collective-permute-done.8.refs_6_), channel_id=1, source_target_pairs={{0,4},{4,0},{8,12},{12,8},{16,20},{20,16},{24,28},{28,24},{1,5},{5... | collective-permute-start | bytes 344072 | tf_op jit(solution)/shard_map/ppermute | solution.py:26
  17.5 1.3 %collective-permute-start.7 = (f32[4,7,8,128]{3,2,1,0:T(8,128)S(1)}, f32[4,7,8,128]{3,2,1,0:T(8,128)S(1)}, u32[]{:S(2)}, u32[]{:S(2)}) collective-permute-start(f32[4,7,8,128]{3,2,1,0:T(8,128)S(1)} %collective-permute-done.6.refs_4_), channel_id=1, source_target_pairs={{0,4},{4,0},{8,12},{12,8},{16,20},{20,16},{24,28},{28,24},{1,5},{5... | collective-permute-start | bytes 344072 | tf_op jit(solution)/shard_map/ppermute | solution.py:26
  17.8 1.3 %collective-permute-start.5 = (f32[4,7,8,128]{3,2,1,0:T(8,128)S(1)}, f32[4,7,8,128]{3,2,1,0:T(8,128)S(1)}, u32[]{:S(2)}, u32[]{:S(2)}) collective-permute-start(f32[4,7,8,128]{3,2,1,0:T(8,128)S(1)} %collective-permute-done.4.refs_2_), channel_id=1, source_target_pairs={{0,4},{4,0},{8,12},{12,8},{16,20},{20,16},{24,28},{28,24},{1,5},{5... | collective-permute-start | bytes 344072 | tf_op jit(solution)/shard_map/ppermute | solution.py:26

commit v8 on v7

--- a/solution.py
+++ b/solution.py
@@ -18,8 +18,23 @@
     return lax.div(value, jnp.int32(size)), lax.rem(value, jnp.int32(size))
 
 
-def mask_order(count):
-    return sorted(range(1, count), key=lambda mask: (-bin(mask).count("1"), mask))
+def ring_place(chip):
+    for shift in (1, 2, 4):
+        chip = chip ^ (chip >> shift)
+    return chip
+
+
+def shift_order(count):
+    return sorted(range(1, count), key=lambda shift: (min(shift, count - shift), shift))
+
+
+def shift_chips(values, shift):
+    rows = lax.axis_size("row")
+    pairs = []
+    for row in range(rows):
+        place = (ring_place(row // 2) + shift) % (rows // 2)
+        pairs.append((row, 2 * (place ^ (place >> 1)) + row % 2))
+    return lax.ppermute(values, "row", pairs)
 
 
 def swap_rows(values, mask):
@@ -60,7 +75,10 @@
     far = back >= 2
     holder = jnp.where(far, (row & -2) | (back & 1), row)
     slot = jnp.where(far, (back & -2) + jnp.where(holder == row, 0, 1), back)
-    return holder ^ lax.axis_index("row"), slot, line, lane
+    row_at = lax.axis_index("row")
+    shift = ring_place(row_at >> 1) - ring_place(holder >> 1) + row_count // 2
+    shift = split_index(shift, row_count // 2)[1]
+    return 2 * shift + ((holder ^ row_at) & 1), slot, line, lane
 
 
 def add_pairs(source, targets, sums):
@@ -81,8 +99,8 @@
     return tuple(sums)
 
 
-def sweep_kernel(row_count, col_count, masks, active_ref, *refs):
-    stacks, (accels_ref, jerks_ref) = refs[: len(masks)], refs[len(masks) :]
+def sweep_kernel(row_count, col_count, labels, active_ref, *refs):
+    stacks, (accels_ref, jerks_ref) = refs[: len(labels)], refs[len(labels) :]
     rows = stacks[0].shape[2]
     count = active_ref.shape[1]
     lane = lax.broadcasted_iota(jnp.int32, (count, LANES), 1)
@@ -96,9 +114,9 @@
 
     picked = [zeros] * 6
     for target in range(count):
-        mask, slot, row, spot = locate(active_ref[0, target], rows, row_count, col_count)
+        label, slot, row, spot = locate(active_ref[0, target], rows, row_count, col_count)
         for at, stack in enumerate(stacks):
-            hit = (lane == jnp.where(mask == masks[at], spot, -1)) & (place == target)
+            hit = (lane == jnp.where(label == labels[at], spot, -1)) & (place == target)
             line = lines(stack, slot, row)
             picked = [jnp.where(hit, line[part], picked[part]) for part in range(6)]
     targets = [jnp.broadcast_to(jnp.sum(value, axis=1, keepdims=True), (count, LANES)) for value in picked]
@@ -121,10 +139,10 @@
             jerks_ref[k - 3 : k - 2, :] = total
 
 
-def sweep(active, stacks, masks, row_count, col_count):
+def sweep(active, stacks, labels, row_count, col_count):
     count = active.shape[0]
     return pl.pallas_call(
-        functools.partial(sweep_kernel, row_count, col_count, masks),
+        functools.partial(sweep_kernel, row_count, col_count, labels),
         out_shape=[jax.ShapeDtypeStruct((3, count), jnp.float32)] * 2,
         in_specs=[pl.BlockSpec(memory_space=pltpu.VMEM)] * (len(stacks) + 1),
         out_specs=[pl.BlockSpec(memory_space=pltpu.VMEM)] * 2,
@@ -138,12 +156,12 @@
     rows = phase.shape[1] // LANES
     own = jnp.concatenate([phase.reshape(6, rows, LANES), mass.reshape(1, rows, LANES)], axis=0)
     stack = gather_cols(own)
-    stacks, masks = [], []
-    for mask in [0] + [2 * mask for mask in reversed(mask_order(row_count // 2))]:
-        held = stack if mask == 0 else swap_rows(stack, mask)
+    stacks, labels = [], []
+    for shift in [0] + shift_order(row_count // 2)[::-1]:
+        held = stack if shift == 0 else shift_chips(stack, shift)
         stacks += [held, swap_rows(held, 1)]
-        masks += [mask, mask + 1]
-    return sweep(active, stacks, masks, row_count, col_count)
+        labels += [2 * shift, 2 * shift + 1]
+    return sweep(active, stacks, labels, row_count, col_count)
 
 
 def solution(mesh):

time: 21.6 us -> 21.6 us (level)
  waiting for transfers between devices: 7.97 us -> 7.06 us
  starting transfers between devices: 9.63 us -> 10.5 us
    ppermute x0 -> x3, starting transfers between devices: none -> 4.68 us  [shift_chips(): return lax.ppermute(values, 'row', pairs)]
    ppermute x8 -> x5, waiting for transfers between devices: 5.49 us -> 1.32 us  [swap_rows(): lax.ppermute(values, 'row', [(at, at ^ mask) for at in range(lax.axis_siz...]
    ppermute x8 -> x5, starting transfers between devices: 4.36 us -> 0.53 us  [swap_rows(): lax.ppermute(values, 'row', [(at, at ^ mask) for at in range(lax.axis_siz...]
    ppermute x0 -> x3, waiting for transfers between devices: none -> 3.26 us  [shift_chips(): return lax.ppermute(values, 'row', pairs)]
where the time goes in v8:
time: 21.6 us; the launch traced here: 21.4 us
  starting transfers between devices  10.5 us (49%)
  waiting for transfers between devices  7.06 us (33%)
  Pallas kernels  2.38 us (11%)
  local copies, waits for them, and re-layouts  0.79 us (4%)
  between operations  0.68 us (3%)
    ppermute x2, starting transfers between devices, shift_cols(): return lax.ppermute(values, ('row', 'col'), pairs)  5.28 us
    ppermute x3, starting transfers between devices, shift_chips(): return lax.ppermute(values, 'row', pairs)  4.68 us
    ppermute x3, waiting for transfers between devices, shift_chips(): return lax.ppermute(values, 'row', pairs)  3.26 us
    ppermute x2, waiting for transfers between devices, shift_cols(): return lax.ppermute(values, ('row', 'col'), pairs)  2.48 us
    pallas_call x1, Pallas kernels, sweep(): pl.pallas_call(functools.partial(sweep_kernel, row_count, col_count, labe...  2.38 us
    ppermute x5, waiting for transfers between devices, swap_rows(): lax.ppermute(values, 'row', [(at, at ^ mask) for at in range(lax.axis_siz...  1.32 us
    unnamed x5, local copies, waits for them, and re-layouts  0.78 us
    ppermute x5, starting transfers between devices, swap_rows(): lax.ppermute(values, 'row', [(at, at ^ mask) for at in range(lax.axis_siz...  0.53 us
  transfers between devices with their start and end apart: 10, of which 7 were waited for; matrix products, arithmetic and copies ran while one was open for 0% of the time, Pallas kernels for 0%

profile of v8, /device:TPU:0, one launch (start us, length us, event | category | flops | bytes accessed | tf_op | source)
XLA Modules:
  0.0 21.4 jit_solution(12123682248380788542)
XLA Ops:
  0.6 0.0 copy-start.1
  0.6 0.8 %copy.7 = f32[1,6,8,128]{3,2,1,0:T(8,128)S(1)} copy(f32[1,6,8,128]{3,1,2,0:T(8,128)} %bitcast.13) | data formatting | bytes 49152
  1.4 0.5 %collective-permute-start.1 = (f32[7,8,128]{2,1,0:T(8,128)S(1)}, f32[7,8,128]{2,1,0:T(8,128)S(1)}, u32[]{:S(2)}, u32[]{:S(2)}) collective-permute-start(f32[7,8,128]{2,1,0:T(8,128)S(1)} %get-tuple-element.2), channel_id=1, source_target_pairs={{0,4},{4,0},{8,12},{12,8},{16,20},{20,16},{24,28},{28,24},{1,5},{5... | collective-permute-start | bytes 86024 | tf_op jit(solution)/shard_map/ppermute | solution.py:41
  1.9 2.6 %collective-permute-start = (f32[7,8,128]{2,1,0:T(8,128)S(1)}, f32[7,8,128]{2,1,0:T(8,128)S(1)}, u32[]{:S(2)}, u32[]{:S(2)}) collective-permute-start(f32[7,8,128]{2,1,0:T(8,128)S(1)} %get-tuple-element.2), channel_id=1, source_target_pairs={{0,1},{1,2},{2,3},{3,0},{4,5},{5,6},{6,7},{7,4},{8,9},{9,10},{10,1... | collective-permute-start | bytes 86024 | tf_op jit(solution)/shard_map/ppermute | solution.py:51
  4.6 0.0 collective-permute-done.1
  4.6 2.6 %collective-permute-start.2 = (f32[2,7,8,128]{3,2,1,0:T(8,128)S(1)}, f32[2,7,8,128]{3,2,1,0:T(8,128)S(1)}, u32[]{:S(2)}, u32[]{:S(2)}) collective-permute-start(f32[2,7,8,128]{3,2,1,0:T(8,128)S(1)} %pad_maximum_fusion), channel_id=1, source_target_pairs={{0,2},{1,3},{2,0},{3,1},{4,7},{5,4},{6,5},{7,6},{8,10},{9,11},{10,... | collective-permute-start | bytes 172040 | tf_op jit(solution)/shard_map/ppermute | solution.py:51
  7.3 1.4 %collective-permute-done = f32[7,8,128]{2,1,0:T(8,128)S(1)} collective-permute-done((f32[7,8,128]{2,1,0:T(8,128)S(1)}, f32[7,8,128]{2,1,0:T(8,128)S(1)}, u32[]{:S(2)}, u32[]{:S(2)}) %collective-permute-start) | collective-permute-done | bytes 28704 | tf_op jit(solution)/shard_map/ppermute | solution.py:51
  8.6 1.1 %collective-permute-done.2 = f32[2,7,8,128]{3,2,1,0:T(8,128)S(1)} collective-permute-done((f32[2,7,8,128]{3,2,1,0:T(8,128)S(1)}, f32[2,7,8,128]{3,2,1,0:T(8,128)S(1)}, u32[]{:S(2)}, u32[]{:S(2)}) %collective-permute-start.2) | collective-permute-done | bytes 57376 | tf_op jit(solution)/shard_map/ppermute | solution.py:51
  9.8 1.7 %collective-permute-start.8 = (f32[4,7,8,128]{3,2,1,0:T(8,128)S(1)}, f32[4,7,8,128]{3,2,1,0:T(8,128)S(1)}, u32[]{:S(2)}, u32[]{:S(2)}) collective-permute-start(f32[4,7,8,128]{3,2,1,0:T(8,128)S(1)} %constant_dynamic-update-slice_fusion.refs_0_), channel_id=1, source_target_pairs={{0,8},{4,12},{8,24},{12,28},{16,0},{20,4},{24,16},{28,20},{1,9},{5... | collective-permute-start | bytes 344072 | tf_op jit(solution)/shard_map/ppermute | solution.py:37
  11.5 0.4 %collective-permute-start.6 = (f32[4,7,8,128]{3,2,1,0:T(8,128)S(1)}, f32[4,7,8,128]{3,2,1,0:T(8,128)S(1)}, u32[]{:S(2)}, u32[]{:S(2)}) collective-permute-start(f32[4,7,8,128]{3,2,1,0:T(8,128)S(1)} %constant_dynamic-update-slice_fusion.refs_0_), channel_id=1, source_target_pairs={{0,16},{4,20},{8,0},{12,4},{16,24},{20,28},{24,8},{28,12},{1,17},{... | collective-permute-start | bytes 344072 | tf_op jit(solution)/shard_map/ppermute | solution.py:37
  11.8 2.6 %collective-permute-start.4 = (f32[4,7,8,128]{3,2,1,0:T(8,128)S(1)}, f32[4,7,8,128]{3,2,1,0:T(8,128)S(1)}, u32[]{:S(2)}, u32[]{:S(2)}) collective-permute-start(f32[4,7,8,128]{3,2,1,0:T(8,128)S(1)} %constant_dynamic-update-slice_fusion.refs_0_), channel_id=1, source_target_pairs={{0,24},{4,28},{8,16},{12,20},{16,8},{20,12},{24,0},{28,4},{1,25},{... | collective-permute-start | bytes 344072 | tf_op jit(solution)/shard_map/ppermute | solution.py:37
  14.4 0.0 collective-permute-start.3
  14.4 1.1 %collective-permute-done.8.refs_6_ = f32[4,7,8,128]{3,2,1,0:T(8,128)S(1)} collective-permute-done((f32[4,7,8,128]{3,2,1,0:T(8,128)S(1)}, f32[4,7,8,128]{3,2,1,0:T(8,128)S(1)}, u32[]{:S(2)}, u32[]{:S(2)}) %collective-permute-start.8) | collective-permute-done | bytes 114720 | tf_op jit(solution)/shard_map/ppermute | solution.py:37
  15.6 0.0 collective-permute-start.9
  15.6 1.0 %collective-permute-done.6.refs_4_ = f32[4,7,8,128]{3,2,1,0:T(8,128)S(1)} collective-permute-done((f32[4,7,8,128]{3,2,1,0:T(8,128)S(1)}, f32[4,7,8,128]{3,2,1,0:T(8,128)S(1)}, u32[]{:S(2)}, u32[]{:S(2)}) %collective-permute-start.6) | collective-permute-done | bytes 114720 | tf_op jit(solution)/shard_map/ppermute | solution.py:37
  16.6 0.0 collective-permute-start.7
  16.6 1.1 %collective-permute-done.4.refs_2_ = f32[4,7,8,128]{3,2,1,0:T(8,128)S(1)} collective-permute-done((f32[4,7,8,128]{3,2,1,0:T(8,128)S(1)}, f32[4,7,8,128]{3,2,1,0:T(8,128)S(1)}, u32[]{:S(2)}, u32[]{:S(2)}) %collective-permute-start.4) | collective-permute-done | bytes 114720 | tf_op jit(solution)/shard_map/ppermute | solution.py:37
  17.7 0.0 collective-permute-start.5
  17.7 0.0 collective-permute-done.3.refs_1_
  17.7 0.0 collective-permute-done.9.refs_7_
  17.7 0.2 collective-permute-done.7.refs_5_
  17.9 1.1 %collective-permute-done.5.refs_3_ = f32[4,7,8,128]{3,2,1,0:T(8,128)S(1)} collective-permute-done((f32[4,7,8,128]{3,2,1,0:T(8,128)S(1)}, f32[4,7,8,128]{3,2,1,0:T(8,128)S(1)}, u32[]{:S(2)}, u32[]{:S(2)}) %collective-permute-start.5) | collective-permute-done | bytes 114720 | tf_op jit(solution)/shard_map/ppermute | solution.py:41
  19.0 0.0 copy-done
  19.0 2.4 %shard_map.50 = (f32[3,8]{1,0:T(4,128)}, f32[3,8]{1,0:T(4,128)}) custom-call(s32[1,8]{1,0:T(1,128)S(1)} %bitcast.11, f32[4,7,8,128]{3,2,1,0:T(8,128)S(1)} %constant_dynamic-update-slice_fusion.refs_0_, f32[4,7,8,128]{3,2,1,0:T(8,128)S(1)} %collective-permute-done.3.refs_1_, f32[4,7,8,128]{3,2,1,0:T(8,128)S(1)} %collective-permute-done.4.refs_2_, ...), custom_call_target="tpu_custom_call" | custom-call | tf_op jit(solution)/shard_map/pallas_call | solution.py:144
  (7 shorter events, 0.0 us)
Async XLA Ops:
  0.6 0.8 %copy-start.1 = (f32[1024]{0:T(1024)S(1)}, f32[1024]{0:T(1024)}, u32[]{:S(2)}) copy-start(f32[1024]{0:T(1024)} %param.4) | copy-start | bytes 12292
  1.4 3.2 %collective-permute-start.1 = (f32[7,8,128]{2,1,0:T(8,128)S(1)}, f32[7,8,128]{2,1,0:T(8,128)S(1)}, u32[]{:S(2)}, u32[]{:S(2)}) collective-permute-start(f32[7,8,128]{2,1,0:T(8,128)S(1)} %get-tuple-element.2), channel_id=1, source_target_pairs={{0,4},{4,0},{8,12},{12,8},{16,20},{20,16},{24,28},{28,24},{1,5},{5... | collective-permute-start | bytes 86024 | tf_op jit(solution)/shard_map/ppermute | solution.py:41
  1.9 6.7 %collective-permute-start = (f32[7,8,128]{2,1,0:T(8,128)S(1)}, f32[7,8,128]{2,1,0:T(8,128)S(1)}, u32[]{:S(2)}, u32[]{:S(2)}) collective-permute-start(f32[7,8,128]{2,1,0:T(8,128)S(1)} %get-tuple-element.2), channel_id=1, source_target_pairs={{0,1},{1,2},{2,3},{3,0},{4,5},{5,6},{6,7},{7,4},{8,9},{9,10},{10,1... | collective-permute-start | bytes 86024 | tf_op jit(solution)/shard_map/ppermute | solution.py:51
  4.6 5.1 %collective-permute-start.2 = (f32[2,7,8,128]{3,2,1,0:T(8,128)S(1)}, f32[2,7,8,128]{3,2,1,0:T(8,128)S(1)}, u32[]{:S(2)}, u32[]{:S(2)}) collective-permute-start(f32[2,7,8,128]{3,2,1,0:T(8,128)S(1)} %pad_maximum_fusion), channel_id=1, source_target_pairs={{0,2},{1,3},{2,0},{3,1},{4,7},{5,4},{6,5},{7,6},{8,10},{9,11},{10,... | collective-permute-start | bytes 172040 | tf_op jit(solution)/shard_map/ppermute | solution.py:51
  9.7 9.3 %copy-start = (s32[8]{0:T(128)S(1)}, s32[8]{0:T(128)}, u32[]{:S(2)}) copy-start(s32[8]{0:T(128)} %param.5) | copy-start | bytes 100
  9.8 5.8 %collective-permute-start.8 = (f32[4,7,8,128]{3,2,1,0:T(8,128)S(1)}, f32[4,7,8,128]{3,2,1,0:T(8,128)S(1)}, u32[]{:S(2)}, u32[]{:S(2)}) collective-permute-start(f32[4,7,8,128]{3,2,1,0:T(8,128)S(1)} %constant_dynamic-update-slice_fusion.refs_0_), channel_id=1, source_target_pairs={{0,8},{4,12},{8,24},{12,28},{16,0},{20,4},{24,16},{28,20},{1,9},{5... | collective-permute-start | bytes 344072 | tf_op jit(solution)/shard_map/ppermute | solution.py:37
  11.5 5.1 %collective-permute-start.6 = (f32[4,7,8,128]{3,2,1,0:T(8,128)S(1)}, f32[4,7,8,128]{3,2,1,0:T(8,128)S(1)}, u32[]{:S(2)}, u32[]{:S(2)}) collective-permute-start(f32[4,7,8,128]{3,2,1,0:T(8,128)S(1)} %constant_dynamic-update-slice_fusion.refs_0_), channel_id=1, source_target_pairs={{0,16},{4,20},{8,0},{12,4},{16,24},{20,28},{24,8},{28,12},{1,17},{... | collective-permute-start | bytes 344072 | tf_op jit(solution)/shard_map/ppermute | solution.py:37
  11.8 5.9 %collective-permute-start.4 = (f32[4,7,8,128]{3,2,1,0:T(8,128)S(1)}, f32[4,7,8,128]{3,2,1,0:T(8,128)S(1)}, u32[]{:S(2)}, u32[]{:S(2)}) collective-permute-start(f32[4,7,8,128]{3,2,1,0:T(8,128)S(1)} %constant_dynamic-update-slice_fusion.refs_0_), channel_id=1, source_target_pairs={{0,24},{4,28},{8,16},{12,20},{16,8},{20,12},{24,0},{28,4},{1,25},{... | collective-permute-start | bytes 344072 | tf_op jit(solution)/shard_map/ppermute | solution.py:37
  14.4 3.3 %collective-permute-start.3 = (f32[4,7,8,128]{3,2,1,0:T(8,128)S(1)}, f32[4,7,8,128]{3,2,1,0:T(8,128)S(1)}, u32[]{:S(2)}, u32[]{:S(2)}) collective-permute-start(f32[4,7,8,128]{3,2,1,0:T(8,128)S(1)} %constant_dynamic-update-slice_fusion.refs_0_), channel_id=1, source_target_pairs={{0,4},{4,0},{8,12},{12,8},{16,20},{20,16},{24,28},{28,24},{1,5},{5... | collective-permute-start | bytes 344072 | tf_op jit(solution)/shard_map/ppermute | solution.py:41
  15.6 2.2 %collective-permute-start.9 = (f32[4,7,8,128]{3,2,1,0:T(8,128)S(1)}, f32[4,7,8,128]{3,2,1,0:T(8,128)S(1)}, u32[]{:S(2)}, u32[]{:S(2)}) collective-permute-start(f32[4,7,8,128]{3,2,1,0:T(8,128)S(1)} %collective-permute-done.8.refs_6_), channel_id=1, source_target_pairs={{0,4},{4,0},{8,12},{12,8},{16,20},{20,16},{24,28},{28,24},{1,5},{5... | collective-permute-start | bytes 344072 | tf_op jit(solution)/shard_map/ppermute | solution.py:41
  16.6 1.3 %collective-permute-start.7 = (f32[4,7,8,128]{3,2,1,0:T(8,128)S(1)}, f32[4,7,8,128]{3,2,1,0:T(8,128)S(1)}, u32[]{:S(2)}, u32[]{:S(2)}) collective-permute-start(f32[4,7,8,128]{3,2,1,0:T(8,128)S(1)} %collective-permute-done.6.refs_4_), channel_id=1, source_target_pairs={{0,4},{4,0},{8,12},{12,8},{16,20},{20,16},{24,28},{28,24},{1,5},{5... | collective-permute-start | bytes 344072 | tf_op jit(solution)/shard_map/ppermute | solution.py:41
  17.7 1.3 %collective-permute-start.5 = (f32[4,7,8,128]{3,2,1,0:T(8,128)S(1)}, f32[4,7,8,128]{3,2,1,0:T(8,128)S(1)}, u32[]{:S(2)}, u32[]{:S(2)}) collective-permute-start(f32[4,7,8,128]{3,2,1,0:T(8,128)S(1)} %collective-permute-done.4.refs_2_), channel_id=1, source_target_pairs={{0,4},{4,0},{8,12},{12,8},{16,20},{20,16},{24,28},{28,24},{1,5},{5... | collective-permute-start | bytes 344072 | tf_op jit(solution)/shard_map/ppermute | solution.py:41

commit v9 on v8

--- a/solution.py
+++ b/solution.py
@@ -156,11 +156,13 @@
     rows = phase.shape[1] // LANES
     own = jnp.concatenate([phase.reshape(6, rows, LANES), mass.reshape(1, rows, LANES)], axis=0)
     stack = gather_cols(own)
-    stacks, labels = [], []
-    for shift in [0] + shift_order(row_count // 2)[::-1]:
-        held = stack if shift == 0 else shift_chips(stack, shift)
+    stacks, labels = [stack], [0]
+    for shift in shift_order(row_count // 2)[::-1]:
+        held = shift_chips(stack, shift)
         stacks += [held, swap_rows(held, 1)]
         labels += [2 * shift, 2 * shift + 1]
+    stacks.append(swap_rows(stack, 1))
+    labels.append(1)
     return sweep(active, stacks, labels, row_count, col_count)
 
 

time: 21.6 us -> 21.6 us (level)
  no operation moved by 1% of the time
where the time goes in v9:
time: 21.6 us; the launch traced here: 21.4 us
  starting transfers between devices  10.5 us (49%)
  waiting for transfers between devices  7.06 us (33%)
  Pallas kernels  2.38 us (11%)
  local copies, waits for them, and re-layouts  0.79 us (4%)
  between operations  0.68 us (3%)
    ppermute x2, starting transfers between devices, shift_cols(): return lax.ppermute(values, ('row', 'col'), pairs)  5.28 us
    ppermute x3, starting transfers between devices, shift_chips(): return lax.ppermute(values, 'row', pairs)  4.68 us
    ppermute x3, waiting for transfers between devices, shift_chips(): return lax.ppermute(values, 'row', pairs)  3.26 us
    ppermute x2, waiting for transfers between devices, shift_cols(): return lax.ppermute(values, ('row', 'col'), pairs)  2.48 us
    pallas_call x1, Pallas kernels, sweep(): pl.pallas_call(functools.partial(sweep_kernel, row_count, col_count, labe...  2.38 us
    ppermute x5, waiting for transfers between devices, swap_rows(): lax.ppermute(values, 'row', [(at, at ^ mask) for at in range(lax.axis_siz...  1.32 us
    unnamed x5, local copies, waits for them, and re-layouts  0.78 us
    ppermute x5, starting transfers between devices, swap_rows(): lax.ppermute(values, 'row', [(at, at ^ mask) for at in range(lax.axis_siz...  0.53 us
  transfers between devices with their start and end apart: 10, of which 7 were waited for; matrix products, arithmetic and copies ran while one was open for 0% of the time, Pallas kernels for 0%

profile of v9, /device:TPU:0, one launch (start us, length us, event | category | flops | bytes accessed | tf_op | source)
XLA Modules:
  0.0 21.4 jit_solution(13132502902825724527)
XLA Ops:
  0.6 0.0 copy-start.1
  0.6 0.8 %copy.7 = f32[1,6,8,128]{3,2,1,0:T(8,128)S(1)} copy(f32[1,6,8,128]{3,1,2,0:T(8,128)} %bitcast.13) | data formatting | bytes 49152
  1.4 0.0 copy-done.1
  1.4 0.5 %collective-permute-start.1 = (f32[7,8,128]{2,1,0:T(8,128)S(1)}, f32[7,8,128]{2,1,0:T(8,128)S(1)}, u32[]{:S(2)}, u32[]{:S(2)}) collective-permute-start(f32[7,8,128]{2,1,0:T(8,128)S(1)} %get-tuple-element.2), channel_id=1, source_target_pairs={{0,4},{4,0},{8,12},{12,8},{16,20},{20,16},{24,28},{28,24},{1,5},{5... | collective-permute-start | bytes 86024 | tf_op jit(solution)/shard_map/ppermute | solution.py:41
  1.9 2.6 %collective-permute-start = (f32[7,8,128]{2,1,0:T(8,128)S(1)}, f32[7,8,128]{2,1,0:T(8,128)S(1)}, u32[]{:S(2)}, u32[]{:S(2)}) collective-permute-start(f32[7,8,128]{2,1,0:T(8,128)S(1)} %get-tuple-element.2), channel_id=1, source_target_pairs={{0,1},{1,2},{2,3},{3,0},{4,5},{5,6},{6,7},{7,4},{8,9},{9,10},{10,1... | collective-permute-start | bytes 86024 | tf_op jit(solution)/shard_map/ppermute | solution.py:51
  4.6 0.0 collective-permute-done.1
  4.6 2.6 %collective-permute-start.2 = (f32[2,7,8,128]{3,2,1,0:T(8,128)S(1)}, f32[2,7,8,128]{3,2,1,0:T(8,128)S(1)}, u32[]{:S(2)}, u32[]{:S(2)}) collective-permute-start(f32[2,7,8,128]{3,2,1,0:T(8,128)S(1)} %pad_maximum_fusion), channel_id=1, source_target_pairs={{0,2},{1,3},{2,0},{3,1},{4,7},{5,4},{6,5},{7,6},{8,10},{9,11},{10,... | collective-permute-start | bytes 172040 | tf_op jit(solution)/shard_map/ppermute | solution.py:51
  7.3 1.4 %collective-permute-done = f32[7,8,128]{2,1,0:T(8,128)S(1)} collective-permute-done((f32[7,8,128]{2,1,0:T(8,128)S(1)}, f32[7,8,128]{2,1,0:T(8,128)S(1)}, u32[]{:S(2)}, u32[]{:S(2)}) %collective-permute-start) | collective-permute-done | bytes 28704 | tf_op jit(solution)/shard_map/ppermute | solution.py:51
  8.6 1.1 %collective-permute-done.2 = f32[2,7,8,128]{3,2,1,0:T(8,128)S(1)} collective-permute-done((f32[2,7,8,128]{3,2,1,0:T(8,128)S(1)}, f32[2,7,8,128]{3,2,1,0:T(8,128)S(1)}, u32[]{:S(2)}, u32[]{:S(2)}) %collective-permute-start.2) | collective-permute-done | bytes 57376 | tf_op jit(solution)/shard_map/ppermute | solution.py:51
  9.8 1.7 %collective-permute-start.7 = (f32[4,7,8,128]{3,2,1,0:T(8,128)S(1)}, f32[4,7,8,128]{3,2,1,0:T(8,128)S(1)}, u32[]{:S(2)}, u32[]{:S(2)}) collective-permute-start(f32[4,7,8,128]{3,2,1,0:T(8,128)S(1)} %constant_dynamic-update-slice_fusion.refs_0_), channel_id=1, source_target_pairs={{0,8},{4,12},{8,24},{12,28},{16,0},{20,4},{24,16},{28,20},{1,9},{5... | collective-permute-start | bytes 344072 | tf_op jit(solution)/shard_map/ppermute | solution.py:37
  11.5 0.4 %collective-permute-start.5 = (f32[4,7,8,128]{3,2,1,0:T(8,128)S(1)}, f32[4,7,8,128]{3,2,1,0:T(8,128)S(1)}, u32[]{:S(2)}, u32[]{:S(2)}) collective-permute-start(f32[4,7,8,128]{3,2,1,0:T(8,128)S(1)} %constant_dynamic-update-slice_fusion.refs_0_), channel_id=1, source_target_pairs={{0,16},{4,20},{8,0},{12,4},{16,24},{20,28},{24,8},{28,12},{1,17},{... | collective-permute-start | bytes 344072 | tf_op jit(solution)/shard_map/ppermute | solution.py:37
  11.8 2.6 %collective-permute-start.3 = (f32[4,7,8,128]{3,2,1,0:T(8,128)S(1)}, f32[4,7,8,128]{3,2,1,0:T(8,128)S(1)}, u32[]{:S(2)}, u32[]{:S(2)}) collective-permute-start(f32[4,7,8,128]{3,2,1,0:T(8,128)S(1)} %constant_dynamic-update-slice_fusion.refs_0_), channel_id=1, source_target_pairs={{0,24},{4,28},{8,16},{12,20},{16,8},{20,12},{24,0},{28,4},{1,25},{... | collective-permute-start | bytes 344072 | tf_op jit(solution)/shard_map/ppermute | solution.py:37
  14.4 0.0 collective-permute-start.9
  14.4 1.1 %collective-permute-done.7.refs_5_ = f32[4,7,8,128]{3,2,1,0:T(8,128)S(1)} collective-permute-done((f32[4,7,8,128]{3,2,1,0:T(8,128)S(1)}, f32[4,7,8,128]{3,2,1,0:T(8,128)S(1)}, u32[]{:S(2)}, u32[]{:S(2)}) %collective-permute-start.7) | collective-permute-done | bytes 114720 | tf_op jit(solution)/shard_map/ppermute | solution.py:37
  15.6 0.0 collective-permute-start.8
  15.6 1.0 %collective-permute-done.5.refs_3_ = f32[4,7,8,128]{3,2,1,0:T(8,128)S(1)} collective-permute-done((f32[4,7,8,128]{3,2,1,0:T(8,128)S(1)}, f32[4,7,8,128]{3,2,1,0:T(8,128)S(1)}, u32[]{:S(2)}, u32[]{:S(2)}) %collective-permute-start.5) | collective-permute-done | bytes 114720 | tf_op jit(solution)/shard_map/ppermute | solution.py:37
  16.6 0.0 collective-permute-start.6
  16.6 1.1 %collective-permute-done.3.refs_1_ = f32[4,7,8,128]{3,2,1,0:T(8,128)S(1)} collective-permute-done((f32[4,7,8,128]{3,2,1,0:T(8,128)S(1)}, f32[4,7,8,128]{3,2,1,0:T(8,128)S(1)}, u32[]{:S(2)}, u32[]{:S(2)}) %collective-permute-start.3) | collective-permute-done | bytes 114720 | tf_op jit(solution)/shard_map/ppermute | solution.py:37
  17.7 0.0 collective-permute-start.4
  17.7 0.0 collective-permute-done.9.refs_7_
  17.7 0.0 collective-permute-done.8.refs_6_
  17.7 0.2 collective-permute-done.6.refs_4_
  17.9 1.1 %collective-permute-done.4.refs_2_ = f32[4,7,8,128]{3,2,1,0:T(8,128)S(1)} collective-permute-done((f32[4,7,8,128]{3,2,1,0:T(8,128)S(1)}, f32[4,7,8,128]{3,2,1,0:T(8,128)S(1)}, u32[]{:S(2)}, u32[]{:S(2)}) %collective-permute-start.4) | collective-permute-done | bytes 114720 | tf_op jit(solution)/shard_map/ppermute | solution.py:41
  19.0 2.4 %shard_map.50 = (f32[3,8]{1,0:T(4,128)}, f32[3,8]{1,0:T(4,128)}) custom-call(s32[1,8]{1,0:T(1,128)S(1)} %bitcast.11, f32[4,7,8,128]{3,2,1,0:T(8,128)S(1)} %constant_dynamic-update-slice_fusion.refs_0_, f32[4,7,8,128]{3,2,1,0:T(8,128)S(1)} %collective-permute-done.3.refs_1_, f32[4,7,8,128]{3,2,1,0:T(8,128)S(1)} %collective-permute-done.4.refs_2_, ...), custom_call_target="tpu_custom_call" | custom-call | tf_op jit(solution)/shard_map/pallas_call | solution.py:144
  (7 shorter events, 0.0 us)
Async XLA Ops:
  0.6 0.8 %copy-start.1 = (f32[1024]{0:T(1024)S(1)}, f32[1024]{0:T(1024)}, u32[]{:S(2)}) copy-start(f32[1024]{0:T(1024)} %param.4) | copy-start | bytes 12292
  1.4 3.2 %collective-permute-start.1 = (f32[7,8,128]{2,1,0:T(8,128)S(1)}, f32[7,8,128]{2,1,0:T(8,128)S(1)}, u32[]{:S(2)}, u32[]{:S(2)}) collective-permute-start(f32[7,8,128]{2,1,0:T(8,128)S(1)} %get-tuple-element.2), channel_id=1, source_target_pairs={{0,4},{4,0},{8,12},{12,8},{16,20},{20,16},{24,28},{28,24},{1,5},{5... | collective-permute-start | bytes 86024 | tf_op jit(solution)/shard_map/ppermute | solution.py:41
  1.9 6.7 %collective-permute-start = (f32[7,8,128]{2,1,0:T(8,128)S(1)}, f32[7,8,128]{2,1,0:T(8,128)S(1)}, u32[]{:S(2)}, u32[]{:S(2)}) collective-permute-start(f32[7,8,128]{2,1,0:T(8,128)S(1)} %get-tuple-element.2), channel_id=1, source_target_pairs={{0,1},{1,2},{2,3},{3,0},{4,5},{5,6},{6,7},{7,4},{8,9},{9,10},{10,1... | collective-permute-start | bytes 86024 | tf_op jit(solution)/shard_map/ppermute | solution.py:51
  4.6 5.1 %collective-permute-start.2 = (f32[2,7,8,128]{3,2,1,0:T(8,128)S(1)}, f32[2,7,8,128]{3,2,1,0:T(8,128)S(1)}, u32[]{:S(2)}, u32[]{:S(2)}) collective-permute-start(f32[2,7,8,128]{3,2,1,0:T(8,128)S(1)} %pad_maximum_fusion), channel_id=1, source_target_pairs={{0,2},{1,3},{2,0},{3,1},{4,7},{5,4},{6,5},{7,6},{8,10},{9,11},{10,... | collective-permute-start | bytes 172040 | tf_op jit(solution)/shard_map/ppermute | solution.py:51
  9.7 9.3 %copy-start = (s32[8]{0:T(128)S(1)}, s32[8]{0:T(128)}, u32[]{:S(2)}) copy-start(s32[8]{0:T(128)} %param.5) | copy-start | bytes 100
  9.8 5.8 %collective-permute-start.7 = (f32[4,7,8,128]{3,2,1,0:T(8,128)S(1)}, f32[4,7,8,128]{3,2,1,0:T(8,128)S(1)}, u32[]{:S(2)}, u32[]{:S(2)}) collective-permute-start(f32[4,7,8,128]{3,2,1,0:T(8,128)S(1)} %constant_dynamic-update-slice_fusion.refs_0_), channel_id=1, source_target_pairs={{0,8},{4,12},{8,24},{12,28},{16,0},{20,4},{24,16},{28,20},{1,9},{5... | collective-permute-start | bytes 344072 | tf_op jit(solution)/shard_map/ppermute | solution.py:37
  11.5 5.1 %collective-permute-start.5 = (f32[4,7,8,128]{3,2,1,0:T(8,128)S(1)}, f32[4,7,8,128]{3,2,1,0:T(8,128)S(1)}, u32[]{:S(2)}, u32[]{:S(2)}) collective-permute-start(f32[4,7,8,128]{3,2,1,0:T(8,128)S(1)} %constant_dynamic-update-slice_fusion.refs_0_), channel_id=1, source_target_pairs={{0,16},{4,20},{8,0},{12,4},{16,24},{20,28},{24,8},{28,12},{1,17},{... | collective-permute-start | bytes 344072 | tf_op jit(solution)/shard_map/ppermute | solution.py:37
  11.8 5.9 %collective-permute-start.3 = (f32[4,7,8,128]{3,2,1,0:T(8,128)S(1)}, f32[4,7,8,128]{3,2,1,0:T(8,128)S(1)}, u32[]{:S(2)}, u32[]{:S(2)}) collective-permute-start(f32[4,7,8,128]{3,2,1,0:T(8,128)S(1)} %constant_dynamic-update-slice_fusion.refs_0_), channel_id=1, source_target_pairs={{0,24},{4,28},{8,16},{12,20},{16,8},{20,12},{24,0},{28,4},{1,25},{... | collective-permute-start | bytes 344072 | tf_op jit(solution)/shard_map/ppermute | solution.py:37
  14.4 3.3 %collective-permute-start.9 = (f32[4,7,8,128]{3,2,1,0:T(8,128)S(1)}, f32[4,7,8,128]{3,2,1,0:T(8,128)S(1)}, u32[]{:S(2)}, u32[]{:S(2)}) collective-permute-start(f32[4,7,8,128]{3,2,1,0:T(8,128)S(1)} %constant_dynamic-update-slice_fusion.refs_0_), channel_id=1, source_target_pairs={{0,4},{4,0},{8,12},{12,8},{16,20},{20,16},{24,28},{28,24},{1,5},{5... | collective-permute-start | bytes 344072 | tf_op jit(solution)/shard_map/ppermute | solution.py:41
  15.6 2.2 %collective-permute-start.8 = (f32[4,7,8,128]{3,2,1,0:T(8,128)S(1)}, f32[4,7,8,128]{3,2,1,0:T(8,128)S(1)}, u32[]{:S(2)}, u32[]{:S(2)}) collective-permute-start(f32[4,7,8,128]{3,2,1,0:T(8,128)S(1)} %collective-permute-done.7.refs_5_), channel_id=1, source_target_pairs={{0,4},{4,0},{8,12},{12,8},{16,20},{20,16},{24,28},{28,24},{1,5},{5... | collective-permute-start | bytes 344072 | tf_op jit(solution)/shard_map/ppermute | solution.py:41
  16.6 1.3 %collective-permute-start.6 = (f32[4,7,8,128]{3,2,1,0:T(8,128)S(1)}, f32[4,7,8,128]{3,2,1,0:T(8,128)S(1)}, u32[]{:S(2)}, u32[]{:S(2)}) collective-permute-start(f32[4,7,8,128]{3,2,1,0:T(8,128)S(1)} %collective-permute-done.5.refs_3_), channel_id=1, source_target_pairs={{0,4},{4,0},{8,12},{12,8},{16,20},{20,16},{24,28},{28,24},{1,5},{5... | collective-permute-start | bytes 344072 | tf_op jit(solution)/shard_map/ppermute | solution.py:41
  17.7 1.3 %collective-permute-start.4 = (f32[4,7,8,128]{3,2,1,0:T(8,128)S(1)}, f32[4,7,8,128]{3,2,1,0:T(8,128)S(1)}, u32[]{:S(2)}, u32[]{:S(2)}) collective-permute-start(f32[4,7,8,128]{3,2,1,0:T(8,128)S(1)} %collective-permute-done.3.refs_1_), channel_id=1, source_target_pairs={{0,4},{4,0},{8,12},{12,8},{16,20},{20,16},{24,28},{28,24},{1,5},{5... | collective-permute-start | bytes 344072 | tf_op jit(solution)/shard_map/ppermute | solution.py:41

commit v10 on v8

--- a/solution.py
+++ b/solution.py
@@ -25,7 +25,7 @@
 
 
 def shift_order(count):
-    return sorted(range(1, count), key=lambda shift: (min(shift, count - shift), shift))
+    return sorted(range(1, count), key=lambda shift: (-min(shift, count - shift), -shift))
 
 
 def shift_chips(values, shift):

time: 21.6 us -> 21.6 us (level)
  starting transfers between devices: 10.5 us -> 10.8 us
  waiting for transfers between devices: 7.06 us -> 6.78 us
    ppermute x5, starting transfers between devices: 0.53 us -> 0.83 us  [swap_rows(): lax.ppermute(values, 'row', [(at, at ^ mask) for at in range(lax.axis_siz...]
    ppermute x5, waiting for transfers between devices: 1.32 us -> 1.02 us  [swap_rows(): lax.ppermute(values, 'row', [(at, at ^ mask) for at in range(lax.axis_siz...]
where the time goes in v10:
time: 21.6 us; the launch traced here: 21.4 us
  starting transfers between devices  10.8 us (50%)
  waiting for transfers between devices  6.78 us (31%)
  Pallas kernels  2.38 us (11%)
  local copies, waits for them, and re-layouts  0.79 us (4%)
  between operations  0.67 us (3%)
    ppermute x2, starting transfers between devices, shift_cols(): return lax.ppermute(values, ('row', 'col'), pairs)  5.28 us
    ppermute x3, starting transfers between devices, shift_chips(): return lax.ppermute(values, 'row', pairs)  4.69 us
    ppermute x3, waiting for transfers between devices, shift_chips(): return lax.ppermute(values, 'row', pairs)  3.27 us
    ppermute x2, waiting for transfers between devices, shift_cols(): return lax.ppermute(values, ('row', 'col'), pairs)  2.48 us
    pallas_call x1, Pallas kernels, sweep(): pl.pallas_call(functools.partial(sweep_kernel, row_count, col_count, labe...  2.38 us
    ppermute x5, waiting for transfers between devices, swap_rows(): lax.ppermute(values, 'row', [(at, at ^ mask) for at in range(lax.axis_siz...  1.02 us
    ppermute x5, starting transfers between devices, swap_rows(): lax.ppermute(values, 'row', [(at, at ^ mask) for at in range(lax.axis_siz...  0.83 us
    unnamed x5, local copies, waits for them, and re-layouts  0.78 us
  transfers between devices with their start and end apart: 10, of which 7 were waited for; matrix products, arithmetic and copies ran while one was open for 0% of the time, Pallas kernels for 0%

profile of v10, /device:TPU:0, one launch (start us, length us, event | category | flops | bytes accessed | tf_op | source)
XLA Modules:
  0.0 21.4 jit_solution(7372899726586903357)
XLA Ops:
  0.6 0.0 copy-start.1
  0.6 0.8 %copy.7 = f32[1,6,8,128]{3,2,1,0:T(8,128)S(1)} copy(f32[1,6,8,128]{3,1,2,0:T(8,128)} %bitcast.13) | data formatting | bytes 49152
  1.4 0.0 copy-done.1
  1.4 0.5 %collective-permute-start.1 = (f32[7,8,128]{2,1,0:T(8,128)S(1)}, f32[7,8,128]{2,1,0:T(8,128)S(1)}, u32[]{:S(2)}, u32[]{:S(2)}) collective-permute-start(f32[7,8,128]{2,1,0:T(8,128)S(1)} %get-tuple-element.2), channel_id=1, source_target_pairs={{0,4},{4,0},{8,12},{12,8},{16,20},{20,16},{24,28},{28,24},{1,5},{5... | collective-permute-start | bytes 86024 | tf_op jit(solution)/shard_map/ppermute | solution.py:41
  1.9 2.6 %collective-permute-start = (f32[7,8,128]{2,1,0:T(8,128)S(1)}, f32[7,8,128]{2,1,0:T(8,128)S(1)}, u32[]{:S(2)}, u32[]{:S(2)}) collective-permute-start(f32[7,8,128]{2,1,0:T(8,128)S(1)} %get-tuple-element.2), channel_id=1, source_target_pairs={{0,1},{1,2},{2,3},{3,0},{4,5},{5,6},{6,7},{7,4},{8,9},{9,10},{10,1... | collective-permute-start | bytes 86024 | tf_op jit(solution)/shard_map/ppermute | solution.py:51
  4.6 0.0 collective-permute-done.1
  4.6 2.6 %collective-permute-start.2 = (f32[2,7,8,128]{3,2,1,0:T(8,128)S(1)}, f32[2,7,8,128]{3,2,1,0:T(8,128)S(1)}, u32[]{:S(2)}, u32[]{:S(2)}) collective-permute-start(f32[2,7,8,128]{3,2,1,0:T(8,128)S(1)} %pad_maximum_fusion), channel_id=1, source_target_pairs={{0,2},{1,3},{2,0},{3,1},{4,7},{5,4},{6,5},{7,6},{8,10},{9,11},{10,... | collective-permute-start | bytes 172040 | tf_op jit(solution)/shard_map/ppermute | solution.py:51
  7.3 1.4 %collective-permute-done = f32[7,8,128]{2,1,0:T(8,128)S(1)} collective-permute-done((f32[7,8,128]{2,1,0:T(8,128)S(1)}, f32[7,8,128]{2,1,0:T(8,128)S(1)}, u32[]{:S(2)}, u32[]{:S(2)}) %collective-permute-start) | collective-permute-done | bytes 28704 | tf_op jit(solution)/shard_map/ppermute | solution.py:51
  8.6 1.1 %collective-permute-done.2 = f32[2,7,8,128]{3,2,1,0:T(8,128)S(1)} collective-permute-done((f32[2,7,8,128]{3,2,1,0:T(8,128)S(1)}, f32[2,7,8,128]{3,2,1,0:T(8,128)S(1)}, u32[]{:S(2)}, u32[]{:S(2)}) %collective-permute-start.2) | collective-permute-done | bytes 57376 | tf_op jit(solution)/shard_map/ppermute | solution.py:51
  9.8 2.7 %collective-permute-start.8 = (f32[4,7,8,128]{3,2,1,0:T(8,128)S(1)}, f32[4,7,8,128]{3,2,1,0:T(8,128)S(1)}, u32[]{:S(2)}, u32[]{:S(2)}) collective-permute-start(f32[4,7,8,128]{3,2,1,0:T(8,128)S(1)} %constant_dynamic-update-slice_fusion.refs_0_), channel_id=1, source_target_pairs={{0,24},{4,28},{8,16},{12,20},{16,8},{20,12},{24,0},{28,4},{1,25},{... | collective-permute-start | bytes 344072 | tf_op jit(solution)/shard_map/ppermute | solution.py:37
  12.4 0.5 %collective-permute-start.6 = (f32[4,7,8,128]{3,2,1,0:T(8,128)S(1)}, f32[4,7,8,128]{3,2,1,0:T(8,128)S(1)}, u32[]{:S(2)}, u32[]{:S(2)}) collective-permute-start(f32[4,7,8,128]{3,2,1,0:T(8,128)S(1)} %constant_dynamic-update-slice_fusion.refs_0_), channel_id=1, source_target_pairs={{0,16},{4,20},{8,0},{12,4},{16,24},{20,28},{24,8},{28,12},{1,17},{... | collective-permute-start | bytes 344072 | tf_op jit(solution)/shard_map/ppermute | solution.py:37
  12.9 1.5 %collective-permute-start.4 = (f32[4,7,8,128]{3,2,1,0:T(8,128)S(1)}, f32[4,7,8,128]{3,2,1,0:T(8,128)S(1)}, u32[]{:S(2)}, u32[]{:S(2)}) collective-permute-start(f32[4,7,8,128]{3,2,1,0:T(8,128)S(1)} %constant_dynamic-update-slice_fusion.refs_0_), channel_id=1, source_target_pairs={{0,8},{4,12},{8,24},{12,28},{16,0},{20,4},{24,16},{28,20},{1,9},{5... | collective-permute-start | bytes 344072 | tf_op jit(solution)/shard_map/ppermute | solution.py:37
  14.4 0.0 collective-permute-start.3
  14.4 2.1 %collective-permute-done.8.refs_6_ = f32[4,7,8,128]{3,2,1,0:T(8,128)S(1)} collective-permute-done((f32[4,7,8,128]{3,2,1,0:T(8,128)S(1)}, f32[4,7,8,128]{3,2,1,0:T(8,128)S(1)}, u32[]{:S(2)}, u32[]{:S(2)}) %collective-permute-start.8) | collective-permute-done | bytes 114720 | tf_op jit(solution)/shard_map/ppermute | solution.py:37
  16.5 0.0 collective-permute-start.9
  16.5 1.0 %collective-permute-done.6.refs_4_ = f32[4,7,8,128]{3,2,1,0:T(8,128)S(1)} collective-permute-done((f32[4,7,8,128]{3,2,1,0:T(8,128)S(1)}, f32[4,7,8,128]{3,2,1,0:T(8,128)S(1)}, u32[]{:S(2)}, u32[]{:S(2)}) %collective-permute-start.6) | collective-permute-done | bytes 114720 | tf_op jit(solution)/shard_map/ppermute | solution.py:37
  17.5 0.0 collective-permute-start.7
  17.5 0.2 collective-permute-done.4.refs_2_
  17.7 0.3 %collective-permute-start.5 = (f32[4,7,8,128]{3,2,1,0:T(8,128)S(1)}, f32[4,7,8,128]{3,2,1,0:T(8,128)S(1)}, u32[]{:S(2)}, u32[]{:S(2)}) collective-permute-start(f32[4,7,8,128]{3,2,1,0:T(8,128)S(1)} %collective-permute-done.4.refs_2_), channel_id=1, source_target_pairs={{0,4},{4,0},{8,12},{12,8},{16,20},{20,16},{24,28},{28,24},{1,5},{5... | collective-permute-start | bytes 344072 | tf_op jit(solution)/shard_map/ppermute | solution.py:41
  18.0 0.0 collective-permute-done.3.refs_1_
  18.0 0.0 collective-permute-done.9.refs_7_
  18.0 0.8 %collective-permute-done.7.refs_5_ = f32[4,7,8,128]{3,2,1,0:T(8,128)S(1)} collective-permute-done((f32[4,7,8,128]{3,2,1,0:T(8,128)S(1)}, f32[4,7,8,128]{3,2,1,0:T(8,128)S(1)}, u32[]{:S(2)}, u32[]{:S(2)}) %collective-permute-start.7) | collective-permute-done | bytes 114720 | tf_op jit(solution)/shard_map/ppermute | solution.py:41
  18.8 0.2 collective-permute-done.5.refs_3_
  19.1 2.4 %shard_map.50 = (f32[3,8]{1,0:T(4,128)}, f32[3,8]{1,0:T(4,128)}) custom-call(s32[1,8]{1,0:T(1,128)S(1)} %bitcast.11, f32[4,7,8,128]{3,2,1,0:T(8,128)S(1)} %constant_dynamic-update-slice_fusion.refs_0_, f32[4,7,8,128]{3,2,1,0:T(8,128)S(1)} %collective-permute-done.3.refs_1_, f32[4,7,8,128]{3,2,1,0:T(8,128)S(1)} %collective-permute-done.4.refs_2_, ...), custom_call_target="tpu_custom_call" | custom-call | tf_op jit(solution)/shard_map/pallas_call | solution.py:144
  (7 shorter events, 0.0 us)
Async XLA Ops:
  0.6 0.8 %copy-start.1 = (f32[1024]{0:T(1024)S(1)}, f32[1024]{0:T(1024)}, u32[]{:S(2)}) copy-start(f32[1024]{0:T(1024)} %param.4) | copy-start | bytes 12292
  1.4 3.2 %collective-permute-start.1 = (f32[7,8,128]{2,1,0:T(8,128)S(1)}, f32[7,8,128]{2,1,0:T(8,128)S(1)}, u32[]{:S(2)}, u32[]{:S(2)}) collective-permute-start(f32[7,8,128]{2,1,0:T(8,128)S(1)} %get-tuple-element.2), channel_id=1, source_target_pairs={{0,4},{4,0},{8,12},{12,8},{16,20},{20,16},{24,28},{28,24},{1,5},{5... | collective-permute-start | bytes 86024 | tf_op jit(solution)/shard_map/ppermute | solution.py:41
  1.9 6.7 %collective-permute-start = (f32[7,8,128]{2,1,0:T(8,128)S(1)}, f32[7,8,128]{2,1,0:T(8,128)S(1)}, u32[]{:S(2)}, u32[]{:S(2)}) collective-permute-start(f32[7,8,128]{2,1,0:T(8,128)S(1)} %get-tuple-element.2), channel_id=1, source_target_pairs={{0,1},{1,2},{2,3},{3,0},{4,5},{5,6},{6,7},{7,4},{8,9},{9,10},{10,1... | collective-permute-start | bytes 86024 | tf_op jit(solution)/shard_map/ppermute | solution.py:51
  4.6 5.1 %collective-permute-start.2 = (f32[2,7,8,128]{3,2,1,0:T(8,128)S(1)}, f32[2,7,8,128]{3,2,1,0:T(8,128)S(1)}, u32[]{:S(2)}, u32[]{:S(2)}) collective-permute-start(f32[2,7,8,128]{3,2,1,0:T(8,128)S(1)} %pad_maximum_fusion), channel_id=1, source_target_pairs={{0,2},{1,3},{2,0},{3,1},{4,7},{5,4},{6,5},{7,6},{8,10},{9,11},{10,... | collective-permute-start | bytes 172040 | tf_op jit(solution)/shard_map/ppermute | solution.py:51
  9.7 9.3 %copy-start = (s32[8]{0:T(128)S(1)}, s32[8]{0:T(128)}, u32[]{:S(2)}) copy-start(s32[8]{0:T(128)} %param.5) | copy-start | bytes 100
  9.8 6.8 %collective-permute-start.8 = (f32[4,7,8,128]{3,2,1,0:T(8,128)S(1)}, f32[4,7,8,128]{3,2,1,0:T(8,128)S(1)}, u32[]{:S(2)}, u32[]{:S(2)}) collective-permute-start(f32[4,7,8,128]{3,2,1,0:T(8,128)S(1)} %constant_dynamic-update-slice_fusion.refs_0_), channel_id=1, source_target_pairs={{0,24},{4,28},{8,16},{12,20},{16,8},{20,12},{24,0},{28,4},{1,25},{... | collective-permute-start | bytes 344072 | tf_op jit(solution)/shard_map/ppermute | solution.py:37
  12.4 5.1 %collective-permute-start.6 = (f32[4,7,8,128]{3,2,1,0:T(8,128)S(1)}, f32[4,7,8,128]{3,2,1,0:T(8,128)S(1)}, u32[]{:S(2)}, u32[]{:S(2)}) collective-permute-start(f32[4,7,8,128]{3,2,1,0:T(8,128)S(1)} %constant_dynamic-update-slice_fusion.refs_0_), channel_id=1, source_target_pairs={{0,16},{4,20},{8,0},{12,4},{16,24},{20,28},{24,8},{28,12},{1,17},{... | collective-permute-start | bytes 344072 | tf_op jit(solution)/shard_map/ppermute | solution.py:37
  12.9 4.8 %collective-permute-start.4 = (f32[4,7,8,128]{3,2,1,0:T(8,128)S(1)}, f32[4,7,8,128]{3,2,1,0:T(8,128)S(1)}, u32[]{:S(2)}, u32[]{:S(2)}) collective-permute-start(f32[4,7,8,128]{3,2,1,0:T(8,128)S(1)} %constant_dynamic-update-slice_fusion.refs_0_), channel_id=1, source_target_pairs={{0,8},{4,12},{8,24},{12,28},{16,0},{20,4},{24,16},{28,20},{1,9},{5... | collective-permute-start | bytes 344072 | tf_op jit(solution)/shard_map/ppermute | solution.py:37
  14.4 3.6 %collective-permute-start.3 = (f32[4,7,8,128]{3,2,1,0:T(8,128)S(1)}, f32[4,7,8,128]{3,2,1,0:T(8,128)S(1)}, u32[]{:S(2)}, u32[]{:S(2)}) collective-permute-start(f32[4,7,8,128]{3,2,1,0:T(8,128)S(1)} %constant_dynamic-update-slice_fusion.refs_0_), channel_id=1, source_target_pairs={{0,4},{4,0},{8,12},{12,8},{16,20},{20,16},{24,28},{28,24},{1,5},{5... | collective-permute-start | bytes 344072 | tf_op jit(solution)/shard_map/ppermute | solution.py:41
  16.5 1.5 %collective-permute-start.9 = (f32[4,7,8,128]{3,2,1,0:T(8,128)S(1)}, f32[4,7,8,128]{3,2,1,0:T(8,128)S(1)}, u32[]{:S(2)}, u32[]{:S(2)}) collective-permute-start(f32[4,7,8,128]{3,2,1,0:T(8,128)S(1)} %collective-permute-done.8.refs_6_), channel_id=1, source_target_pairs={{0,4},{4,0},{8,12},{12,8},{16,20},{20,16},{24,28},{28,24},{1,5},{5... | collective-permute-start | bytes 344072 | tf_op jit(solution)/shard_map/ppermute | solution.py:41
  17.5 1.3 %collective-permute-start.7 = (f32[4,7,8,128]{3,2,1,0:T(8,128)S(1)}, f32[4,7,8,128]{3,2,1,0:T(8,128)S(1)}, u32[]{:S(2)}, u32[]{:S(2)}) collective-permute-start(f32[4,7,8,128]{3,2,1,0:T(8,128)S(1)} %collective-permute-done.6.refs_4_), channel_id=1, source_target_pairs={{0,4},{4,0},{8,12},{12,8},{16,20},{20,16},{24,28},{28,24},{1,5},{5... | collective-permute-start | bytes 344072 | tf_op jit(solution)/shard_map/ppermute | solution.py:41
  17.7 1.3 %collective-permute-start.5 = (f32[4,7,8,128]{3,2,1,0:T(8,128)S(1)}, f32[4,7,8,128]{3,2,1,0:T(8,128)S(1)}, u32[]{:S(2)}, u32[]{:S(2)}) collective-permute-start(f32[4,7,8,128]{3,2,1,0:T(8,128)S(1)} %collective-permute-done.4.refs_2_), channel_id=1, source_target_pairs={{0,4},{4,0},{8,12},{12,8},{16,20},{20,16},{24,28},{28,24},{1,5},{5... | collective-permute-start | bytes 344072 | tf_op jit(solution)/shard_map/ppermute | solution.py:41
